TPU v7x, 256 devices: a whole 4x4x8 slice. The times are simulated.
256 devices in a mesh: role: 2 (over core), expert: 8 (over z), shard: 16 (over x, y).
Axes of the slice: x: 4, y: 4, z: 8, core: 2. Of those that a mesh axis runs over, the one named last changes fastest.
Arguments:
- query: bfloat16 [512, 6144], P(('expert', 'shard'), 'role')
- new_kv: bfloat16 [512, 2, 1024], P(('expert', 'shard'), None, 'role'), may hold values from -6 to 6
- kv_cache: bfloat16 [512, 2, 128, 1024], P(('expert', 'shard'), None, None, 'role')
- lengths: int32 [512], P(('expert', 'shard')), may hold values from 32 to 128
- residual: bfloat16 [512, 6144], P(('expert', 'shard'), 'role'), may hold values from -8 to 8
- norm_gain: bfloat16 [6144], P('role'), may hold values from 0.099609375 to 1.8984375
- expert_ids: int32 [512, 2], P(('expert', 'shard')), may hold values from 0 to 7, all different within a row; in each aligned block of 4 rows (0 to 3, 4 to 7, ...) at most 2 rows name the same one
- router_logits: float32 [512, 8], P(('expert', 'shard')), may hold values from -0.75 to 0.75
- w_gate: bfloat16 [8, 6144, 8192], P('expert', 'role', 'shard'), may hold values from -0.078125 to 0.078125
- w_up: bfloat16 [8, 6144, 8192], P('expert', 'role', 'shard'), may hold values from -0.078125 to 0.078125
- w_down: bfloat16 [8, 8192, 6144], P('expert', 'shard', 'role'), may hold values from -0.0625 to 0.0625
Outputs:
- layer_out: bfloat16 [512, 6144], P(('expert', 'shard'), 'role')
Inputs may be any that keep to these rules, and one draw needn't show every extreme that they name: `expert_ids`: the requests of one device name each expert at most 2 times.
All inputs are finite; a program needn't handle non-finite values.
Results may differ from a plain program's by a relative error of at most 0.0065.
Values may be sent and summed in bfloat16 or wider, within the bound.
No kernel may reach another device: no remote copies, remote signals or barrier semaphores. Data moves between devices by JAX's collectives and lax.ppermute only.
A program may use at most 64 MiB of HBM per device.

v0:
```python
import jax
import jax.numpy as jnp
from jax import lax
from jax.sharding import PartitionSpec as P

MODEL_WIDTH = 6144
HEADS = 48
KV_HEADS = 8
HD = 128
TOP = 2
EXPERT_CAPACITY = 2


def per_device(
    query,
    new_kv,
    kv_cache,
    lengths,
    residual,
    norm_gain,
    expert_ids,
    router_logits,
    w_gate,
    w_up,
    w_down,
):
    group = HEADS // KV_HEADS
    scale = 1.0 / HD**0.5
    token_rows = query.shape[0]
    context = kv_cache.shape[2]
    local_heads = new_kv.shape[2] // HD
    q = query.reshape(token_rows, local_heads, group, HD)
    keys = kv_cache[:, 0].reshape(token_rows, context, local_heads, HD)
    values = kv_cache[:, 1].reshape(token_rows, context, local_heads, HD)
    new_k = new_kv[:, 0].reshape(token_rows, local_heads, HD)
    new_v = new_kv[:, 1].reshape(token_rows, local_heads, HD)
    scores = jnp.einsum("rkgd,rckd->rkgc", q, keys, preferred_element_type=jnp.float32) * scale
    own = jnp.einsum("rkgd,rkd->rkg", q, new_k, preferred_element_type=jnp.float32) * scale
    valid = (jnp.arange(context, dtype=jnp.int32)[None, :] < lengths[:, None])[:, None, None, :]
    top = jnp.maximum(jnp.max(jnp.where(valid, scores, -jnp.inf), axis=-1), own)
    ecache = jnp.where(valid, jnp.exp(scores - top[..., None]), 0.0)
    eown = jnp.exp(own - top)
    total = jnp.sum(ecache, axis=-1) + eown
    pcache = (ecache / total[..., None]).astype(jnp.bfloat16)
    pown = (eown / total).astype(jnp.bfloat16)
    attn = jnp.einsum("rkgc,rckd->rkgd", pcache, values, preferred_element_type=jnp.float32)
    attn = attn + pown.astype(jnp.float32)[..., None] * new_v.astype(jnp.float32)[:, :, None, :]
    hidden = (residual.astype(jnp.float32) + attn.reshape(token_rows, -1)).astype(jnp.bfloat16)
    hf = hidden.astype(jnp.float32)
    squared_total = lax.psum(jnp.sum(hf * hf, axis=-1), "role")
    inv_rms = lax.rsqrt(squared_total / MODEL_WIDTH + 1e-05)
    normed = (hf * inv_rms[:, None] * norm_gain.astype(jnp.float32)).astype(jnp.bfloat16)
    experts = lax.axis_size("expert")
    shards = lax.axis_size("shard")
    pairs = token_rows * TOP
    flat = expert_ids.reshape(pairs)
    onehot = (flat[:, None] == jnp.arange(experts, dtype=jnp.int32)[None, :]).astype(jnp.int32)
    rank = jnp.cumsum(onehot, axis=0) - onehot
    slot = jnp.sum(rank * onehot, axis=1)
    slot_hit = (slot[:, None] == jnp.arange(EXPERT_CAPACITY, dtype=jnp.int32)[None, :]).astype(
        jnp.float32
    )
    select = (onehot.astype(jnp.float32).T[:, None, :] * slot_hit.T[None, :, :]).reshape(
        experts * EXPERT_CAPACITY, pairs
    )
    owner = (
        jnp.arange(pairs, dtype=jnp.int32)[:, None] // TOP
        == jnp.arange(token_rows, dtype=jnp.int32)[None, :]
    ).astype(jnp.float32)
    dispatch_rows = jnp.dot(select, owner, precision=lax.Precision.HIGHEST).astype(jnp.bfloat16)
    half = normed.shape[1]
    outgoing = (
        jnp.dot(dispatch_rows, normed, preferred_element_type=jnp.float32)
        .astype(jnp.bfloat16)
        .reshape(experts, EXPERT_CAPACITY, half)
    )
    chosen = jnp.sum(
        onehot.astype(jnp.float32).reshape(token_rows, TOP, experts) * router_logits[:, None, :],
        axis=-1,
    )
    weights = jnp.stack(
        [jax.nn.sigmoid(chosen[:, 0] - chosen[:, 1]), jax.nn.sigmoid(chosen[:, 1] - chosen[:, 0])],
        axis=-1,
    ).reshape(pairs)
    combine = jnp.dot(owner.T * weights[None, :], select.T, precision=lax.Precision.HIGHEST)
    copies = jnp.broadcast_to(outgoing[:, None], (experts, shards, EXPERT_CAPACITY, half)).reshape(
        experts * shards, EXPERT_CAPACITY, half
    )
    received = lax.all_to_all(copies, ("expert", "shard"), split_axis=0, concat_axis=0, tiled=True)
    ordered = (
        received.reshape(experts, shards, EXPERT_CAPACITY, half)
        .transpose(1, 0, 2, 3)
        .reshape(shards * experts, EXPERT_CAPACITY, half)
    )
    gate = jnp.einsum("ncd,df->ncf", ordered, w_gate[0], preferred_element_type=jnp.float32)
    upper = jnp.einsum("ncd,df->ncf", ordered, w_up[0], preferred_element_type=jnp.float32)
    partial_pre = jnp.concatenate([gate, upper], axis=-1)
    pre = lax.psum(partial_pre, "role")
    hidden_width = w_gate.shape[2]
    act = (
        (jax.nn.silu(pre[..., :hidden_width]) * pre[..., hidden_width:])
        .astype(jnp.bfloat16)
        .reshape(-1, hidden_width)
    )
    count_rows = experts * EXPERT_CAPACITY
    full_terms = jnp.dot(act, w_down[0], preferred_element_type=jnp.float32)
    summed_all = lax.psum(full_terms, "shard")
    summed = lax.dynamic_slice_in_dim(
        summed_all, lax.axis_index("shard") * count_rows, count_rows, 0
    )
    returned = lax.all_to_all(
        summed.astype(jnp.bfloat16).reshape(experts, EXPERT_CAPACITY, half),
        "expert",
        split_axis=0,
        concat_axis=0,
        tiled=True,
    )
    moe = jnp.dot(
        combine,
        returned.reshape(experts * EXPERT_CAPACITY, half).astype(jnp.float32),
        precision=lax.Precision.HIGHEST,
    )
    return (hf + moe).astype(jnp.bfloat16)


def solution(mesh):
    in_specs = (
        P(("expert", "shard"), "role"),
        P(("expert", "shard"), None, "role"),
        P(("expert", "shard"), None, None, "role"),
        P(("expert", "shard")),
        P(("expert", "shard"), "role"),
        P("role"),
        P(("expert", "shard"), None),
        P(("expert", "shard"), None),
        P("expert", "role", "shard"),
        P("expert", "role", "shard"),
        P("expert", "shard", "role"),
    )
    out_specs = P(("expert", "shard"), "role")
    return jax.shard_map(
        per_device, mesh=mesh, in_specs=in_specs, out_specs=out_specs, check_vma=False
    )
```

profile of v0, /device:TPU:32, one launch (start us, length us, event | category | flops | bytes accessed | tf_op | source)
XLA Modules:
  0.0 233.0 jit_solution(4327824129075916831)
XLA Ops:
  6.6 0.9 copy.37
  7.9 2.3 fusion.37
  10.2 2.0 copy.46
  12.3 2.1 copy.45
  14.5 1.4 select_reduce_fusion
  16.1 1.5 convolution_add_fusion.1
  17.8 2.5 %psum.21 = f32[4]{0:T(128)S(1)} all-reduce(f32[4]{0:T(128)S(1)} %get-tuple-element.5), channel_id=1, replica_groups=mesh['role'=2,'expert'=8,'shard'=16] {'role'}, use_global_device_ids=true, to_apply=%region_6.7 | all-reduce | flops 4 | bytes 32 | tf_op jit(solution)/shard_map/psum | solution.py:50
  20.9 0.8 broadcast_in_dim.26
  21.7 57.8 %all_to_all.10 = bf16[128,2,3072]{2,1,0:T(2,128)(2,1)S(1)} all-to-all(bf16[128,2,3072]{2,1,0:T(2,128)(2,1)S(1)} %bitcast.39), channel_id=1, replica_groups=mesh['role'=2,'expert'=8,'shard'=16] {'expert','shard'}, dimensions={0} | all-to-all | bytes 3145728 | tf_op jit(solution)/shard_map/all_to_all | solution.py:89
  79.9 1.1 fusion.3
  81.0 0.7 copy-done.8
  81.7 1.1 fusion.5
  82.9 1.1 pad_maximum_fusion
  84.4 24.0 %all-reduce.3.cloned.1.call-done = f32[128,2,1024]{2,0,1:T(8,128)} async-done(((f32[128,2,1024]{2,0,1:T(8,128)}), f32[128,2,1024]{2,0,1:T(8,128)}) %all-reduce.3.cloned.1.call-update) | async-done | bytes 1048592 | tf_op jit(solution)/shard_map/psum | solution.py:98
  108.4 1.4 fusion.11
  109.8 1.0 copy.40
  110.7 1.1 reshape.155
  111.8 2.7 %fusion.1 = f32[256,3072]{1,0:T(8,128)} fusion(bf16[256,512]{1,0:T(8,128)(2,1)S(1)} %reshape.155, bf16[1,512,3072]{2,1,0:T(8,128)(2,1)S(1)} %copy-done), kind=kOutput, calls=%fused_computation.3 | convolution fusion | flops 805306368 | bytes 6553600 | tf_op jit(solution)/shard_map/dot_general | solution.py:106
  114.5 94.5 %all-reduce.4 = bf16[256,3072]{1,0:T(8,128)(2,1)} all-reduce(f32[256,3072]{1,0:T(8,128)} %fusion.1), channel_id=1, replica_groups=mesh['role'=2,'expert'=8,'shard'=16] {'shard'}, use_global_device_ids=true, to_apply=%region_8.9 | all-reduce | flops 786432 | bytes 4718592 | tf_op jit(solution)/shard_map/psum | solution.py:107
  209.0 0.9 dynamic-slice_convert_fusion
  209.9 0.7 reshape.156
  210.5 7.5 %all-to-all-start.1 = ((bf16[8,2,3072]{2,1,0:T(2,128)(2,1)}), bf16[8,2,3072]{2,1,0:T(2,128)(2,1)S(1)}, u32[]{:S(2)}, u32[]{:S(2)}) async-start(bf16[8,2,3072]{2,1,0:T(2,128)(2,1)} %reshape.156), calls=%async_computation.1 | async-start | bytes 196608 | tf_op jit(solution)/shard_map/all_to_all | solution.py:111
  218.2 7.1 %all-to-all-done.1 = bf16[8,2,3072]{2,1,0:T(2,128)(2,1)S(1)} async-done(((bf16[8,2,3072]{2,1,0:T(2,128)(2,1)}), bf16[8,2,3072]{2,1,0:T(2,128)(2,1)S(1)}, u32[]{:S(2)}, u32[]{:S(2)}) %all-to-all-start.1) | async-done | bytes 98336 | tf_op jit(solution)/shard_map/all_to_all | solution.py:111
  225.3 0.8 fusion
  (50 shorter events, 2.5 us)
Async XLA Ops:
  6.5 105.3 %copy-start = (bf16[1,512,3072]{2,1,0:T(8,128)(2,1)S(1)}, bf16[1,512,3072]{2,1,0:T(8,128)(2,1)}, u32[]{:S(2)}) copy-start(bf16[1,512,3072]{2,1,0:T(8,128)(2,1)} %param.21) | copy-start | bytes 9437188
  6.5 5.7 %copy-start.9 = (s32[4]{0:T(128)S(1)}, s32[4]{0:T(128)}, u32[]{:S(2)}) copy-start(s32[4]{0:T(128)} %param.14) | copy-start | bytes 52
  6.5 5.7 %copy-start.1 = (bf16[4,3072]{1,0:T(4,128)(2,1)S(1)}, bf16[4,3072]{1,0:T(4,128)(2,1)}, u32[]{:S(2)}) copy-start(bf16[4,3072]{1,0:T(4,128)(2,1)} %param.11) | copy-start | bytes 73732
  6.5 7.8 %copy-start.3 = (bf16[4,2,512]{2,1,0:T(2,128)(2,1)S(1)}, bf16[4,2,512]{2,1,0:T(2,128)(2,1)}, u32[]{:S(2)}) copy-start(bf16[4,2,512]{2,1,0:T(2,128)(2,1)} %param.12) | copy-start | bytes 24580
  6.5 11.1 %copy-start.4 = (bf16[3072]{0:T(1024)(128)(2,1)S(1)}, bf16[3072]{0:T(1024)(128)(2,1)}, u32[]{:S(2)}) copy-start(bf16[3072]{0:T(1024)(128)(2,1)} %param.16) | copy-start | bytes 18436
  6.5 11.1 %copy-start.2 = (bf16[4,3072]{1,0:T(4,128)(2,1)S(1)}, bf16[4,3072]{1,0:T(4,128)(2,1)}, u32[]{:S(2)}) copy-start(bf16[4,3072]{1,0:T(4,128)(2,1)} %param.15) | copy-start | bytes 73732
  6.6 101.9 %all-reduce.3.cloned.1.call-start = ((), (), s32[]{:S(2)}) async-start(), calls=%async_computation.2 | async-start | bytes 2097152 | tf_op jit(solution)/shard_map/psum | solution.py:98
  21.7 58.2 %copy-start.7 = (bf16[1,3072,512]{2,1,0:T(8,128)(2,1)S(1)}, bf16[1,3072,512]{2,1,0:T(8,128)(2,1)}, u32[]{:S(2)}) copy-start(bf16[1,3072,512]{2,1,0:T(8,128)(2,1)} %param.20) | copy-start | bytes 9437188
  79.9 1.9 copy-start.8
  82.9 1.2 copy-start.5
  82.9 1.2 copy-start.6
  210.5 14.8 %all-to-all-start.1 = ((bf16[8,2,3072]{2,1,0:T(2,128)(2,1)}), bf16[8,2,3072]{2,1,0:T(2,128)(2,1)S(1)}, u32[]{:S(2)}, u32[]{:S(2)}) async-start(bf16[8,2,3072]{2,1,0:T(2,128)(2,1)} %reshape.156), calls=%async_computation.1 | async-start | bytes 196608 | tf_op jit(solution)/shard_map/all_to_all | solution.py:111
Sparse Core Ops, SparseCore 0:
  84.2 24.2 all-reduce.2
where the time goes:
time: 234 us; the launch traced here: 233 us
  blocking collectives  155 us (66%)
  waiting for transfers between devices  31.2 us (13%)
  between operations  13.6 us (6%)
  local copies, waits for them, and re-layouts  13.2 us (6%)
  matrix products  9.31 us (4%)
  starting transfers between devices  7.52 us (3%)
  other arithmetic  3.42 us (1%)
    psum x1, blocking collectives, per_device(): summed_all = lax.psum(full_terms, 'shard')  94.5 us
    all_to_all x1, blocking collectives, per_device(): lax.all_to_all(copies, ('expert', 'shard'), split_axis=0, concat_axis=0,...  57.8 us
    psum x1, waiting for transfers between devices, per_device(): pre = lax.psum(partial_pre, 'role')  24 us
    all_to_all x1, starting transfers between devices, per_device(): lax.all_to_all(summed.astype(jnp.bfloat16).reshape(experts, EXPERT_CAPACI...  7.49 us
    all_to_all x1, waiting for transfers between devices, per_device(): lax.all_to_all(summed.astype(jnp.bfloat16).reshape(experts, EXPERT_CAPACI...  7.15 us
    unnamed x23, local copies, waits for them, and re-layouts  5.8 us
  transfers between devices with their start and end apart: 2, of which 2 were waited for; matrix products, arithmetic and copies ran while one was open for 0% of the time, Pallas kernels for 0%

commit v1 on v0

v1 whole, which is shorter than its diff:
```python
import functools

import jax
import jax.numpy as jnp
from jax import lax
from jax.experimental import pallas as pl
from jax.experimental.pallas import tpu as pltpu
from jax.sharding import Mesh
from jax.sharding import PartitionSpec as P

MODEL_WIDTH = 6144
HALF = 3072
GROUP = 6
HD = 128
CTX = 128
ROWS = 4
LOCAL_HEADS = 4
EXPERTS = 8
CAP = 2
HIDDEN = 512
AXES = ("role", "expert", "x", "y")
SHIFTS = (0, 1, -1, 2)
VMEM_SPEC = pl.BlockSpec(memory_space=pltpu.VMEM)
SMEM_SPEC = pl.BlockSpec(memory_space=pltpu.SMEM)
F32 = jnp.float32
BF16 = jnp.bfloat16


def call(body, out_shape, in_specs, flops=0, nbytes=0, scratch=()):
    single = not isinstance(out_shape, (tuple, list))
    out_specs = VMEM_SPEC if single else [VMEM_SPEC] * len(out_shape)
    return pl.pallas_call(
        body,
        out_shape=out_shape,
        in_specs=in_specs,
        out_specs=out_specs,
        scratch_shapes=list(scratch),
        compiler_params=pltpu.CompilerParams(vmem_limit_bytes=40 * 1024 * 1024),
        cost_estimate=pl.CostEstimate(flops=flops, bytes_accessed=nbytes, transcendentals=0),
    )


def attend_body(len_ref, q_ref, new_ref, kv_ref, res_ref, hidden_ref, sq_ref):
    scale = 1.0 / HD**0.5
    m_rows = GROUP * ROWS
    row_req = lax.broadcasted_iota(jnp.int32, (m_rows, 1), 0) % ROWS
    row_len = jnp.zeros((m_rows, 1), jnp.int32)
    for r in range(ROWS):
        row_len = jnp.where(row_req == r, len_ref[r], row_len)
    col = lax.broadcasted_iota(jnp.int32, (m_rows, ROWS * CTX), 1)
    valid = (col // CTX == row_req) & (col % CTX < row_len)
    own_valid = lax.broadcasted_iota(jnp.int32, (m_rows, ROWS), 1) == row_req
    nt = (((1,), (1,)), ((), ()))
    acc = jnp.zeros((ROWS, HD), F32)
    new = new_ref[...].astype(F32)
    for k in range(LOCAL_HEADS):
        sl = slice(k * HD, (k + 1) * HD)
        q = jnp.concatenate(
            [
                q_ref[:, (k * GROUP + g) * HD : (k * GROUP + g + 1) * HD].astype(F32)
                for g in range(GROUP)
            ],
            axis=0,
        ).astype(BF16)
        keys = kv_ref[:, 0, :, sl].reshape(ROWS * CTX, HD)
        vals = kv_ref[:, 1, :, sl].reshape(ROWS * CTX, HD)
        nk = new[:, 0, sl].astype(BF16)
        nv = new[:, 1, sl].astype(BF16)
        s = lax.dot_general(q, keys, nt, preferred_element_type=F32) * scale
        so = lax.dot_general(q, nk, nt, preferred_element_type=F32) * scale
        s = jnp.where(valid, s, -jnp.inf)
        so = jnp.where(own_valid, so, -jnp.inf)
        top = jnp.maximum(
            jnp.max(s, axis=1, keepdims=True), jnp.max(so, axis=1, keepdims=True)
        )
        e = jnp.exp(s - top)
        eo = jnp.exp(so - top)
        total = jnp.sum(e, axis=1, keepdims=True) + jnp.sum(eo, axis=1, keepdims=True)
        p = (e / total).astype(BF16)
        po = (eo / total).astype(BF16)
        attn = jnp.dot(p, vals, preferred_element_type=F32) + jnp.dot(
            po, nv, preferred_element_type=F32
        )
        for g in range(GROUP):
            h = k * GROUP + g
            hs = slice(h * HD, (h + 1) * HD)
            hid = (res_ref[:, hs].astype(F32) + attn[g * ROWS : (g + 1) * ROWS]).astype(BF16)
            hidden_ref[:, hs] = hid
            hf = hid.astype(F32)
            acc = acc + hf * hf
    sq_ref[...] = acc


def slot_rows(ids):
    rows = []
    for p in range(len(ids)):
        slot = jnp.int32(0)
        for q in range(p):
            slot = slot + (ids[q] == ids[p]).astype(jnp.int32)
        rows.append(ids[p] * CAP + slot)
    return rows


def dispatch_body(ids_ref, hidden_ref, sq_ref, sq2_ref, gain_ref, out_ref):
    ids = [ids_ref[p // 2, p % 2] for p in range(2 * ROWS)]
    rows = slot_rows(ids)
    total = jnp.sum(sq_ref[...] + sq2_ref[...], axis=1, keepdims=True)
    inv = lax.rsqrt(total / MODEL_WIDTH + 1e-05)
    normed = (hidden_ref[...].astype(F32) * inv * gain_ref[...].astype(F32)).astype(BF16)
    ri = lax.broadcasted_iota(jnp.int32, (EXPERTS * CAP, ROWS), 0)
    ci = lax.broadcasted_iota(jnp.int32, (EXPERTS * CAP, ROWS), 1)
    select = jnp.zeros((EXPERTS * CAP, ROWS), F32)
    for p in range(2 * ROWS):
        select = jnp.where((ri == rows[p]) & (ci == p // 2), 1.0, select)
    out = jnp.dot(select.astype(BF16), normed, preferred_element_type=F32).astype(BF16)
    for e in range(EXPERTS):
        out_ref[e] = out[e * CAP : (e + 1) * CAP]


def gate_body(x0, x1, x2, x3, wg_ref, wu_ref, own_ref, send_ref):
    x = jnp.concatenate([x0[...], x1[...], x2[...], x3[...]], axis=0)
    for n in range(0, HIDDEN, 256):
        for at, w_ref in ((0, wg_ref), (HIDDEN, wu_ref)):
            got = jnp.dot(x, w_ref[:, n : n + 256], preferred_element_type=F32)
            own_ref[:, at + n : at + n + 256] = got
            send_ref[:, at + n : at + n + 256] = got.astype(BF16)


def down_body(own_ref, got_ref, wd_ref, o0, o1, o2, o3, act_ref):
    for jb in range(4):
        for ja in range(4):
            at = (jb * 4 + ja) * 16
            peer = (ja * 4 + jb) * 16
            pre = own_ref[at : at + 16] + got_ref[peer : peer + 16].astype(F32)
            gate = pre[:, :HIDDEN]
            act_ref[at : at + 16] = (gate * jax.nn.sigmoid(gate) * pre[:, HIDDEN:]).astype(BF16)
    outs = (o0, o1, o2, o3)
    act = act_ref[...]
    for n in range(0, HALF, 512):
        got = jnp.dot(act, wd_ref[:, n : n + 512], preferred_element_type=F32).astype(BF16)
        for j in range(4):
            outs[j][:, n : n + 512] = got[j * 64 : (j + 1) * 64]


def combine_body(ids_ref, logit_ref, hidden_ref, back_ref, out_ref):
    ids = [ids_ref[p // 2, p % 2] for p in range(2 * ROWS)]
    rows = slot_rows(ids)
    ci = lax.broadcasted_iota(jnp.int32, (CAP, 1), 0)
    for t in range(ROWS):
        a, b = ids[2 * t], ids[2 * t + 1]
        diff = jnp.full((CAP, 1), logit_ref[t, a] - logit_ref[t, b], F32)
        wa = jnp.where(ci == rows[2 * t] - a * CAP, jax.nn.sigmoid(diff), 0.0)
        wb = jnp.where(ci == rows[2 * t + 1] - b * CAP, jax.nn.sigmoid(-diff), 0.0)
        both = back_ref[a].astype(F32) * wa + back_ref[b].astype(F32) * wb
        moe = jnp.sum(both, axis=0, keepdims=True)
        out_ref[t : t + 1] = (hidden_ref[t : t + 1].astype(F32) + moe).astype(BF16)


def index_of(role, z, x, y):
    return ((role * 8 + z) * 4 + x) * 4 + y


def permutation(move):
    return [
        (index_of(r, z, x, y), index_of(*move(r, z, x, y)))
        for r in range(2)
        for z in range(8)
        for x in range(4)
        for y in range(4)
    ]


def along_x(s, r, z, x, y):
    return r, z, (x + s) % 4, y


def along_y(s, r, z, x, y):
    return r, z, x, (y + s) % 4


def ring(which, s):
    def move(r, z, x, y):
        first = along_x if (r == 0) == (which == 0) else along_y
        return first(s, r, z, x, y)

    return permutation(move)


def send(value, which, s):
    return lax.ppermute(value, AXES, ring(which, s))


def swap(value):
    return lax.ppermute(value, "role", [(0, 1), (1, 0)])


def add_up(parts):
    total = parts[0].astype(F32)
    for p in parts[1:]:
        total = total + p.astype(F32)
    return total.astype(BF16)


def per_device(
    query, new_kv, kv_cache, lengths, residual, norm_gain, expert_ids, router_logits, w_gate, w_up, w_down
):
    hidden, sq = call(
        attend_body,
        (jax.ShapeDtypeStruct((ROWS, HALF), BF16), jax.ShapeDtypeStruct((ROWS, HD), F32)),
        [SMEM_SPEC] + [VMEM_SPEC] * 4,
        flops=50_000_000,
        nbytes=1_200_000,
    )(lengths, query, new_kv, kv_cache, residual)
    outgoing = call(
        dispatch_body,
        jax.ShapeDtypeStruct((EXPERTS, CAP, HALF), BF16),
        [SMEM_SPEC] + [VMEM_SPEC] * 4,
        flops=400_000,
        nbytes=150_000,
    )(expert_ids, hidden, sq, swap(sq), norm_gain.reshape(1, HALF))
    arrived = lax.all_to_all(outgoing, "expert", split_axis=0, concat_axis=0, tiled=True)
    block = arrived.reshape(EXPERTS * CAP, HALF)
    plane = jnp.concatenate([block] + [send(block, 0, s) for s in SHIFTS[1:]], axis=0)
    pieces = [plane] + [send(plane, 1, s) for s in SHIFTS[1:]]
    own, partial = call(
        gate_body,
        (jax.ShapeDtypeStruct((256, 2 * HIDDEN), F32), jax.ShapeDtypeStruct((256, 2 * HIDDEN), BF16)),
        [VMEM_SPEC] * 6,
        flops=2 * 256 * HALF * 1024,
        nbytes=9_000_000,
    )(*pieces, w_gate[0], w_up[0])
    terms = call(
        down_body,
        [jax.ShapeDtypeStruct((64, HALF), BF16)] * 4,
        [VMEM_SPEC] * 3,
        flops=2 * 256 * HALF * 512,
        nbytes=6_000_000,
        scratch=[pltpu.VMEM((256, HIDDEN), BF16)],
    )(own, swap(partial), w_down[0])
    rows_b = add_up([terms[0]] + [send(terms[j], 1, -SHIFTS[j]) for j in (1, 2, 3)])
    parts = [rows_b[16 * j : 16 * j + 16] for j in range(4)]
    rows_a = add_up([parts[0]] + [send(parts[j], 0, -SHIFTS[j]) for j in (1, 2, 3)])
    back = lax.all_to_all(
        rows_a.reshape(EXPERTS, CAP, HALF), "expert", split_axis=0, concat_axis=0, tiled=True
    )
    return call(
        combine_body,
        jax.ShapeDtypeStruct((ROWS, HALF), BF16),
        [SMEM_SPEC] * 2 + [VMEM_SPEC] * 2,
        flops=100_000,
        nbytes=150_000,
    )(expert_ids, router_logits, hidden, back)


def solution(mesh):
    fine = Mesh(mesh.devices.reshape(2, 8, 4, 4), AXES)
    rows = ("expert", "x", "y")
    shard = ("x", "y")
    in_specs = (
        P(rows, "role"),
        P(rows, None, "role"),
        P(rows, None, None, "role"),
        P(rows),
        P(rows, "role"),
        P("role"),
        P(rows, None),
        P(rows, None),
        P("expert", "role", shard),
        P("expert", "role", shard),
        P("expert", shard, "role"),
    )
    return jax.shard_map(
        per_device, mesh=fine, in_specs=in_specs, out_specs=P(rows, "role"), check_vma=False
    )
```

time: 234 us -> 99 us (0.42)
  blocking collectives: 155 us -> 26.3 us
  starting transfers between devices: 7.52 us -> 22.7 us
  between operations: 13.6 us -> 0.15 us
  matrix products: 9.31 us -> 0 us
  Pallas kernels: 0 us -> 7.1 us
  local copies, waits for them, and re-layouts: 13.2 us -> 9.44 us
  other arithmetic: 3.42 us -> 0.25 us
    psum x2 -> x0, blocking collectives: 97 us -> none  [the longest x1 94.5 us: per_device(): summed_all = lax.psum(full_terms, 'shard')]
    ppermute x0 -> x14, waiting for transfers between devices: none -> 31.8 us  [the longest x12 29.9 us: send(): return lax.ppermute(value, AXES, ring(which, s))]
    all_to_all x1 -> x2, blocking collectives: 57.8 us -> 26.3 us  [the longest x1 15.9 us: per_device(): lax.all_to_all(outgoing, 'expert', split_axis=0, concat_axis=0, tiled=True)]
    psum x1 -> x0, waiting for transfers between devices: 24 us -> none  [per_device(): pre = lax.psum(partial_pre, 'role')]
    ppermute x0 -> x14, starting transfers between devices: none -> 22.7 us  [the longest x12 22.5 us: send(): return lax.ppermute(value, AXES, ring(which, s))]
    dot_general x10 -> x0, matrix products: 9.31 us -> none  [the longest x1 2.65 us: per_device(): full_terms = jnp.dot(act, w_down[0], preferred_element_type=jnp.float32)]
    all_to_all x1 -> x0, starting transfers between devices: 7.49 us -> none  [per_device(): lax.all_to_all(summed.astype(jnp.bfloat16).reshape(experts, EXPERT_CAPACI...]
    all_to_all x1 -> x0, waiting for transfers between devices: 7.15 us -> none  [per_device(): lax.all_to_all(summed.astype(jnp.bfloat16).reshape(experts, EXPERT_CAPACI...]
  transfers between devices with their start and end apart: 2 -> 14, of which waited for: 2 -> 9; matrix products, arithmetic and copies ran while one was open for 0% -> 2% of each run, Pallas kernels for 0% -> 0%
where the time goes in v1:
time: 99 us; the launch traced here: 97.8 us
  waiting for transfers between devices  31.8 us (32%)
  blocking collectives  26.3 us (27%)
  starting transfers between devices  22.7 us (23%)
  local copies, waits for them, and re-layouts  9.44 us (10%)
  Pallas kernels  7.1 us (7%)
    ppermute x12, waiting for transfers between devices, send(): return lax.ppermute(value, AXES, ring(which, s))  29.9 us
    ppermute x12, starting transfers between devices, send(): return lax.ppermute(value, AXES, ring(which, s))  22.5 us
    all_to_all x1, blocking collectives, per_device(): lax.all_to_all(outgoing, 'expert', split_axis=0, concat_axis=0, tiled=True)  15.9 us
    all_to_all x1, blocking collectives, per_device(): lax.all_to_all(rows_a.reshape(EXPERTS, CAP, HALF), 'expert', split_axis=0...  10.4 us
    unnamed x22, local copies, waits for them, and re-layouts  8.63 us
    pallas_call x1, Pallas kernels, per_device(): call(attend_body, (jax.ShapeDtypeStruct((ROWS, HALF), BF16), jax.ShapeDty...  2.06 us
  transfers between devices with their start and end apart: 14, of which 9 were waited for; matrix products, arithmetic and copies ran while one was open for 2% of the time, Pallas kernels for 0%

profile of v1, /device:TPU:32, one launch (start us, length us, event | category | flops | bytes accessed | tf_op | source)
XLA Modules:
  0.0 97.8 jit_solution(16159871207653793880)
XLA Ops:
  0.0 1.2 %copy-done.3 = bf16[4,2,128,512]{3,2,1,0:T(8,128)(2,1)S(1)} copy-done((bf16[4,2,128,512]{3,2,1,0:T(8,128)(2,1)S(1)}, bf16[4,2,128,512]{3,2,1,0:T(8,128)(2,1)}, u32[]{:S(2)}) %copy-start.3) | copy-done | bytes 1048600
  4.1 2.1 %shard_map.109 = (bf16[4,3072]{1,0:T(4,128)(2,1)S(1)}, f32[4,128]{1,0:T(4,128)S(1)}) custom-call(s32[4]{0:T(128)S(1)} %copy-done.8, bf16[4,3072]{1,0:T(4,128)(2,1)S(1)} %copy-done.4, bf16[4,2,512]{2,1,0:T(2,128)(2,1)S(1)} %copy-done.6, bf16[4,2,128,512]{3,2,1,0:T(8,128)(2,1)S(1)} %copy-done.3, bf16[4,3072]{1,0:T(4,128)(2,1)S(1)} %copy-done.5), custom_call_target="tpu_custom_call" | custom-call | flops 50000000 | bytes 1200000 | tf_op jit(solution)/shard_map/pallas_call | solution.py:207
  8.5 15.9 %all_to_all.10 = bf16[8,2,3072]{2,1,0:T(2,128)(2,1)S(1)} all-to-all(bf16[8,2,3072]{2,1,0:T(2,128)(2,1)S(1)} %shard_map.110), channel_id=1, replica_groups=mesh['role'=2,'expert'=8,'x'=4,'y'=4] {'expert'}, dimensions={0} | all-to-all | bytes 196608 | tf_op jit(solution)/shard_map/all_to_all | solution.py:221
  24.5 3.1 %collective-permute-start.3 = (bf16[16,3072]{1,0:T(8,128)(2,1)S(1)}, bf16[16,3072]{1,0:T(8,128)(2,1)S(1)}, u32[]{:S(2)}, u32[]{:S(2)}) collective-permute-start(bf16[16,3072]{1,0:T(8,128)(2,1)S(1)} %reshape.10), channel_id=1, source_target_pairs={{0,8},{1,9},{2,10},{3,11},{4,12},{5,13},{6,14},{7,15},{8,0},{9,1},... | collective-permute-start | bytes 294920 | tf_op jit(solution)/shard_map/ppermute | solution.py:190
  27.6 1.1 %collective-permute-start.2 = (bf16[16,3072]{1,0:T(8,128)(2,1)S(1)}, bf16[16,3072]{1,0:T(8,128)(2,1)S(1)}, u32[]{:S(2)}, u32[]{:S(2)}) collective-permute-start(bf16[16,3072]{1,0:T(8,128)(2,1)S(1)} %reshape.10), channel_id=1, source_target_pairs={{0,12},{1,13},{2,14},{3,15},{4,0},{5,1},{6,2},{7,3},{8,4},{9,5},{1... | collective-permute-start | bytes 294920 | tf_op jit(solution)/shard_map/ppermute | solution.py:190
  29.6 4.9 %collective-permute-done.1 = bf16[16,3072]{1,0:T(8,128)(2,1)S(1)} collective-permute-done((bf16[16,3072]{1,0:T(8,128)(2,1)S(1)}, bf16[16,3072]{1,0:T(8,128)(2,1)S(1)}, u32[]{:S(2)}, u32[]{:S(2)}) %collective-permute-start.1) | collective-permute-done | bytes 98336 | tf_op jit(solution)/shard_map/ppermute | solution.py:190
  34.6 8.4 %collective-permute-start.6 = (bf16[64,3072]{1,0:T(8,128)(2,1)S(1)}, bf16[64,3072]{1,0:T(8,128)(2,1)S(1)}, u32[]{:S(2)}, u32[]{:S(2)}) collective-permute-start(bf16[64,3072]{1,0:T(8,128)(2,1)S(1)} %constant_dynamic-update-slice_fusion.x0), channel_id=1, source_target_pairs={{0,2},{1,3},{2,0},{3,1},{4,6},{5,7},{6,4},{7,5},{8,10},{9,11},{10,... | collective-permute-start | bytes 1179656 | tf_op jit(solution)/shard_map/ppermute | solution.py:190
  43.2 1.9 %collective-permute-start.4 = (bf16[64,3072]{1,0:T(8,128)(2,1)S(1)}, bf16[64,3072]{1,0:T(8,128)(2,1)S(1)}, u32[]{:S(2)}, u32[]{:S(2)}) collective-permute-start(bf16[64,3072]{1,0:T(8,128)(2,1)S(1)} %constant_dynamic-update-slice_fusion.x0), channel_id=1, source_target_pairs={{0,1},{1,2},{2,3},{3,0},{4,5},{5,6},{6,7},{7,4},{8,9},{9,10},{10,1... | collective-permute-start | bytes 1179656 | tf_op jit(solution)/shard_map/ppermute | solution.py:190
  45.1 3.8 %collective-permute-done.6.x3 = bf16[64,3072]{1,0:T(8,128)(2,1)S(1)} collective-permute-done((bf16[64,3072]{1,0:T(8,128)(2,1)S(1)}, bf16[64,3072]{1,0:T(8,128)(2,1)S(1)}, u32[]{:S(2)}, u32[]{:S(2)}) %collective-permute-start.6) | collective-permute-done | bytes 393248 | tf_op jit(solution)/shard_map/ppermute | solution.py:190
  48.9 4.9 %collective-permute-done.5.x2 = bf16[64,3072]{1,0:T(8,128)(2,1)S(1)} collective-permute-done((bf16[64,3072]{1,0:T(8,128)(2,1)S(1)}, bf16[64,3072]{1,0:T(8,128)(2,1)S(1)}, u32[]{:S(2)}, u32[]{:S(2)}) %collective-permute-start.5) | collective-permute-done | bytes 393248 | tf_op jit(solution)/shard_map/ppermute | solution.py:190
  53.8 1.9 %copy-done.1 = bf16[1,3072,512]{2,1,0:T(8,128)(2,1)S(1)} copy-done((bf16[1,3072,512]{2,1,0:T(8,128)(2,1)S(1)}, bf16[1,3072,512]{2,1,0:T(8,128)(2,1)}, u32[]{:S(2)}) %copy-start.1) | copy-done | bytes 3145752
  55.6 1.9 %copy-done.2 = bf16[1,3072,512]{2,1,0:T(8,128)(2,1)S(1)} copy-done((bf16[1,3072,512]{2,1,0:T(8,128)(2,1)S(1)}, bf16[1,3072,512]{2,1,0:T(8,128)(2,1)}, u32[]{:S(2)}) %copy-start.2) | copy-done | bytes 3145752
  57.5 1.8 %shard_map.111 = (f32[256,1024]{1,0:T(8,128)S(1)}, bf16[256,1024]{1,0:T(8,128)(2,1)S(1)}) custom-call(bf16[64,3072]{1,0:T(8,128)(2,1)S(1)} %constant_dynamic-update-slice_fusion.x0, bf16[64,3072]{1,0:T(8,128)(2,1)S(1)} %collective-permute-done.4.x1, bf16[64,3072]{1,0:T(8,128)(2,1)S(1)} %collective-permute-done.5.x2, ...), custom_call_target="tpu_custom_call" | custom-call | flops 1610612736 | bytes 9000000 | tf_op jit(solution)/shard_map/pallas_call | solution.py:225
  59.4 1.9 %collective-permute-done.7.got_ref = bf16[256,1024]{1,0:T(8,128)(2,1)S(1)} collective-permute-done((bf16[256,1024]{1,0:T(8,128)(2,1)S(1)}, bf16[256,1024]{1,0:T(8,128)(2,1)S(1)}, u32[]{:S(2)}, u32[]{:S(2)}) %collective-permute-start.7) | collective-permute-done | bytes 524320 | tf_op jit(solution)/shard_map/ppermute | solution.py:194
  62.4 2.7 %collective-permute-start.8 = (bf16[64,3072]{1,0:T(8,128)(2,1)S(1)}, bf16[64,3072]{1,0:T(8,128)(2,1)S(1)}, u32[]{:S(2)}, u32[]{:S(2)}) collective-permute-start(bf16[64,3072]{1,0:T(8,128)(2,1)S(1)} %get-tuple-element.18), channel_id=1, source_target_pairs={{0,3},{1,0},{2,1},{3,2},{4,7},{5,4},{6,5},{7,6},{8,11},{9,8},{10,9... | collective-permute-start | bytes 1179656 | tf_op jit(solution)/shard_map/ppermute | solution.py:190
  65.1 2.2 %collective-permute-start.10 = (bf16[64,3072]{1,0:T(8,128)(2,1)S(1)}, bf16[64,3072]{1,0:T(8,128)(2,1)S(1)}, u32[]{:S(2)}, u32[]{:S(2)}) collective-permute-start(bf16[64,3072]{1,0:T(8,128)(2,1)S(1)} %get-tuple-element.20), channel_id=1, source_target_pairs={{0,2},{1,3},{2,0},{3,1},{4,6},{5,7},{6,4},{7,5},{8,10},{9,11},{10,... | collective-permute-start | bytes 1179656 | tf_op jit(solution)/shard_map/ppermute | solution.py:190
  67.2 7.4 %collective-permute-done.8 = bf16[64,3072]{1,0:T(8,128)(2,1)S(1)} collective-permute-done((bf16[64,3072]{1,0:T(8,128)(2,1)S(1)}, bf16[64,3072]{1,0:T(8,128)(2,1)S(1)}, u32[]{:S(2)}, u32[]{:S(2)}) %collective-permute-start.8) | collective-permute-done | bytes 393248 | tf_op jit(solution)/shard_map/ppermute | solution.py:190
  74.6 3.7 %collective-permute-done.9 = bf16[64,3072]{1,0:T(8,128)(2,1)S(1)} collective-permute-done((bf16[64,3072]{1,0:T(8,128)(2,1)S(1)}, bf16[64,3072]{1,0:T(8,128)(2,1)S(1)}, u32[]{:S(2)}, u32[]{:S(2)}) %collective-permute-start.9) | collective-permute-done | bytes 393248 | tf_op jit(solution)/shard_map/ppermute | solution.py:190
  78.7 1.9 %collective-permute-start.12 = (bf16[16,3072]{1,0:T(8,128)(2,1)S(1)}, bf16[16,3072]{1,0:T(8,128)(2,1)S(1)}, u32[]{:S(2)}, u32[]{:S(2)}) collective-permute-start(bf16[16,3072]{1,0:T(8,128)(2,1)S(1)} %get-tuple-element.23), channel_id=1, source_target_pairs={{0,4},{1,5},{2,6},{3,7},{4,8},{5,9},{6,10},{7,11},{8,12},{9,13},{1... | collective-permute-start | bytes 294920 | tf_op jit(solution)/shard_map/ppermute | solution.py:190
  80.6 2.6 %collective-permute-done.11 = bf16[16,3072]{1,0:T(8,128)(2,1)S(1)} collective-permute-done((bf16[16,3072]{1,0:T(8,128)(2,1)S(1)}, bf16[16,3072]{1,0:T(8,128)(2,1)S(1)}, u32[]{:S(2)}, u32[]{:S(2)}) %collective-permute-start.11) | collective-permute-done | bytes 98336 | tf_op jit(solution)/shard_map/ppermute | solution.py:190
  83.2 1.6 %collective-permute-done.13 = bf16[16,3072]{1,0:T(8,128)(2,1)S(1)} collective-permute-done((bf16[16,3072]{1,0:T(8,128)(2,1)S(1)}, bf16[16,3072]{1,0:T(8,128)(2,1)S(1)}, u32[]{:S(2)}, u32[]{:S(2)}) %collective-permute-start.13) | collective-permute-done | bytes 98336 | tf_op jit(solution)/shard_map/ppermute | solution.py:190
  84.8 1.1 %collective-permute-done.12 = bf16[16,3072]{1,0:T(8,128)(2,1)S(1)} collective-permute-done((bf16[16,3072]{1,0:T(8,128)(2,1)S(1)}, bf16[16,3072]{1,0:T(8,128)(2,1)S(1)}, u32[]{:S(2)}, u32[]{:S(2)}) %collective-permute-start.12) | collective-permute-done | bytes 98336 | tf_op jit(solution)/shard_map/ppermute | solution.py:190
  86.0 10.4 %all_to_all.11.back_ref = bf16[8,2,3072]{2,1,0:T(2,128)(2,1)S(1)} all-to-all(bf16[8,2,3072]{2,1,0:T(2,128)(2,1)S(1)} %reshape.11), channel_id=1, replica_groups=mesh['role'=2,'expert'=8,'x'=4,'y'=4] {'expert'}, dimensions={0} | all-to-all | bytes 196608 | tf_op jit(solution)/shard_map/all_to_all | solution.py:243
  96.3 1.4 %shard_map.113 = bf16[4,3072]{1,0:T(4,128)(2,1)} custom-call(s32[4,2]{1,0:T(4,128)S(1)} %copy.13.ids_ref, f32[4,8]{1,0:T(4,128)S(1)} %copy-done.7, bf16[4,3072]{1,0:T(4,128)(2,1)S(1)} %get-tuple-element.13.hidden_ref, bf16[8,2,3072]{2,1,0:T(2,128)(2,1)S(1)} %all_to_all.11.back_ref), custom_call_target="tpu_custom_call" | custom-call | flops 100000 | bytes 150000 | tf_op jit(solution)/shard_map/pallas_call | solution.py:246
  (40 shorter events, 7.9 us)
Async XLA Ops:
  0.0 1.2 %copy-start.3 = (bf16[4,2,128,512]{3,2,1,0:T(8,128)(2,1)S(1)}, bf16[4,2,128,512]{3,2,1,0:T(8,128)(2,1)}, u32[]{:S(2)}) copy-start(bf16[4,2,128,512]{3,2,1,0:T(8,128)(2,1)} %kv_ref.1) | copy-start | bytes 3145732
  1.2 0.7 copy-start.4
  2.0 0.7 copy-start.5
  2.7 0.7 copy-start.6
  3.4 0.7 copy-start.8
  6.1 1.6 %collective-permute-start = (f32[4,128]{1,0:T(4,128)S(1)}, f32[4,128]{1,0:T(4,128)S(1)}, u32[]{:S(2)}, u32[]{:S(2)}) collective-permute-start(f32[4,128]{1,0:T(4,128)S(1)} %get-tuple-element.14.sq_ref), channel_id=1, source_target_pairs={{0,128},{128,0},{1,129},{129,1},{2,130},{130,2},{3,131},{131,3},{4... | collective-permute-start | bytes 6152 | tf_op jit(solution)/shard_map/ppermute | solution.py:194
  24.5 10.1 %collective-permute-start.3 = (bf16[16,3072]{1,0:T(8,128)(2,1)S(1)}, bf16[16,3072]{1,0:T(8,128)(2,1)S(1)}, u32[]{:S(2)}, u32[]{:S(2)}) collective-permute-start(bf16[16,3072]{1,0:T(8,128)(2,1)S(1)} %reshape.10), channel_id=1, source_target_pairs={{0,8},{1,9},{2,10},{3,11},{4,12},{5,13},{6,14},{7,15},{8,0},{9,1},... | collective-permute-start | bytes 294920 | tf_op jit(solution)/shard_map/ppermute | solution.py:190
  27.6 7.0 %collective-permute-start.2 = (bf16[16,3072]{1,0:T(8,128)(2,1)S(1)}, bf16[16,3072]{1,0:T(8,128)(2,1)S(1)}, u32[]{:S(2)}, u32[]{:S(2)}) collective-permute-start(bf16[16,3072]{1,0:T(8,128)(2,1)S(1)} %reshape.10), channel_id=1, source_target_pairs={{0,12},{1,13},{2,14},{3,15},{4,0},{5,1},{6,2},{7,3},{8,4},{9,5},{1... | collective-permute-start | bytes 294920 | tf_op jit(solution)/shard_map/ppermute | solution.py:190
  28.7 5.8 %collective-permute-start.1 = (bf16[16,3072]{1,0:T(8,128)(2,1)S(1)}, bf16[16,3072]{1,0:T(8,128)(2,1)S(1)}, u32[]{:S(2)}, u32[]{:S(2)}) collective-permute-start(bf16[16,3072]{1,0:T(8,128)(2,1)S(1)} %reshape.10), channel_id=1, source_target_pairs={{0,4},{1,5},{2,6},{3,7},{4,8},{5,9},{6,10},{7,11},{8,12},{9,13},{1... | collective-permute-start | bytes 294920 | tf_op jit(solution)/shard_map/ppermute | solution.py:190
  34.6 14.2 %collective-permute-start.6 = (bf16[64,3072]{1,0:T(8,128)(2,1)S(1)}, bf16[64,3072]{1,0:T(8,128)(2,1)S(1)}, u32[]{:S(2)}, u32[]{:S(2)}) collective-permute-start(bf16[64,3072]{1,0:T(8,128)(2,1)S(1)} %constant_dynamic-update-slice_fusion.x0), channel_id=1, source_target_pairs={{0,2},{1,3},{2,0},{3,1},{4,6},{5,7},{6,4},{7,5},{8,10},{9,11},{10,... | collective-permute-start | bytes 1179656 | tf_op jit(solution)/shard_map/ppermute | solution.py:190
  43.0 10.7 %collective-permute-start.5 = (bf16[64,3072]{1,0:T(8,128)(2,1)S(1)}, bf16[64,3072]{1,0:T(8,128)(2,1)S(1)}, u32[]{:S(2)}, u32[]{:S(2)}) collective-permute-start(bf16[64,3072]{1,0:T(8,128)(2,1)S(1)} %constant_dynamic-update-slice_fusion.x0), channel_id=1, source_target_pairs={{0,3},{1,0},{2,1},{3,2},{4,7},{5,4},{6,5},{7,6},{8,11},{9,8},{10,9... | collective-permute-start | bytes 1179656 | tf_op jit(solution)/shard_map/ppermute | solution.py:190
  43.2 10.5 %collective-permute-start.4 = (bf16[64,3072]{1,0:T(8,128)(2,1)S(1)}, bf16[64,3072]{1,0:T(8,128)(2,1)S(1)}, u32[]{:S(2)}, u32[]{:S(2)}) collective-permute-start(bf16[64,3072]{1,0:T(8,128)(2,1)S(1)} %constant_dynamic-update-slice_fusion.x0), channel_id=1, source_target_pairs={{0,1},{1,2},{2,3},{3,0},{4,5},{5,6},{6,7},{7,4},{8,9},{9,10},{10,1... | collective-permute-start | bytes 1179656 | tf_op jit(solution)/shard_map/ppermute | solution.py:190
  53.8 1.9 %copy-start.1 = (bf16[1,3072,512]{2,1,0:T(8,128)(2,1)S(1)}, bf16[1,3072,512]{2,1,0:T(8,128)(2,1)}, u32[]{:S(2)}) copy-start(bf16[1,3072,512]{2,1,0:T(8,128)(2,1)} %param.19) | copy-start | bytes 9437188
  55.6 1.9 %copy-start.2 = (bf16[1,3072,512]{2,1,0:T(8,128)(2,1)S(1)}, bf16[1,3072,512]{2,1,0:T(8,128)(2,1)}, u32[]{:S(2)}) copy-start(bf16[1,3072,512]{2,1,0:T(8,128)(2,1)} %param.20) | copy-start | bytes 9437188
  57.5 3.8 %copy-start = (bf16[1,512,3072]{2,1,0:T(8,128)(2,1)S(1)}, bf16[1,512,3072]{2,1,0:T(8,128)(2,1)}, u32[]{:S(2)}) copy-start(bf16[1,512,3072]{2,1,0:T(8,128)(2,1)} %param.21) | copy-start | bytes 9437188
  59.3 2.0 %collective-permute-start.7 = (bf16[256,1024]{1,0:T(8,128)(2,1)S(1)}, bf16[256,1024]{1,0:T(8,128)(2,1)S(1)}, u32[]{:S(2)}, u32[]{:S(2)}) collective-permute-start(bf16[256,1024]{1,0:T(8,128)(2,1)S(1)} %get-tuple-element.16), channel_id=1, source_target_pairs={{0,128},{128,0},{1,129},{129,1},{2,130},{130,2},{3,131},{131,3},{4... | collective-permute-start | bytes 1572872 | tf_op jit(solution)/shard_map/ppermute | solution.py:194
  61.3 35.0 %copy-start.7 = (f32[4,8]{1,0:T(4,128)S(1)}, f32[4,8]{1,0:T(4,128)}, u32[]{:S(2)}) copy-start(f32[4,8]{1,0:T(4,128)} %logit_ref.1) | copy-start | bytes 388
  62.4 12.2 %collective-permute-start.8 = (bf16[64,3072]{1,0:T(8,128)(2,1)S(1)}, bf16[64,3072]{1,0:T(8,128)(2,1)S(1)}, u32[]{:S(2)}, u32[]{:S(2)}) collective-permute-start(bf16[64,3072]{1,0:T(8,128)(2,1)S(1)} %get-tuple-element.18), channel_id=1, source_target_pairs={{0,3},{1,0},{2,1},{3,2},{4,7},{5,4},{6,5},{7,6},{8,11},{9,8},{10,9... | collective-permute-start | bytes 1179656 | tf_op jit(solution)/shard_map/ppermute | solution.py:190
  65.1 13.2 %collective-permute-start.9 = (bf16[64,3072]{1,0:T(8,128)(2,1)S(1)}, bf16[64,3072]{1,0:T(8,128)(2,1)S(1)}, u32[]{:S(2)}, u32[]{:S(2)}) collective-permute-start(bf16[64,3072]{1,0:T(8,128)(2,1)S(1)} %get-tuple-element.19), channel_id=1, source_target_pairs={{0,1},{1,2},{2,3},{3,0},{4,5},{5,6},{6,7},{7,4},{8,9},{9,10},{10,1... | collective-permute-start | bytes 1179656 | tf_op jit(solution)/shard_map/ppermute | solution.py:190
  65.1 13.2 %collective-permute-start.10 = (bf16[64,3072]{1,0:T(8,128)(2,1)S(1)}, bf16[64,3072]{1,0:T(8,128)(2,1)S(1)}, u32[]{:S(2)}, u32[]{:S(2)}) collective-permute-start(bf16[64,3072]{1,0:T(8,128)(2,1)S(1)} %get-tuple-element.20), channel_id=1, source_target_pairs={{0,2},{1,3},{2,0},{3,1},{4,6},{5,7},{6,4},{7,5},{8,10},{9,11},{10,... | collective-permute-start | bytes 1179656 | tf_op jit(solution)/shard_map/ppermute | solution.py:190
  78.5 4.7 %collective-permute-start.11 = (bf16[16,3072]{1,0:T(8,128)(2,1)S(1)}, bf16[16,3072]{1,0:T(8,128)(2,1)S(1)}, u32[]{:S(2)}, u32[]{:S(2)}) collective-permute-start(bf16[16,3072]{1,0:T(8,128)(2,1)S(1)} %get-tuple-element.21), channel_id=1, source_target_pairs={{0,12},{1,13},{2,14},{3,15},{4,0},{5,1},{6,2},{7,3},{8,4},{9,5},{1... | collective-permute-start | bytes 294920 | tf_op jit(solution)/shard_map/ppermute | solution.py:190
  78.6 6.2 %collective-permute-start.13 = (bf16[16,3072]{1,0:T(8,128)(2,1)S(1)}, bf16[16,3072]{1,0:T(8,128)(2,1)S(1)}, u32[]{:S(2)}, u32[]{:S(2)}) collective-permute-start(bf16[16,3072]{1,0:T(8,128)(2,1)S(1)} %get-tuple-element.22), channel_id=1, source_target_pairs={{0,8},{1,9},{2,10},{3,11},{4,12},{5,13},{6,14},{7,15},{8,0},{9,1},... | collective-permute-start | bytes 294920 | tf_op jit(solution)/shard_map/ppermute | solution.py:190
  78.7 7.2 %collective-permute-start.12 = (bf16[16,3072]{1,0:T(8,128)(2,1)S(1)}, bf16[16,3072]{1,0:T(8,128)(2,1)S(1)}, u32[]{:S(2)}, u32[]{:S(2)}) collective-permute-start(bf16[16,3072]{1,0:T(8,128)(2,1)S(1)} %get-tuple-element.23), channel_id=1, source_target_pairs={{0,4},{1,5},{2,6},{3,7},{4,8},{5,9},{6,10},{7,11},{8,12},{9,13},{1... | collective-permute-start | bytes 294920 | tf_op jit(solution)/shard_map/ppermute | solution.py:190

commit v2 on v1

v2 whole, which is shorter than its diff:
```python
import jax
import jax.numpy as jnp
from jax import lax
from jax.experimental import pallas as pl
from jax.experimental.pallas import tpu as pltpu
from jax.sharding import Mesh
from jax.sharding import PartitionSpec as P

MODEL_WIDTH = 6144
HALF = 3072
GROUP = 6
HD = 128
CTX = 128
ROWS = 4
LOCAL_HEADS = 4
EXPERTS = 8
CAP = 2
HIDDEN = 512
AXES = ("role", "expert", "x", "y")
SHIFTS = (0, 1, -1, 2)
VMEM_SPEC = pl.BlockSpec(memory_space=pltpu.VMEM)
HBM_SPEC = pl.BlockSpec(memory_space=pltpu.HBM)
F32 = jnp.float32
BF16 = jnp.bfloat16


def call(body, out_shape, in_specs, flops=0, nbytes=0, scratch=()):
    single = not isinstance(out_shape, (tuple, list))
    out_specs = VMEM_SPEC if single else [VMEM_SPEC] * len(out_shape)
    return pl.pallas_call(
        body,
        out_shape=out_shape,
        in_specs=in_specs,
        out_specs=out_specs,
        scratch_shapes=list(scratch),
        compiler_params=pltpu.CompilerParams(vmem_limit_bytes=16 * 1024 * 1024),
        cost_estimate=pl.CostEstimate(flops=flops, bytes_accessed=nbytes, transcendentals=0),
    )


def in_hbm(value):
    return pltpu.with_memory_space_constraint(value, pltpu.HBM)


def attend_body(
    len_hbm, ids_hbm, logit_hbm, q_hbm, new_hbm, kv_hbm, res_hbm,
    hidden_ref, out_ref, comb_ref,
    len_ref, ids_ref, logit_ref, q_ref, new_ref, k_ref, v_ref, res_ref, sems,
):
    pairs = (
        (kv_hbm.at[:, 0], k_ref),
        (q_hbm, q_ref),
        (len_hbm, len_ref),
        (new_hbm, new_ref),
        (kv_hbm.at[:, 1], v_ref),
        (res_hbm, res_ref),
        (ids_hbm, ids_ref),
        (logit_hbm, logit_ref),
    )
    copies = [pltpu.make_async_copy(a, b, sems.at[i]) for i, (a, b) in enumerate(pairs)]
    for c in copies:
        c.start()
    scale = 1.0 / HD**0.5
    m_rows = GROUP * ROWS
    nt = (((1,), (1,)), ((), ()))
    for c in copies[:4]:
        c.wait()
    row_req = lax.broadcasted_iota(jnp.int32, (m_rows, 1), 0) % ROWS
    row_len = jnp.zeros((m_rows, 1), jnp.int32)
    for r in range(ROWS):
        row_len = jnp.where(row_req == r, len_ref[r], row_len)
    col = lax.broadcasted_iota(jnp.int32, (m_rows, ROWS * CTX), 1)
    valid = (col // CTX == row_req) & (col % CTX < row_len)
    own_valid = lax.broadcasted_iota(jnp.int32, (m_rows, ROWS), 1) == row_req
    new = new_ref[...].astype(F32)
    scores, owns = [], []
    for k in range(LOCAL_HEADS):
        sl = slice(k * HD, (k + 1) * HD)
        q = jnp.concatenate(
            [
                q_ref[:, (k * GROUP + g) * HD : (k * GROUP + g + 1) * HD].astype(F32)
                for g in range(GROUP)
            ],
            axis=0,
        ).astype(BF16)
        keys = k_ref[:, :, sl].reshape(ROWS * CTX, HD)
        nk = new[:, 0, sl].astype(BF16)
        s = lax.dot_general(q, keys, nt, preferred_element_type=F32) * scale
        so = lax.dot_general(q, nk, nt, preferred_element_type=F32) * scale
        scores.append(jnp.where(valid, s, -jnp.inf))
        owns.append(jnp.where(own_valid, so, -jnp.inf))
    tops = [
        jnp.maximum(jnp.max(s, axis=1, keepdims=True), jnp.max(so, axis=1, keepdims=True))
        for s, so in zip(scores, owns)
    ]
    es = [jnp.exp(s - t) for s, t in zip(scores, tops)]
    eos = [jnp.exp(so - t) for so, t in zip(owns, tops)]
    totals = [
        jnp.sum(e, axis=1, keepdims=True) + jnp.sum(eo, axis=1, keepdims=True)
        for e, eo in zip(es, eos)
    ]
    for c in copies[4:]:
        c.wait()
    for k in range(LOCAL_HEADS):
        sl = slice(k * HD, (k + 1) * HD)
        vals = v_ref[:, :, sl].reshape(ROWS * CTX, HD)
        nv = new[:, 1, sl].astype(BF16)
        p = (es[k] / totals[k]).astype(BF16)
        po = (eos[k] / totals[k]).astype(BF16)
        attn = jnp.dot(p, vals, preferred_element_type=F32) + jnp.dot(
            po, nv, preferred_element_type=F32
        )
        for g in range(GROUP):
            h = k * GROUP + g
            hs = slice(h * HD, (h + 1) * HD)
            hidden_ref[:, hs] = (
                res_ref[:, hs].astype(F32) + attn[g * ROWS : (g + 1) * ROWS]
            ).astype(BF16)
    ids = [ids_ref[p % 2, p // 2] for p in range(2 * ROWS)]
    rows = slot_rows(ids)
    ri = lax.broadcasted_iota(jnp.int32, (EXPERTS * CAP, ROWS), 0)
    ci = lax.broadcasted_iota(jnp.int32, (EXPERTS * CAP, ROWS), 1)
    select = jnp.zeros((EXPERTS * CAP, ROWS), F32)
    for p in range(2 * ROWS):
        select = jnp.where((ri == rows[p]) & (ci == p // 2), 1.0, select)
    out = jnp.dot(select.astype(BF16), hidden_ref[...], preferred_element_type=F32).astype(BF16)
    for e in range(EXPERTS):
        for a in range(4):
            out_ref[a * EXPERTS + e] = out[e * CAP : (e + 1) * CAP]
    lane = lax.broadcasted_iota(jnp.int32, (ROWS, HD), 1)
    tok = lax.broadcasted_iota(jnp.int32, (ROWS, HD), 0)
    diff = jnp.zeros((ROWS, HD), F32)
    for t in range(ROWS):
        gap = logit_ref[t, ids[2 * t]] - logit_ref[t, ids[2 * t + 1]]
        diff = jnp.where(tok == t, gap, diff)
    wa, wb = jax.nn.sigmoid(diff), jax.nn.sigmoid(-diff)
    place = lane % (EXPERTS * CAP)
    comb = jnp.zeros((ROWS, HD), F32)
    for t in range(ROWS):
        comb = jnp.where((tok == t) & (place == rows[2 * t]), wa, comb)
        comb = jnp.where((tok == t) & (place == rows[2 * t + 1]), wb, comb)
    high = comb.astype(BF16).astype(F32)
    mid = (comb - high).astype(BF16).astype(F32)
    low = comb - high - mid
    comb_ref[...] = jnp.concatenate([high, mid, low, jnp.zeros_like(low)], axis=0).astype(BF16)


def slot_rows(ids):
    rows = []
    for p in range(len(ids)):
        slot = jnp.int32(0)
        for q in range(p):
            slot = slot + (ids[q] == ids[p]).astype(jnp.int32)
        rows.append(ids[p] * CAP + slot)
    return rows


CHUNK = 512


def weights_body(after_ref, gain_ref, wg_hbm, wu_hbm, wd_hbm, wg_ref, wu_ref, wd_ref, stage, sems):
    del after_ref
    steps = [(i, w) for i in range(HALF // CHUNK) for w in (0, 1)]
    sources, targets = (wg_hbm, wu_hbm), (wg_ref, wu_ref)

    def fetch(n):
        i, w = steps[n]
        return pltpu.make_async_copy(
            sources[w].at[0, pl.ds(i * CHUNK, CHUNK)], stage.at[n], sems.at[n]
        )

    down = pltpu.make_async_copy(wd_hbm.at[0], wd_ref, sems.at[len(steps)])
    for n in range(len(steps)):
        fetch(n).start()
    down.start()
    for n, (i, w) in enumerate(steps):
        fetch(n).wait()
        for r in range(CHUNK // HD):
            at = i * CHUNK + r * HD
            row = gain_ref[:, at : at + HD].astype(F32)
            tile = jnp.transpose(jnp.broadcast_to(row, (HD, HD)))
            for c in range(HIDDEN // HD):
                cs = slice(c * HD, (c + 1) * HD)
                part = stage[n, r * HD : (r + 1) * HD, cs].astype(F32) * tile
                targets[w][at : at + HD, cs] = part.astype(BF16)
    down.wait()


def gate_body(x0, x1, wg_ref, wu_ref, own_ref, sq_ref, send_ref):
    half = x0.shape[0]
    x = jnp.concatenate([x0[...], x1[...]], axis=0)
    for at, w_ref in ((0, wg_ref), (HIDDEN, wu_ref)):
        got = jnp.dot(x, w_ref[...], preferred_element_type=F32)
        own_ref[:, at : at + HIDDEN] = got
        send_ref[:, at : at + HIDDEN] = got.astype(BF16)
    lane = lax.broadcasted_iota(jnp.int32, (half, HD), 1)
    for n, x_ref in enumerate((x0, x1)):
        acc = jnp.zeros((half, HD), F32)
        for c in range(0, HALF, HD):
            part = x_ref[:, c : c + HD].astype(F32)
            acc = acc + part * part
        total = jnp.broadcast_to(jnp.sum(acc, axis=1, keepdims=True), (half, HD))
        high = total.astype(BF16).astype(F32)
        low = jnp.where(high < jnp.inf, total - high, 0.0)
        sq_ref[n * half : (n + 1) * half] = total
        send_ref[n * half : (n + 1) * half, 2 * HIDDEN :] = jnp.where(
            lane < HD // 2, high, low
        ).astype(BF16)


PLACES = {0: (0, 0), 3: (0, 64), 1: (1, 0), 2: (1, 64)}


def coordinates():
    role, x, y = (lax.axis_index(n) for n in ("role", "x", "y"))
    return jnp.where(role == 0, x, y), jnp.where(role == 0, y, x)


def block_at(start, place, shift):
    return pl.ds(pl.multiple_of(start + lax.rem(place - shift + 4, 4) * 16, 16), 16)


def down_body(own0, sq0, own1, sq1, got0, got1, wd_ref, o0, o1, o2, o3, act_ref):
    owns, sqs, gots = (own0, own1), (sq0, sq1), (got0, got1)
    my_a, my_b = coordinates()
    for jb in range(4):
        for ja in range(4):
            h, at = PLACES[jb]
            ph, pat = PLACES[ja]
            mine = block_at(at, my_a, SHIFTS[ja])
            peer = block_at(pat, my_b, SHIFTS[jb])
            got = gots[ph][peer].astype(F32)
            lane = 2 * HIDDEN
            extra = got[:, lane : lane + 1] + got[:, lane + HD // 2 : lane + HD // 2 + 1]
            total = sqs[h][mine][:, :1] + extra
            inv = lax.rsqrt(total / MODEL_WIDTH + 1e-05)
            pre = owns[h][mine] + got[:, : 2 * HIDDEN]
            pre = jnp.where(inv > 0.0, pre * inv, 0.0)
            gate = pre[:, :HIDDEN]
            place = (jb * 4 + ja) * 16
            act_ref[place : place + 16] = (gate * jax.nn.sigmoid(gate) * pre[:, HIDDEN:]).astype(BF16)
    outs = (o0, o1, o2, o3)
    act = act_ref[...]
    for n in range(0, HALF, 512):
        got = jnp.dot(act, wd_ref[:, n : n + 512], preferred_element_type=F32).astype(BF16)
        for j in range(4):
            outs[j][:, n : n + 512] = got[j * 64 : (j + 1) * 64]


def gather_body(t0, t1, t2, t3, out_ref):
    my_a, _ = coordinates()
    for ja in range(4):
        at = slice(16 * ja, 16 * ja + 16)
        total = t0[at].astype(F32) + t1[at].astype(F32) + t2[at].astype(F32) + t3[at].astype(F32)
        out_ref[block_at(0, my_a, SHIFTS[ja])] = total.astype(BF16)


def combine_body(comb_ref, hidden_ref, back_ref, out_ref):
    got = jnp.dot(comb_ref[:, :64], back_ref[...], preferred_element_type=F32)
    moe = got[:ROWS] + got[ROWS : 2 * ROWS] + got[2 * ROWS : 3 * ROWS]
    out_ref[...] = (hidden_ref[...].astype(F32) + moe).astype(BF16)


def index_of(role, z, x, y):
    return ((role * 8 + z) * 4 + x) * 4 + y


def permutation(move):
    return [
        (index_of(r, z, x, y), index_of(*move(r, z, x, y)))
        for r in range(2)
        for z in range(8)
        for x in range(4)
        for y in range(4)
    ]


def along_x(s, r, z, x, y):
    return r, z, (x + s) % 4, y


def along_y(s, r, z, x, y):
    return r, z, x, (y + s) % 4


def send(value, s):
    return lax.ppermute(
        value,
        AXES,
        permutation(lambda r, z, x, y: along_y(s, r, z, x, y) if r == 0 else along_x(s, r, z, x, y)),
    )


def swap(value):
    return lax.ppermute(value, "role", [(0, 1), (1, 0)])


def exchange(value):
    groups = [[index_of(0, z, x, y) for x in range(4) for z in range(8)] for y in range(4)]
    groups += [[index_of(1, z, x, y) for y in range(4) for z in range(8)] for x in range(4)]
    return lax.all_to_all(
        value, AXES, split_axis=0, concat_axis=0, axis_index_groups=groups, tiled=True
    )


def per_device(
    query, new_kv, kv_cache, lengths, residual, norm_gain, expert_ids, router_logits, w_gate, w_up, w_down
):
    shape = jax.ShapeDtypeStruct
    hidden, outgoing, comb = call(
        attend_body,
        (shape((ROWS, HALF), BF16), shape((4 * EXPERTS, CAP, HALF), BF16), shape((4 * ROWS, HD), BF16)),
        [HBM_SPEC] * 7,
        flops=50_000_000,
        nbytes=1_200_000,
        scratch=[
            pltpu.SMEM((ROWS,), jnp.int32),
            pltpu.SMEM((2, ROWS), jnp.int32),
            pltpu.SMEM((ROWS, EXPERTS), F32),
            pltpu.VMEM((ROWS, HALF), BF16),
            pltpu.VMEM((ROWS, 2, HIDDEN), BF16),
            pltpu.VMEM((ROWS, CTX, HIDDEN), BF16),
            pltpu.VMEM((ROWS, CTX, HIDDEN), BF16),
            pltpu.VMEM((ROWS, HALF), BF16),
            pltpu.SemaphoreType.DMA((8,)),
        ],
    )(*map(in_hbm, (lengths, expert_ids.T, router_logits, query, new_kv, kv_cache, residual)))
    plane = exchange(outgoing).reshape(64, HALF)
    count = 2 * HALF // CHUNK
    wg, wu, wd = call(
        weights_body,
        (
            pltpu.VMEM((HALF, HIDDEN), BF16),
            pltpu.VMEM((HALF, HIDDEN), BF16),
            pltpu.VMEM((HIDDEN, HALF), BF16),
        ),
        [HBM_SPEC, VMEM_SPEC, HBM_SPEC, HBM_SPEC, HBM_SPEC],
        flops=20_000_000,
        nbytes=18_000_000,
        scratch=[
            pltpu.VMEM((count, CHUNK, HIDDEN), BF16),
            pltpu.SemaphoreType.DMA((count + 1,)),
        ],
    )(plane, norm_gain.reshape(1, HALF), *map(in_hbm, (w_gate, w_up, w_down)))
    pieces = [plane] + [send(plane, s) for s in SHIFTS[1:]]

    def gate(x0, x1):
        return call(
            gate_body,
            (shape((128, 2 * HIDDEN), F32), shape((128, HD), F32), shape((128, 2 * HIDDEN + HD), BF16)),
            [VMEM_SPEC] * 4,
            flops=2 * 128 * HALF * 1024,
            nbytes=8_000_000,
        )(x0, x1, wg, wu)

    own0, sq0, send0 = gate(pieces[0], pieces[3])
    own1, sq1, send1 = gate(pieces[1], pieces[2])
    terms = call(
        down_body,
        [shape((64, HALF), BF16)] * 4,
        [VMEM_SPEC] * 7,
        flops=2 * 256 * HALF * 512,
        nbytes=6_000_000,
        scratch=[pltpu.VMEM((256, HIDDEN), BF16)],
    )(own0, sq0, own1, sq1, swap(send0), swap(send1), wd)
    summed = call(
        gather_body,
        shape((64, HALF), BF16),
        [VMEM_SPEC] * 4,
        flops=800_000,
        nbytes=2_000_000,
    )(terms[0], *[send(terms[j], -SHIFTS[j]) for j in (1, 2, 3)])
    back = exchange(summed.reshape(4 * EXPERTS, CAP, HALF)).reshape(64, HALF)
    return call(
        combine_body,
        shape((ROWS, HALF), BF16),
        [VMEM_SPEC] * 3,
        flops=100_000,
        nbytes=150_000,
    )(comb, hidden, back)


def solution(mesh):
    fine = Mesh(mesh.devices.reshape(2, 8, 4, 4), AXES)
    rows = ("expert", "x", "y")
    shard = ("x", "y")
    in_specs = (
        P(rows, "role"),
        P(rows, None, "role"),
        P(rows, None, None, "role"),
        P(rows),
        P(rows, "role"),
        P("role"),
        P(rows, None),
        P(rows, None),
        P("expert", "role", shard),
        P("expert", "role", shard),
        P("expert", shard, "role"),
    )
    return jax.shard_map(
        per_device, mesh=fine, in_specs=in_specs, out_specs=P(rows, "role"), check_vma=False
    )
```

time: 99 us -> 82 us (0.83)
  blocking collectives: 26.3 us -> 43.3 us
  starting transfers between devices: 22.7 us -> 7.87 us
  waiting for transfers between devices: 31.8 us -> 18.8 us
  local copies, waits for them, and re-layouts: 9.44 us -> 1.14 us
  Pallas kernels: 7.1 us -> 10.2 us
    all_to_all x2, blocking collectives: 26.3 us -> 43.3 us  [exchange(): lax.all_to_all(value, AXES, split_axis=0, concat_axis=0, axis_index_group...]
    ppermute x12 -> x6, starting transfers between devices: 22.5 us -> 7.23 us  [send(): lax.ppermute(value, AXES, permutation(lambda r, z, x, y: along_y(s, r, z,...]
    ppermute x12 -> x6, waiting for transfers between devices: 29.9 us -> 17.6 us  [send(): lax.ppermute(value, AXES, permutation(lambda r, z, x, y: along_y(s, r, z,...]
    unnamed x22 -> x0, local copies, waits for them, and re-layouts: 8.63 us -> none
    pallas_call x5 -> x7, Pallas kernels: 7.1 us -> 10.2 us  [the longest x1 3.91 us: per_device(): call(weights_body, (pltpu.VMEM((HALF, HIDDEN), BF16), pltpu.VMEM((HALF, H...]
  transfers between devices with their start and end apart: 14 -> 8, of which waited for: 9 -> 5; matrix products, arithmetic and copies ran while one was open for 2% -> 1% of each run, Pallas kernels for 0% -> 7%
where the time goes in v2:
time: 82 us; the launch traced here: 81.4 us
  blocking collectives  43.3 us (53%)
  waiting for transfers between devices  18.8 us (23%)
  Pallas kernels  10.2 us (12%)
  starting transfers between devices  7.87 us (10%)
  local copies, waits for them, and re-layouts  1.14 us (1%)
    all_to_all x2, blocking collectives, exchange(): lax.all_to_all(value, AXES, split_axis=0, concat_axis=0, axis_index_group...  43.3 us
    ppermute x6, waiting for transfers between devices, send(): lax.ppermute(value, AXES, permutation(lambda r, z, x, y: along_y(s, r, z,...  17.6 us
    ppermute x6, starting transfers between devices, send(): lax.ppermute(value, AXES, permutation(lambda r, z, x, y: along_y(s, r, z,...  7.23 us
    pallas_call x1, Pallas kernels, per_device(): call(weights_body, (pltpu.VMEM((HALF, HIDDEN), BF16), pltpu.VMEM((HALF, H...  3.91 us
    pallas_call x2, Pallas kernels, gate(): call(gate_body, (shape((128, 2 * HIDDEN), F32), shape((128, HD), F32), sh...  2.13 us
    pallas_call x1, Pallas kernels, per_device(): call(attend_body, (shape((ROWS, HALF), BF16), shape((4 * EXPERTS, CAP, HA...  1.97 us
  transfers between devices with their start and end apart: 8, of which 5 were waited for; matrix products, arithmetic and copies ran while one was open for 1% of the time, Pallas kernels for 7%

profile of v2, /device:TPU:32, one launch (start us, length us, event | category | flops | bytes accessed | tf_op | source)
XLA Modules:
  0.0 81.4 jit_solution(187302156536524071)
XLA Ops:
  0.0 2.0 %shard_map.109 = (bf16[4,3072]{1,0:T(4,128)(2,1)S(1)}, bf16[32,2,3072]{2,1,0:T(2,128)(2,1)S(1)}, bf16[16,128]{1,0:T(8,128)(2,1)S(1)}) custom-call(s32[4]{0:T(128)} %len_hbm.1, s32[2,4]{1,0:T(2,128)} %bitcast.1, f32[4,8]{1,0:T(4,128)} %logit_hbm.1, bf16[4,3072]{1,0:T(4,128)(2,1)} %q_hbm.1, bf16[4,2,512]{2,1,0:T(2,128)(2,1)} %new_hbm.1, ...), custom_call_target="tpu_custom_call" | custom-call | flops 50000000 | bytes 1200000 | tf_op jit(solution)/shard_map/pallas_call | solution.py:310
  2.0 26.0 %all_to_all.10 = bf16[32,2,3072]{2,1,0:T(2,128)(2,1)S(1)} all-to-all(bf16[32,2,3072]{2,1,0:T(2,128)(2,1)S(1)} %get-tuple-element.23), channel_id=1, replica_groups={{0,16,32,48,64,80,96,112,4,20,36,52,68,84,100,116,8,24,40,56,72,88,104,..., dimensions={0} | all-to-all | bytes 786432 | tf_op jit(solution)/shard_map/all_to_all | solution.py:301
  28.0 0.1 reshape.12.after_ref.x0
  28.2 2.9 %collective-permute-start.2 = (bf16[64,3072]{1,0:T(8,128)(2,1)S(1)}, bf16[64,3072]{1,0:T(8,128)(2,1)S(1)}, u32[]{:S(2)}, u32[]{:S(2)}) collective-permute-start(bf16[64,3072]{1,0:T(8,128)(2,1)S(1)} %reshape.12.after_ref.x0), channel_id=1, source_target_pairs={{0,3},{1,0},{2,1},{3,2},{4,7},{5,4},{6,5},{7,6},{8,11},{9,8},{10,9... | collective-permute-start | bytes 1179656 | tf_op jit(solution)/shard_map/ppermute | solution.py:287
  31.0 2.3 %collective-permute-start = (bf16[64,3072]{1,0:T(8,128)(2,1)S(1)}, bf16[64,3072]{1,0:T(8,128)(2,1)S(1)}, u32[]{:S(2)}, u32[]{:S(2)}) collective-permute-start(bf16[64,3072]{1,0:T(8,128)(2,1)S(1)} %reshape.12.after_ref.x0), channel_id=1, source_target_pairs={{0,2},{1,3},{2,0},{3,1},{4,6},{5,7},{6,4},{7,5},{8,10},{9,11},{10,... | collective-permute-start | bytes 1179656 | tf_op jit(solution)/shard_map/ppermute | solution.py:287
  33.3 0.7 reshape.13.gain_ref
  34.0 3.9 %shard_map.110 = (bf16[3072,512]{1,0:T(8,128)(2,1)S(1)}, bf16[3072,512]{1,0:T(8,128)(2,1)S(1)}, bf16[512,3072]{1,0:T(8,128)(2,1)S(1)}) custom-call(bf16[64,3072]{1,0:T(8,128)(2,1)S(1)} %reshape.12.after_ref.x0, bf16[1,3072]{1,0:T(2,128)(2,1)S(1)} %reshape.13.gain_ref, bf16[1,3072,512]{2,1,0:T(8,128)(2,1)} %wg_hbm.1, bf16[1,3072,512]{2,1,0:T(8,128)(2,1)} %wu_hbm.1, ...), custom_call_target="tpu_custom_call" | custom-call | flops 20000000 | bytes 18000000 | tf_op jit(solution)/shard_map/pallas_call | solution.py:330
  37.9 2.7 %collective-permute-done.2.x1 = bf16[64,3072]{1,0:T(8,128)(2,1)S(1)} collective-permute-done((bf16[64,3072]{1,0:T(8,128)(2,1)S(1)}, bf16[64,3072]{1,0:T(8,128)(2,1)S(1)}, u32[]{:S(2)}, u32[]{:S(2)}) %collective-permute-start.2) | collective-permute-done | bytes 393248 | tf_op jit(solution)/shard_map/ppermute | solution.py:287
  40.6 3.7 %collective-permute-done.1.x0 = bf16[64,3072]{1,0:T(8,128)(2,1)S(1)} collective-permute-done((bf16[64,3072]{1,0:T(8,128)(2,1)S(1)}, bf16[64,3072]{1,0:T(8,128)(2,1)S(1)}, u32[]{:S(2)}, u32[]{:S(2)}) %collective-permute-start.1) | collective-permute-done | bytes 393248 | tf_op jit(solution)/shard_map/ppermute | solution.py:287
  44.2 1.1 %shard_map.112 = (f32[128,1024]{1,0:T(8,128)S(1)}, f32[128,128]{1,0:T(8,128)S(1)}, bf16[128,1152]{1,0:T(8,128)(2,1)S(1)}) custom-call(bf16[64,3072]{1,0:T(8,128)(2,1)S(1)} %collective-permute-done.1.x0, bf16[64,3072]{1,0:T(8,128)(2,1)S(1)} %collective-permute-done.2.x1, bf16[3072,512]{1,0:T(8,128)(2,1)S(1)} %get-tuple-element.24.wg_ref, ...), custom_call_target="tpu_custom_call" | custom-call | flops 805306368 | bytes 8000000 | tf_op jit(solution)/shard_map/pallas_call | solution.py:348
  45.3 0.1 collective-permute-start.4
  45.4 1.1 %shard_map.111 = (f32[128,1024]{1,0:T(8,128)S(1)}, f32[128,128]{1,0:T(8,128)S(1)}, bf16[128,1152]{1,0:T(8,128)(2,1)S(1)}) custom-call(bf16[64,3072]{1,0:T(8,128)(2,1)S(1)} %reshape.12.after_ref.x0, bf16[64,3072]{1,0:T(8,128)(2,1)S(1)} %collective-permute-done.x1, bf16[3072,512]{1,0:T(8,128)(2,1)S(1)} %get-tuple-element.24.wg_ref, ...), custom_call_target="tpu_custom_call" | custom-call | flops 805306368 | bytes 8000000 | tf_op jit(solution)/shard_map/pallas_call | solution.py:348
  46.5 0.6 collective-permute-start.3
  47.0 1.2 %collective-permute-done.3.got0 = bf16[128,1152]{1,0:T(8,128)(2,1)S(1)} collective-permute-done((bf16[128,1152]{1,0:T(8,128)(2,1)S(1)}, bf16[128,1152]{1,0:T(8,128)(2,1)S(1)}, u32[]{:S(2)}, u32[]{:S(2)}) %collective-permute-start.3) | collective-permute-done | bytes 294944 | tf_op jit(solution)/shard_map/ppermute | solution.py:295
  48.2 1.2 %shard_map.113 = (bf16[64,3072]{1,0:T(8,128)(2,1)S(1)}, bf16[64,3072]{1,0:T(8,128)(2,1)S(1)}, bf16[64,3072]{1,0:T(8,128)(2,1)S(1)}, bf16[64,3072]{1,0:T(8,128)(2,1)S(1)}) custom-call(f32[128,1024]{1,0:T(8,128)S(1)} %get-tuple-element.26.own0, f32[128,128]{1,0:T(8,128)S(1)} %get-tuple-element.27.sq0, f32[128,1024]{1,0:T(8,128)S(1)} %get-tuple-element.28.own1, ...), custom_call_target="tpu_custom_call" | custom-call | flops 805306368 | bytes 6000000 | tf_op jit(solution)/shard_map/pallas_call | solution.py:358
  49.5 0.1 collective-permute-start.5
  49.6 2.0 %collective-permute-start.6 = (bf16[64,3072]{1,0:T(8,128)(2,1)S(1)}, bf16[64,3072]{1,0:T(8,128)(2,1)S(1)}, u32[]{:S(2)}, u32[]{:S(2)}) collective-permute-start(bf16[64,3072]{1,0:T(8,128)(2,1)S(1)} %get-tuple-element.35), channel_id=1, source_target_pairs={{0,1},{1,2},{2,3},{3,0},{4,5},{5,6},{6,7},{7,4},{8,9},{9,10},{10,1... | collective-permute-start | bytes 1179656 | tf_op jit(solution)/shard_map/ppermute | solution.py:287
  51.6 5.7 %collective-permute-done.5.t1 = bf16[64,3072]{1,0:T(8,128)(2,1)S(1)} collective-permute-done((bf16[64,3072]{1,0:T(8,128)(2,1)S(1)}, bf16[64,3072]{1,0:T(8,128)(2,1)S(1)}, u32[]{:S(2)}, u32[]{:S(2)}) %collective-permute-start.5) | collective-permute-done | bytes 393248 | tf_op jit(solution)/shard_map/ppermute | solution.py:287
  57.3 5.5 %collective-permute-done.6.t2 = bf16[64,3072]{1,0:T(8,128)(2,1)S(1)} collective-permute-done((bf16[64,3072]{1,0:T(8,128)(2,1)S(1)}, bf16[64,3072]{1,0:T(8,128)(2,1)S(1)}, u32[]{:S(2)}, u32[]{:S(2)}) %collective-permute-start.6) | collective-permute-done | bytes 393248 | tf_op jit(solution)/shard_map/ppermute | solution.py:287
  62.9 0.2 shard_map.114
  63.1 0.1 reshape.14
  63.2 17.2 %all_to_all.11 = bf16[32,2,3072]{2,1,0:T(2,128)(2,1)S(1)} all-to-all(bf16[32,2,3072]{2,1,0:T(2,128)(2,1)S(1)} %reshape.14), channel_id=1, replica_groups={{0,16,32,48,64,80,96,112,4,20,36,52,68,84,100,116,8,24,40,56,72,88,104,..., dimensions={0} | all-to-all | bytes 786432 | tf_op jit(solution)/shard_map/all_to_all | solution.py:301
  80.5 0.1 reshape.15.back_ref
  80.6 0.8 shard_map.115
  (5 shorter events, 0.0 us)
Async XLA Ops:
  28.2 12.4 %collective-permute-start.2 = (bf16[64,3072]{1,0:T(8,128)(2,1)S(1)}, bf16[64,3072]{1,0:T(8,128)(2,1)S(1)}, u32[]{:S(2)}, u32[]{:S(2)}) collective-permute-start(bf16[64,3072]{1,0:T(8,128)(2,1)S(1)} %reshape.12.after_ref.x0), channel_id=1, source_target_pairs={{0,3},{1,0},{2,1},{3,2},{4,7},{5,4},{6,5},{7,6},{8,11},{9,8},{10,9... | collective-permute-start | bytes 1179656 | tf_op jit(solution)/shard_map/ppermute | solution.py:287
  31.0 13.2 %collective-permute-start.1 = (bf16[64,3072]{1,0:T(8,128)(2,1)S(1)}, bf16[64,3072]{1,0:T(8,128)(2,1)S(1)}, u32[]{:S(2)}, u32[]{:S(2)}) collective-permute-start(bf16[64,3072]{1,0:T(8,128)(2,1)S(1)} %reshape.12.after_ref.x0), channel_id=1, source_target_pairs={{0,1},{1,2},{2,3},{3,0},{4,5},{5,6},{6,7},{7,4},{8,9},{9,10},{10,1... | collective-permute-start | bytes 1179656 | tf_op jit(solution)/shard_map/ppermute | solution.py:287
  31.0 14.3 %collective-permute-start = (bf16[64,3072]{1,0:T(8,128)(2,1)S(1)}, bf16[64,3072]{1,0:T(8,128)(2,1)S(1)}, u32[]{:S(2)}, u32[]{:S(2)}) collective-permute-start(bf16[64,3072]{1,0:T(8,128)(2,1)S(1)} %reshape.12.after_ref.x0), channel_id=1, source_target_pairs={{0,2},{1,3},{2,0},{3,1},{4,6},{5,7},{6,4},{7,5},{8,10},{9,11},{10,... | collective-permute-start | bytes 1179656 | tf_op jit(solution)/shard_map/ppermute | solution.py:287
  45.3 1.7 %collective-permute-start.4 = (bf16[128,1152]{1,0:T(8,128)(2,1)S(1)}, bf16[128,1152]{1,0:T(8,128)(2,1)S(1)}, u32[]{:S(2)}, u32[]{:S(2)}) collective-permute-start(bf16[128,1152]{1,0:T(8,128)(2,1)S(1)} %get-tuple-element.31), channel_id=1, source_target_pairs={{0,128},{128,0},{1,129},{129,1},{2,130},{130,2},{3,131},{131,3},{4... | collective-permute-start | bytes 884744 | tf_op jit(solution)/shard_map/ppermute | solution.py:295
  46.5 1.8 %collective-permute-start.3 = (bf16[128,1152]{1,0:T(8,128)(2,1)S(1)}, bf16[128,1152]{1,0:T(8,128)(2,1)S(1)}, u32[]{:S(2)}, u32[]{:S(2)}) collective-permute-start(bf16[128,1152]{1,0:T(8,128)(2,1)S(1)} %get-tuple-element.30), channel_id=1, source_target_pairs={{0,128},{128,0},{1,129},{129,1},{2,130},{130,2},{3,131},{131,3},{4... | collective-permute-start | bytes 884744 | tf_op jit(solution)/shard_map/ppermute | solution.py:295
  49.5 7.9 %collective-permute-start.5 = (bf16[64,3072]{1,0:T(8,128)(2,1)S(1)}, bf16[64,3072]{1,0:T(8,128)(2,1)S(1)}, u32[]{:S(2)}, u32[]{:S(2)}) collective-permute-start(bf16[64,3072]{1,0:T(8,128)(2,1)S(1)} %get-tuple-element.34), channel_id=1, source_target_pairs={{0,3},{1,0},{2,1},{3,2},{4,7},{5,4},{6,5},{7,6},{8,11},{9,8},{10,9... | collective-permute-start | bytes 1179656 | tf_op jit(solution)/shard_map/ppermute | solution.py:287
  49.6 13.3 %collective-permute-start.6 = (bf16[64,3072]{1,0:T(8,128)(2,1)S(1)}, bf16[64,3072]{1,0:T(8,128)(2,1)S(1)}, u32[]{:S(2)}, u32[]{:S(2)}) collective-permute-start(bf16[64,3072]{1,0:T(8,128)(2,1)S(1)} %get-tuple-element.35), channel_id=1, source_target_pairs={{0,1},{1,2},{2,3},{3,0},{4,5},{5,6},{6,7},{7,4},{8,9},{9,10},{10,1... | collective-permute-start | bytes 1179656 | tf_op jit(solution)/shard_map/ppermute | solution.py:287
  51.6 11.3 %collective-permute-start.7 = (bf16[64,3072]{1,0:T(8,128)(2,1)S(1)}, bf16[64,3072]{1,0:T(8,128)(2,1)S(1)}, u32[]{:S(2)}, u32[]{:S(2)}) collective-permute-start(bf16[64,3072]{1,0:T(8,128)(2,1)S(1)} %get-tuple-element.36), channel_id=1, source_target_pairs={{0,2},{1,3},{2,0},{3,1},{4,6},{5,7},{6,4},{7,5},{8,10},{9,11},{10,... | collective-permute-start | bytes 1179656 | tf_op jit(solution)/shard_map/ppermute | solution.py:287

commit v3 on v2

--- a/solution.py
+++ b/solution.py
@@ -17,7 +17,8 @@
 CAP = 2
 HIDDEN = 512
 AXES = ("role", "expert", "x", "y")
-SHIFTS = (0, 1, -1, 2)
+ORDER = (2, 1, -1)
+SHIFTS = (0,) + ORDER
 VMEM_SPEC = pl.BlockSpec(memory_space=pltpu.VMEM)
 HBM_SPEC = pl.BlockSpec(memory_space=pltpu.HBM)
 F32 = jnp.float32
@@ -125,7 +126,7 @@
         select = jnp.where((ri == rows[p]) & (ci == p // 2), 1.0, select)
     out = jnp.dot(select.astype(BF16), hidden_ref[...], preferred_element_type=F32).astype(BF16)
     for e in range(EXPERTS):
-        for a in range(4):
+        for a in range(2):
             out_ref[a * EXPERTS + e] = out[e * CAP : (e + 1) * CAP]
     lane = lax.broadcasted_iota(jnp.int32, (ROWS, HD), 1)
     tok = lax.broadcasted_iota(jnp.int32, (ROWS, HD), 0)
@@ -155,60 +156,75 @@
     return rows
 
 
-CHUNK = 512
-
-
-def weights_body(after_ref, gain_ref, wg_hbm, wu_hbm, wd_hbm, wg_ref, wu_ref, wd_ref, stage, sems):
-    del after_ref
-    steps = [(i, w) for i in range(HALF // CHUNK) for w in (0, 1)]
+CHUNK = 768
+PART = 32
+
+
+def scale_rows(x_ref, gain, scaled_ref, at, sq_ref, send_ref):
+    lane = lax.broadcasted_iota(jnp.int32, (PART, HD), 1)
+    acc = jnp.zeros((PART, HD), F32)
+    for c in range(0, HALF, HD):
+        part = x_ref[:, c : c + HD].astype(F32)
+        acc = acc + part * part
+        scaled_ref[at : at + PART, c : c + HD] = (part * gain(c)).astype(BF16)
+    total = jnp.broadcast_to(jnp.sum(acc, axis=1, keepdims=True), (PART, HD))
+    high = total.astype(BF16).astype(F32)
+    low = jnp.where(high < jnp.inf, total - high, 0.0)
+    sq_ref[at : at + PART] = total
+    send_ref[at : at + PART, 2 * HIDDEN :] = jnp.where(lane < HD // 2, high, low).astype(BF16)
+
+
+def first_body(*refs):
+    xs, (gain_hbm, wg_hbm, wu_hbm, wd_hbm) = refs[:5], refs[5:9]
+    own_ref, sq_ref, send_ref, gain_out, wg_ref, wu_ref, wd_ref = refs[9:16]
+    gain_ref, scaled_ref, sems = refs[16:]
+    steps = [(k, w) for k in range(0, HALF, CHUNK) for w in (0, 1)]
     sources, targets = (wg_hbm, wu_hbm), (wg_ref, wu_ref)
 
     def fetch(n):
-        i, w = steps[n]
-        return pltpu.make_async_copy(
-            sources[w].at[0, pl.ds(i * CHUNK, CHUNK)], stage.at[n], sems.at[n]
+        k, w = steps[n]
+        rows = pl.ds(k, CHUNK)
+        return pltpu.make_async_copy(sources[w].at[0, rows], targets[w].at[rows], sems.at[n])
+
+    count = len(steps)
+    gain_copy = pltpu.make_async_copy(gain_hbm, gain_ref, sems.at[count])
+    down_copy = pltpu.make_async_copy(wd_hbm.at[0], wd_ref, sems.at[count + 1])
+    gain_copy.start()
+    for n in range(count):
+        fetch(n).start()
+    down_copy.start()
+    gain_copy.wait()
+    for c in range(0, HALF, HD):
+        gain_out[:, c : c + HD] = gain_ref[pl.ds(c, HD)].astype(F32).reshape(1, HD)
+    for n, x_ref in enumerate(xs):
+        scale_rows(
+            x_ref, lambda c: gain_out[:, c : c + HD], scaled_ref, n * PART, sq_ref, send_ref
         )
-
-    down = pltpu.make_async_copy(wd_hbm.at[0], wd_ref, sems.at[len(steps)])
-    for n in range(len(steps)):
-        fetch(n).start()
-    down.start()
-    for n, (i, w) in enumerate(steps):
+    for n, (k, w) in enumerate(steps):
         fetch(n).wait()
-        for r in range(CHUNK // HD):
-            at = i * CHUNK + r * HD
-            row = gain_ref[:, at : at + HD].astype(F32)
-            tile = jnp.transpose(jnp.broadcast_to(row, (HD, HD)))
-            for c in range(HIDDEN // HD):
-                cs = slice(c * HD, (c + 1) * HD)
-                part = stage[n, r * HD : (r + 1) * HD, cs].astype(F32) * tile
-                targets[w][at : at + HD, cs] = part.astype(BF16)
-    down.wait()
-
-
-def gate_body(x0, x1, wg_ref, wu_ref, own_ref, sq_ref, send_ref):
-    half = x0.shape[0]
-    x = jnp.concatenate([x0[...], x1[...]], axis=0)
+        rows = slice(k, k + CHUNK)
+        at = slice(w * HIDDEN, (w + 1) * HIDDEN)
+        got = jnp.dot(scaled_ref[:, rows], targets[w][rows], preferred_element_type=F32)
+        if k:
+            got = got + own_ref[:, at]
+        own_ref[:, at] = got
+        if k + CHUNK == HALF:
+            send_ref[:, at] = got.astype(BF16)
+    down_copy.wait()
+
+
+def second_body(*refs):
+    xs, (gain_ref, wg_ref, wu_ref) = refs[:3], refs[3:6]
+    own_ref, sq_ref, send_ref, scaled_ref = refs[6:]
+    for n, x_ref in enumerate(xs):
+        scale_rows(
+            x_ref, lambda c: gain_ref[:, c : c + HD], scaled_ref, n * PART, sq_ref, send_ref
+        )
+    x = scaled_ref[...]
     for at, w_ref in ((0, wg_ref), (HIDDEN, wu_ref)):
         got = jnp.dot(x, w_ref[...], preferred_element_type=F32)
         own_ref[:, at : at + HIDDEN] = got
         send_ref[:, at : at + HIDDEN] = got.astype(BF16)
-    lane = lax.broadcasted_iota(jnp.int32, (half, HD), 1)
-    for n, x_ref in enumerate((x0, x1)):
-        acc = jnp.zeros((half, HD), F32)
-        for c in range(0, HALF, HD):
-            part = x_ref[:, c : c + HD].astype(F32)
-            acc = acc + part * part
-        total = jnp.broadcast_to(jnp.sum(acc, axis=1, keepdims=True), (half, HD))
-        high = total.astype(BF16).astype(F32)
-        low = jnp.where(high < jnp.inf, total - high, 0.0)
-        sq_ref[n * half : (n + 1) * half] = total
-        send_ref[n * half : (n + 1) * half, 2 * HIDDEN :] = jnp.where(
-            lane < HD // 2, high, low
-        ).astype(BF16)
-
-
-PLACES = {0: (0, 0), 3: (0, 64), 1: (1, 0), 2: (1, 64)}
 
 
 def coordinates():
@@ -216,47 +232,48 @@
     return jnp.where(role == 0, x, y), jnp.where(role == 0, y, x)
 
 
-def block_at(start, place, shift):
-    return pl.ds(pl.multiple_of(start + lax.rem(place - shift + 4, 4) * 16, 16), 16)
-
-
-def down_body(own0, sq0, own1, sq1, got0, got1, wd_ref, o0, o1, o2, o3, act_ref):
-    owns, sqs, gots = (own0, own1), (sq0, sq1), (got0, got1)
+def down_body(own0, sq0, own1, sq1, got0, got1, wd_ref, *rest):
+    outs, (act_ref, got_ref) = rest[:8], rest[8:]
+    early = got0.shape[0]
+    got_ref[:early] = got0[...]
+    got_ref[early:] = got1[...]
     my_a, my_b = coordinates()
-    for jb in range(4):
-        for ja in range(4):
-            h, at = PLACES[jb]
-            ph, pat = PLACES[ja]
-            mine = block_at(at, my_a, SHIFTS[ja])
-            peer = block_at(pat, my_b, SHIFTS[jb])
-            got = gots[ph][peer].astype(F32)
-            lane = 2 * HIDDEN
-            extra = got[:, lane : lane + 1] + got[:, lane + HD // 2 : lane + HD // 2 + 1]
-            total = sqs[h][mine][:, :1] + extra
-            inv = lax.rsqrt(total / MODEL_WIDTH + 1e-05)
-            pre = owns[h][mine] + got[:, : 2 * HIDDEN]
-            pre = jnp.where(inv > 0.0, pre * inv, 0.0)
-            gate = pre[:, :HIDDEN]
-            place = (jb * 4 + ja) * 16
-            act_ref[place : place + 16] = (gate * jax.nn.sigmoid(gate) * pre[:, HIDDEN:]).astype(BF16)
-    outs = (o0, o1, o2, o3)
+    for jp in range(2):
+        for jb in range(4):
+            for ai in range(2):
+                at = (jp * 8 + jb * 2 + ai) * 16
+                ours, sqs, mine = (own0, sq0, at) if at < early else (own1, sq1, at - early)
+                away = lax.rem(my_a - 2 * lax.rem(my_a // 2 + jp, 2) - ai + 4, 4)
+                peer_b = jnp.where(away == 2, 1, jnp.where(away == 1, 2, away))
+                peer_a = lax.rem(my_b - SHIFTS[jb] + 4, 4)
+                peer_p = lax.rem(peer_a // 2 + my_b // 2, 2)
+                peer = (peer_p * 8 + peer_b * 2 + lax.rem(peer_a, 2)) * 16
+                got = got_ref[pl.ds(pl.multiple_of(peer, 16), 16)].astype(F32)
+                lane = 2 * HIDDEN
+                extra = got[:, lane : lane + 1] + got[:, lane + HD // 2 : lane + HD // 2 + 1]
+                total = sqs[mine : mine + 16][:, :1] + extra
+                inv = lax.rsqrt(total / MODEL_WIDTH + 1e-05)
+                pre = ours[mine : mine + 16] + got[:, : 2 * HIDDEN]
+                pre = jnp.where(inv > 0.0, pre * inv, 0.0)
+                gate = pre[:, :HIDDEN]
+                act = gate * jax.nn.sigmoid(gate) * pre[:, HIDDEN:]
+                act_ref[at : at + 16] = act.astype(BF16)
     act = act_ref[...]
     for n in range(0, HALF, 512):
         got = jnp.dot(act, wd_ref[:, n : n + 512], preferred_element_type=F32).astype(BF16)
-        for j in range(4):
-            outs[j][:, n : n + 512] = got[j * 64 : (j + 1) * 64]
-
-
-def gather_body(t0, t1, t2, t3, out_ref):
-    my_a, _ = coordinates()
-    for ja in range(4):
-        at = slice(16 * ja, 16 * ja + 16)
-        total = t0[at].astype(F32) + t1[at].astype(F32) + t2[at].astype(F32) + t3[at].astype(F32)
-        out_ref[block_at(0, my_a, SHIFTS[ja])] = total.astype(BF16)
+        for j in range(8):
+            outs[j][:, n : n + 512] = got[j * PART : (j + 1) * PART]
+
+
+def sum_body(*refs):
+    total = refs[0][...].astype(F32)
+    for r in refs[1:-1]:
+        total = total + r[...].astype(F32)
+    refs[-1][...] = total.astype(BF16)
 
 
 def combine_body(comb_ref, hidden_ref, back_ref, out_ref):
-    got = jnp.dot(comb_ref[:, :64], back_ref[...], preferred_element_type=F32)
+    got = jnp.dot(comb_ref[:, :PART], back_ref[...], preferred_element_type=F32)
     moe = got[:ROWS] + got[ROWS : 2 * ROWS] + got[2 * ROWS : 3 * ROWS]
     out_ref[...] = (hidden_ref[...].astype(F32) + moe).astype(BF16)
 
@@ -283,7 +300,7 @@
     return r, z, x, (y + s) % 4
 
 
-def send(value, s):
+def send_b(value, s):
     return lax.ppermute(
         value,
         AXES,
@@ -291,13 +308,25 @@
     )
 
 
+def send_a(value):
+    return lax.ppermute(
+        value,
+        AXES,
+        permutation(lambda r, z, x, y: along_x(2, r, z, x, y) if r == 0 else along_y(2, r, z, x, y)),
+    )
+
+
 def swap(value):
     return lax.ppermute(value, "role", [(0, 1), (1, 0)])
 
 
 def exchange(value):
-    groups = [[index_of(0, z, x, y) for x in range(4) for z in range(8)] for y in range(4)]
-    groups += [[index_of(1, z, x, y) for y in range(4) for z in range(8)] for x in range(4)]
+    groups = []
+    for p in (0, 2):
+        for o in range(4):
+            pair = [(a, z) for a in (p, p + 1) for z in range(8)]
+            groups.append([index_of(0, z, a, o) for a, z in pair])
+            groups.append([index_of(1, z, o, a) for a, z in pair])
     return lax.all_to_all(
         value, AXES, split_axis=0, concat_axis=0, axis_index_groups=groups, tiled=True
     )
@@ -309,7 +338,7 @@
     shape = jax.ShapeDtypeStruct
     hidden, outgoing, comb = call(
         attend_body,
-        (shape((ROWS, HALF), BF16), shape((4 * EXPERTS, CAP, HALF), BF16), shape((4 * ROWS, HD), BF16)),
+        (shape((ROWS, HALF), BF16), shape((2 * EXPERTS, CAP, HALF), BF16), shape((4 * ROWS, HD), BF16)),
         [HBM_SPEC] * 7,
         flops=50_000_000,
         nbytes=1_200_000,
@@ -325,52 +354,66 @@
             pltpu.SemaphoreType.DMA((8,)),
         ],
     )(*map(in_hbm, (lengths, expert_ids.T, router_logits, query, new_kv, kv_cache, residual)))
-    plane = exchange(outgoing).reshape(64, HALF)
-    count = 2 * HALF // CHUNK
-    wg, wu, wd = call(
-        weights_body,
-        (
+    near = exchange(outgoing).reshape(PART, HALF)
+    far = send_a(near)
+    near_b = [send_b(near, s) for s in ORDER]
+    far_b = [send_b(far, s) for s in ORDER]
+
+    def partials(rows):
+        return (
+            shape((rows, 2 * HIDDEN), F32),
+            shape((rows, HD), F32),
+            shape((rows, 2 * HIDDEN + HD), BF16),
+        )
+
+    own0, sq0, send0, gain, wg, wu, wd = call(
+        first_body,
+        partials(5 * PART)
+        + (
+            shape((1, HALF), F32),
             pltpu.VMEM((HALF, HIDDEN), BF16),
             pltpu.VMEM((HALF, HIDDEN), BF16),
             pltpu.VMEM((HIDDEN, HALF), BF16),
         ),
-        [HBM_SPEC, VMEM_SPEC, HBM_SPEC, HBM_SPEC, HBM_SPEC],
-        flops=20_000_000,
-        nbytes=18_000_000,
+        [VMEM_SPEC] * 5 + [HBM_SPEC] * 4,
+        flops=2 * 5 * PART * HALF * 1024,
+        nbytes=20_000_000,
         scratch=[
-            pltpu.VMEM((count, CHUNK, HIDDEN), BF16),
-            pltpu.SemaphoreType.DMA((count + 1,)),
+            pltpu.VMEM((HALF,), BF16),
+            pltpu.VMEM((5 * PART, HALF), BF16),
+            pltpu.SemaphoreType.DMA((2 * HALF // CHUNK + 2,)),
         ],
-    )(plane, norm_gain.reshape(1, HALF), *map(in_hbm, (w_gate, w_up, w_down)))
-    pieces = [plane] + [send(plane, s) for s in SHIFTS[1:]]
-
-    def gate(x0, x1):
-        return call(
-            gate_body,
-            (shape((128, 2 * HIDDEN), F32), shape((128, HD), F32), shape((128, 2 * HIDDEN + HD), BF16)),
-            [VMEM_SPEC] * 4,
-            flops=2 * 128 * HALF * 1024,
-            nbytes=8_000_000,
-        )(x0, x1, wg, wu)
-
-    own0, sq0, send0 = gate(pieces[0], pieces[3])
-    own1, sq1, send1 = gate(pieces[1], pieces[2])
+    )(near, *near_b, far, *map(in_hbm, (norm_gain, w_gate, w_up, w_down)))
+    own1, sq1, send1 = call(
+        second_body,
+        partials(3 * PART),
+        [VMEM_SPEC] * 6,
+        flops=2 * 3 * PART * HALF * 1024,
+        nbytes=8_000_000,
+        scratch=[pltpu.VMEM((3 * PART, HALF), BF16)],
+    )(*far_b, gain, wg, wu)
     terms = call(
         down_body,
-        [shape((64, HALF), BF16)] * 4,
+        [shape((PART, HALF), BF16)] * 8,
         [VMEM_SPEC] * 7,
         flops=2 * 256 * HALF * 512,
         nbytes=6_000_000,
-        scratch=[pltpu.VMEM((256, HIDDEN), BF16)],
+        scratch=[pltpu.VMEM((256, HIDDEN), BF16), pltpu.VMEM((256, 2 * HIDDEN + HD), BF16)],
     )(own0, sq0, own1, sq1, swap(send0), swap(send1), wd)
-    summed = call(
-        gather_body,
-        shape((64, HALF), BF16),
-        [VMEM_SPEC] * 4,
-        flops=800_000,
-        nbytes=2_000_000,
-    )(terms[0], *[send(terms[j], -SHIFTS[j]) for j in (1, 2, 3)])
-    back = exchange(summed.reshape(4 * EXPERTS, CAP, HALF)).reshape(64, HALF)
+
+    def add_up(parts):
+        return call(
+            sum_body,
+            shape((PART, HALF), BF16),
+            [VMEM_SPEC] * len(parts),
+            flops=400_000,
+            nbytes=1_000_000,
+        )(*parts)
+
+    far_sum = add_up([terms[4]] + [send_b(terms[4 + j], -SHIFTS[j]) for j in (1, 2, 3)])
+    near_got = [send_b(terms[j], -SHIFTS[j]) for j in (1, 2, 3)]
+    summed = add_up([terms[0]] + near_got + [send_a(far_sum)])
+    back = exchange(summed.reshape(2 * EXPERTS, CAP, HALF)).reshape(PART, HALF)
     return call(
         combine_body,
         shape((ROWS, HALF), BF16),

time: 82 us -> 77.7 us (0.948)
  starting transfers between devices: 7.87 us -> 27.3 us
  blocking collectives: 43.3 us -> 30.8 us
  waiting for transfers between devices: 18.8 us -> 9.73 us
  local copies, waits for them, and re-layouts: 1.14 us -> 0.23 us
  Pallas kernels: 10.2 us -> 9.35 us
    ppermute x6 -> x14, starting transfers between devices: 7.23 us -> 26.6 us  [the longest x12 20.9 us: send_b(): lax.ppermute(value, AXES, permutation(lambda r, z, x, y: along_y(s, r, z,...]
    all_to_all x2, blocking collectives: 43.3 us -> 30.8 us  [exchange(): lax.all_to_all(value, AXES, split_axis=0, concat_axis=0, axis_index_group...]
    ppermute x6 -> x14, waiting for transfers between devices: 17.6 us -> 8.62 us  [the longest x2 4.55 us: send_a(): lax.ppermute(value, AXES, permutation(lambda r, z, x, y: along_x(2, r, z,...]
    reshape x4 -> x3, local copies, waits for them, and re-layouts: 1.14 us -> 0.23 us  [the longest x2 0.15 us: per_device(): back = exchange(summed.reshape(2 * EXPERTS, CAP, HALF)).reshape(PART, HALF)]
    pallas_call x6, Pallas kernels: 9.46 us -> 8.58 us  [the longest x1 3.89 us: per_device(): call(first_body, partials(5 * PART) + (shape((1, HALF), F32), pltpu.VMEM(...]
  transfers between devices with their start and end apart: 8 -> 16, of which waited for: 5 -> 5; matrix products, arithmetic and copies ran while one was open for 1% -> 0% of each run, Pallas kernels for 7% -> 7%
where the time goes in v3:
time: 77.7 us; the launch traced here: 77.5 us
  blocking collectives  30.8 us (40%)
  starting transfers between devices  27.3 us (35%)
  waiting for transfers between devices  9.73 us (13%)
  Pallas kernels  9.35 us (12%)
    all_to_all x2, blocking collectives, exchange(): lax.all_to_all(value, AXES, split_axis=0, concat_axis=0, axis_index_group...  30.8 us
    ppermute x12, starting transfers between devices, send_b(): lax.ppermute(value, AXES, permutation(lambda r, z, x, y: along_y(s, r, z,...  20.9 us
    ppermute x2, starting transfers between devices, send_a(): lax.ppermute(value, AXES, permutation(lambda r, z, x, y: along_x(2, r, z,...  5.77 us
    ppermute x2, waiting for transfers between devices, send_a(): lax.ppermute(value, AXES, permutation(lambda r, z, x, y: along_x(2, r, z,...  4.55 us
    ppermute x12, waiting for transfers between devices, send_b(): lax.ppermute(value, AXES, permutation(lambda r, z, x, y: along_y(s, r, z,...  4.08 us
    pallas_call x1, Pallas kernels, per_device(): call(first_body, partials(5 * PART) + (shape((1, HALF), F32), pltpu.VMEM(...  3.89 us
    pallas_call x1, Pallas kernels, per_device(): call(attend_body, (shape((ROWS, HALF), BF16), shape((2 * EXPERTS, CAP, HA...  1.97 us
  transfers between devices with their start and end apart: 16, of which 5 were waited for; matrix products, arithmetic and copies ran while one was open for 0% of the time, Pallas kernels for 7%

profile of v3, /device:TPU:32, one launch (start us, length us, event | category | flops | bytes accessed | tf_op | source)
XLA Modules:
  0.0 77.5 jit_solution(1981671965639855256)
XLA Ops:
  0.0 2.0 %shard_map.109 = (bf16[4,3072]{1,0:T(4,128)(2,1)S(1)}, bf16[16,2,3072]{2,1,0:T(2,128)(2,1)S(1)}, bf16[16,128]{1,0:T(8,128)(2,1)S(1)}) custom-call(s32[4]{0:T(128)} %len_hbm.1, s32[2,4]{1,0:T(2,128)} %bitcast.1, f32[4,8]{1,0:T(4,128)} %logit_hbm.1, bf16[4,3072]{1,0:T(4,128)(2,1)} %q_hbm.1, bf16[4,2,512]{2,1,0:T(2,128)(2,1)} %new_hbm.1, ...), custom_call_target="tpu_custom_call" | custom-call | flops 50000000 | bytes 1200000 | tf_op jit(solution)/shard_map/pallas_call | solution.py:339
  2.0 18.3 %all_to_all.10 = bf16[16,2,3072]{2,1,0:T(2,128)(2,1)S(1)} all-to-all(bf16[16,2,3072]{2,1,0:T(2,128)(2,1)S(1)} %get-tuple-element.28), channel_id=1, replica_groups={{0,16,32,48,64,80,96,112,4,20,36,52,68,84,100,116},{128,144,160,176,192..., dimensions={0} | all-to-all | bytes 393216 | tf_op jit(solution)/shard_map/all_to_all | solution.py:330
  20.3 2.9 %collective-permute-start.3 = (bf16[32,3072]{1,0:T(8,128)(2,1)S(1)}, bf16[32,3072]{1,0:T(8,128)(2,1)S(1)}, u32[]{:S(2)}, u32[]{:S(2)}) collective-permute-start(bf16[32,3072]{1,0:T(8,128)(2,1)S(1)} %reshape.9.refs_0_), channel_id=1, source_target_pairs={{0,8},{1,9},{2,10},{3,11},{4,12},{5,13},{6,14},{7,15},{8,0},{9,1},... | collective-permute-start | bytes 589832 | tf_op jit(solution)/shard_map/ppermute | solution.py:312
  23.2 2.9 %collective-permute-start = (bf16[32,3072]{1,0:T(8,128)(2,1)S(1)}, bf16[32,3072]{1,0:T(8,128)(2,1)S(1)}, u32[]{:S(2)}, u32[]{:S(2)}) collective-permute-start(bf16[32,3072]{1,0:T(8,128)(2,1)S(1)} %reshape.9.refs_0_), channel_id=1, source_target_pairs={{0,2},{1,3},{2,0},{3,1},{4,6},{5,7},{6,4},{7,5},{8,10},{9,11},{10,... | collective-permute-start | bytes 589832 | tf_op jit(solution)/shard_map/ppermute | solution.py:304
  26.1 1.2 %collective-permute-start.1 = (bf16[32,3072]{1,0:T(8,128)(2,1)S(1)}, bf16[32,3072]{1,0:T(8,128)(2,1)S(1)}, u32[]{:S(2)}, u32[]{:S(2)}) collective-permute-start(bf16[32,3072]{1,0:T(8,128)(2,1)S(1)} %reshape.9.refs_0_), channel_id=1, source_target_pairs={{0,1},{1,2},{2,3},{3,0},{4,5},{5,6},{6,7},{7,4},{8,9},{9,10},{10,1... | collective-permute-start | bytes 589832 | tf_op jit(solution)/shard_map/ppermute | solution.py:304
  27.3 2.1 %collective-permute-start.2 = (bf16[32,3072]{1,0:T(8,128)(2,1)S(1)}, bf16[32,3072]{1,0:T(8,128)(2,1)S(1)}, u32[]{:S(2)}, u32[]{:S(2)}) collective-permute-start(bf16[32,3072]{1,0:T(8,128)(2,1)S(1)} %reshape.9.refs_0_), channel_id=1, source_target_pairs={{0,3},{1,0},{2,1},{3,2},{4,7},{5,4},{6,5},{7,6},{8,11},{9,8},{10,9... | collective-permute-start | bytes 589832 | tf_op jit(solution)/shard_map/ppermute | solution.py:304
  29.5 3.1 %collective-permute-start.4 = (bf16[32,3072]{1,0:T(8,128)(2,1)S(1)}, bf16[32,3072]{1,0:T(8,128)(2,1)S(1)}, u32[]{:S(2)}, u32[]{:S(2)}) collective-permute-start(bf16[32,3072]{1,0:T(8,128)(2,1)S(1)} %collective-permute-done.3.refs_4_), channel_id=1, source_target_pairs={{0,2},{1,3},{2,0},{3,1},{4,6},{5,7},{6,4},{7,5},{8,10},{9,11},{10,... | collective-permute-start | bytes 589832 | tf_op jit(solution)/shard_map/ppermute | solution.py:304
  32.6 1.2 %collective-permute-start.5 = (bf16[32,3072]{1,0:T(8,128)(2,1)S(1)}, bf16[32,3072]{1,0:T(8,128)(2,1)S(1)}, u32[]{:S(2)}, u32[]{:S(2)}) collective-permute-start(bf16[32,3072]{1,0:T(8,128)(2,1)S(1)} %collective-permute-done.3.refs_4_), channel_id=1, source_target_pairs={{0,1},{1,2},{2,3},{3,0},{4,5},{5,6},{6,7},{7,4},{8,9},{9,10},{10,1... | collective-permute-start | bytes 589832 | tf_op jit(solution)/shard_map/ppermute | solution.py:304
  33.9 2.0 %collective-permute-start.6 = (bf16[32,3072]{1,0:T(8,128)(2,1)S(1)}, bf16[32,3072]{1,0:T(8,128)(2,1)S(1)}, u32[]{:S(2)}, u32[]{:S(2)}) collective-permute-start(bf16[32,3072]{1,0:T(8,128)(2,1)S(1)} %collective-permute-done.3.refs_4_), channel_id=1, source_target_pairs={{0,3},{1,0},{2,1},{3,2},{4,7},{5,4},{6,5},{7,6},{8,11},{9,8},{10,9... | collective-permute-start | bytes 589832 | tf_op jit(solution)/shard_map/ppermute | solution.py:304
  35.9 3.9 %shard_map.110 = (f32[160,1024]{1,0:T(8,128)S(1)}, f32[160,128]{1,0:T(8,128)S(1)}, bf16[160,1152]{1,0:T(8,128)(2,1)S(1)}, f32[1,3072]{1,0:T(1,128)S(1)}, bf16[30...) custom-call(bf16[32,3072]{1,0:T(8,128)(2,1)S(1)} %reshape.9.refs_0_, ...), custom_call_target="tpu_custom_call" | custom-call | flops 1006632960 | bytes 20000000 | tf_op jit(solution)/shard_map/pallas_call | solution.py:369
  39.9 1.2 %shard_map.111 = (f32[96,1024]{1,0:T(8,128)S(1)}, f32[96,128]{1,0:T(8,128)S(1)}, bf16[96,1152]{1,0:T(8,128)(2,1)S(1)}) custom-call(bf16[32,3072]{1,0:T(8,128)(2,1)S(1)} %collective-permute-done.4.refs_0_, bf16[32,3072]{1,0:T(8,128)(2,1)S(1)} %collective-permute-done.5.refs_1_, bf16[32,3072]{1,0:T(8,128)(2,1)S(1)} %collective-permute-done.6.refs_2_, ...), custom_call_target="tpu_custom_call" | custom-call | flops 603979776 | bytes 8000000 | tf_op jit(solution)/shard_map/pallas_call | solution.py:387
  41.1 0.6 collective-permute-start.8
  41.7 1.1 %collective-permute-done.8.got1 = bf16[96,1152]{1,0:T(8,128)(2,1)S(1)} collective-permute-done((bf16[96,1152]{1,0:T(8,128)(2,1)S(1)}, bf16[96,1152]{1,0:T(8,128)(2,1)S(1)}, u32[]{:S(2)}, u32[]{:S(2)}) %collective-permute-start.8) | collective-permute-done | bytes 221216 | tf_op jit(solution)/shard_map/ppermute | solution.py:320
  42.8 1.3 %shard_map.112 = (bf16[32,3072]{1,0:T(8,128)(2,1)S(1)}, bf16[32,3072]{1,0:T(8,128)(2,1)S(1)}, bf16[32,3072]{1,0:T(8,128)(2,1)S(1)}, bf16[32,3072]{1,0:T(8,128)(2...) custom-call(f32[160,1024]{1,0:T(8,128)S(1)} %get-tuple-element.29.ow, ...), custom_call_target="tpu_custom_call" | custom-call | flops 805306368 | bytes 6000000 | tf_op jit(solution)/shard_map/pallas_call | solution.py:395
  44.1 1.8 %collective-permute-start.12 = (bf16[32,3072]{1,0:T(8,128)(2,1)S(1)}, bf16[32,3072]{1,0:T(8,128)(2,1)S(1)}, u32[]{:S(2)}, u32[]{:S(2)}) collective-permute-start(bf16[32,3072]{1,0:T(8,128)(2,1)S(1)} %get-tuple-element.44), channel_id=1, source_target_pairs={{0,2},{1,3},{2,0},{3,1},{4,6},{5,7},{6,4},{7,5},{8,10},{9,11},{10,... | collective-permute-start | bytes 589832 | tf_op jit(solution)/shard_map/ppermute | solution.py:304
  45.8 1.7 %collective-permute-start.13 = (bf16[32,3072]{1,0:T(8,128)(2,1)S(1)}, bf16[32,3072]{1,0:T(8,128)(2,1)S(1)}, u32[]{:S(2)}, u32[]{:S(2)}) collective-permute-start(bf16[32,3072]{1,0:T(8,128)(2,1)S(1)} %get-tuple-element.45), channel_id=1, source_target_pairs={{0,3},{1,0},{2,1},{3,2},{4,7},{5,4},{6,5},{7,6},{8,11},{9,8},{10,9... | collective-permute-start | bytes 589832 | tf_op jit(solution)/shard_map/ppermute | solution.py:304
  47.9 2.0 %collective-permute-start.9 = (bf16[32,3072]{1,0:T(8,128)(2,1)S(1)}, bf16[32,3072]{1,0:T(8,128)(2,1)S(1)}, u32[]{:S(2)}, u32[]{:S(2)}) collective-permute-start(bf16[32,3072]{1,0:T(8,128)(2,1)S(1)} %get-tuple-element.40), channel_id=1, source_target_pairs={{0,2},{1,3},{2,0},{3,1},{4,6},{5,7},{6,4},{7,5},{8,10},{9,11},{10,... | collective-permute-start | bytes 589832 | tf_op jit(solution)/shard_map/ppermute | solution.py:304
  49.8 2.6 %collective-permute-start.10 = (bf16[32,3072]{1,0:T(8,128)(2,1)S(1)}, bf16[32,3072]{1,0:T(8,128)(2,1)S(1)}, u32[]{:S(2)}, u32[]{:S(2)}) collective-permute-start(bf16[32,3072]{1,0:T(8,128)(2,1)S(1)} %get-tuple-element.41), channel_id=1, source_target_pairs={{0,3},{1,0},{2,1},{3,2},{4,7},{5,4},{6,5},{7,6},{8,11},{9,8},{10,9... | collective-permute-start | bytes 589832 | tf_op jit(solution)/shard_map/ppermute | solution.py:304
  52.5 1.1 %collective-permute-done.13.refs_2_ = bf16[32,3072]{1,0:T(8,128)(2,1)S(1)} collective-permute-done((bf16[32,3072]{1,0:T(8,128)(2,1)S(1)}, bf16[32,3072]{1,0:T(8,128)(2,1)S(1)}, u32[]{:S(2)}, u32[]{:S(2)}) %collective-permute-start.13) | collective-permute-done | bytes 196640 | tf_op jit(solution)/shard_map/ppermute | solution.py:304
  53.5 3.0 %collective-permute-done.14.refs_3_ = bf16[32,3072]{1,0:T(8,128)(2,1)S(1)} collective-permute-done((bf16[32,3072]{1,0:T(8,128)(2,1)S(1)}, bf16[32,3072]{1,0:T(8,128)(2,1)S(1)}, u32[]{:S(2)}, u32[]{:S(2)}) %collective-permute-start.14) | collective-permute-done | bytes 196640 | tf_op jit(solution)/shard_map/ppermute | solution.py:304
  56.6 2.9 %collective-permute-start.15 = (bf16[32,3072]{1,0:T(8,128)(2,1)S(1)}, bf16[32,3072]{1,0:T(8,128)(2,1)S(1)}, u32[]{:S(2)}, u32[]{:S(2)}) collective-permute-start(bf16[32,3072]{1,0:T(8,128)(2,1)S(1)} %shard_map.113), channel_id=1, source_target_pairs={{0,8},{1,9},{2,10},{3,11},{4,12},{5,13},{6,14},{7,15},{8,0},{9,1},... | collective-permute-start | bytes 589832 | tf_op jit(solution)/shard_map/ppermute | solution.py:312
  59.6 4.3 %collective-permute-done.15.refs_4_ = bf16[32,3072]{1,0:T(8,128)(2,1)S(1)} collective-permute-done((bf16[32,3072]{1,0:T(8,128)(2,1)S(1)}, bf16[32,3072]{1,0:T(8,128)(2,1)S(1)}, u32[]{:S(2)}, u32[]{:S(2)}) %collective-permute-start.15) | collective-permute-done | bytes 196640 | tf_op jit(solution)/shard_map/ppermute | solution.py:312
  64.1 12.5 %all_to_all.11 = bf16[16,2,3072]{2,1,0:T(2,128)(2,1)S(1)} all-to-all(bf16[16,2,3072]{2,1,0:T(2,128)(2,1)S(1)} %reshape.10), channel_id=1, replica_groups={{0,16,32,48,64,80,96,112,4,20,36,52,68,84,100,116},{128,144,160,176,192..., dimensions={0} | all-to-all | bytes 393216 | tf_op jit(solution)/shard_map/all_to_all | solution.py:330
  76.7 0.8 shard_map.115
  (20 shorter events, 1.1 us)
Async XLA Ops:
  20.3 9.2 %collective-permute-start.3 = (bf16[32,3072]{1,0:T(8,128)(2,1)S(1)}, bf16[32,3072]{1,0:T(8,128)(2,1)S(1)}, u32[]{:S(2)}, u32[]{:S(2)}) collective-permute-start(bf16[32,3072]{1,0:T(8,128)(2,1)S(1)} %reshape.9.refs_0_), channel_id=1, source_target_pairs={{0,8},{1,9},{2,10},{3,11},{4,12},{5,13},{6,14},{7,15},{8,0},{9,1},... | collective-permute-start | bytes 589832 | tf_op jit(solution)/shard_map/ppermute | solution.py:312
  23.2 10.7 %collective-permute-start = (bf16[32,3072]{1,0:T(8,128)(2,1)S(1)}, bf16[32,3072]{1,0:T(8,128)(2,1)S(1)}, u32[]{:S(2)}, u32[]{:S(2)}) collective-permute-start(bf16[32,3072]{1,0:T(8,128)(2,1)S(1)} %reshape.9.refs_0_), channel_id=1, source_target_pairs={{0,2},{1,3},{2,0},{3,1},{4,6},{5,7},{6,4},{7,5},{8,10},{9,11},{10,... | collective-permute-start | bytes 589832 | tf_op jit(solution)/shard_map/ppermute | solution.py:304
  26.1 9.8 %collective-permute-start.1 = (bf16[32,3072]{1,0:T(8,128)(2,1)S(1)}, bf16[32,3072]{1,0:T(8,128)(2,1)S(1)}, u32[]{:S(2)}, u32[]{:S(2)}) collective-permute-start(bf16[32,3072]{1,0:T(8,128)(2,1)S(1)} %reshape.9.refs_0_), channel_id=1, source_target_pairs={{0,1},{1,2},{2,3},{3,0},{4,5},{5,6},{6,7},{7,4},{8,9},{9,10},{10,1... | collective-permute-start | bytes 589832 | tf_op jit(solution)/shard_map/ppermute | solution.py:304
  27.3 8.6 %collective-permute-start.2 = (bf16[32,3072]{1,0:T(8,128)(2,1)S(1)}, bf16[32,3072]{1,0:T(8,128)(2,1)S(1)}, u32[]{:S(2)}, u32[]{:S(2)}) collective-permute-start(bf16[32,3072]{1,0:T(8,128)(2,1)S(1)} %reshape.9.refs_0_), channel_id=1, source_target_pairs={{0,3},{1,0},{2,1},{3,2},{4,7},{5,4},{6,5},{7,6},{8,11},{9,8},{10,9... | collective-permute-start | bytes 589832 | tf_op jit(solution)/shard_map/ppermute | solution.py:304
  29.5 10.3 %collective-permute-start.4 = (bf16[32,3072]{1,0:T(8,128)(2,1)S(1)}, bf16[32,3072]{1,0:T(8,128)(2,1)S(1)}, u32[]{:S(2)}, u32[]{:S(2)}) collective-permute-start(bf16[32,3072]{1,0:T(8,128)(2,1)S(1)} %collective-permute-done.3.refs_4_), channel_id=1, source_target_pairs={{0,2},{1,3},{2,0},{3,1},{4,6},{5,7},{6,4},{7,5},{8,10},{9,11},{10,... | collective-permute-start | bytes 589832 | tf_op jit(solution)/shard_map/ppermute | solution.py:304
  32.6 7.3 %collective-permute-start.5 = (bf16[32,3072]{1,0:T(8,128)(2,1)S(1)}, bf16[32,3072]{1,0:T(8,128)(2,1)S(1)}, u32[]{:S(2)}, u32[]{:S(2)}) collective-permute-start(bf16[32,3072]{1,0:T(8,128)(2,1)S(1)} %collective-permute-done.3.refs_4_), channel_id=1, source_target_pairs={{0,1},{1,2},{2,3},{3,0},{4,5},{5,6},{6,7},{7,4},{8,9},{9,10},{10,1... | collective-permute-start | bytes 589832 | tf_op jit(solution)/shard_map/ppermute | solution.py:304
  33.9 6.0 %collective-permute-start.6 = (bf16[32,3072]{1,0:T(8,128)(2,1)S(1)}, bf16[32,3072]{1,0:T(8,128)(2,1)S(1)}, u32[]{:S(2)}, u32[]{:S(2)}) collective-permute-start(bf16[32,3072]{1,0:T(8,128)(2,1)S(1)} %collective-permute-done.3.refs_4_), channel_id=1, source_target_pairs={{0,3},{1,0},{2,1},{3,2},{4,7},{5,4},{6,5},{7,6},{8,11},{9,8},{10,9... | collective-permute-start | bytes 589832 | tf_op jit(solution)/shard_map/ppermute | solution.py:304
  39.8 1.9 %collective-permute-start.7 = (bf16[160,1152]{1,0:T(8,128)(2,1)S(1)}, bf16[160,1152]{1,0:T(8,128)(2,1)S(1)}, u32[]{:S(2)}, u32[]{:S(2)}) collective-permute-start(bf16[160,1152]{1,0:T(8,128)(2,1)S(1)} %get-tuple-element.36), channel_id=1, source_target_pairs={{0,128},{128,0},{1,129},{129,1},{2,130},{130,2},{3,131},{131,3},{4... | collective-permute-start | bytes 1105928 | tf_op jit(solution)/shard_map/ppermute | solution.py:320
  41.1 1.7 %collective-permute-start.8 = (bf16[96,1152]{1,0:T(8,128)(2,1)S(1)}, bf16[96,1152]{1,0:T(8,128)(2,1)S(1)}, u32[]{:S(2)}, u32[]{:S(2)}) collective-permute-start(bf16[96,1152]{1,0:T(8,128)(2,1)S(1)} %get-tuple-element.37), channel_id=1, source_target_pairs={{0,128},{128,0},{1,129},{129,1},{2,130},{130,2},{3,131},{131,3},{4... | collective-permute-start | bytes 663560 | tf_op jit(solution)/shard_map/ppermute | solution.py:320
  44.1 8.4 %collective-permute-start.12 = (bf16[32,3072]{1,0:T(8,128)(2,1)S(1)}, bf16[32,3072]{1,0:T(8,128)(2,1)S(1)}, u32[]{:S(2)}, u32[]{:S(2)}) collective-permute-start(bf16[32,3072]{1,0:T(8,128)(2,1)S(1)} %get-tuple-element.44), channel_id=1, source_target_pairs={{0,2},{1,3},{2,0},{3,1},{4,6},{5,7},{6,4},{7,5},{8,10},{9,11},{10,... | collective-permute-start | bytes 589832 | tf_op jit(solution)/shard_map/ppermute | solution.py:304
  45.8 7.7 %collective-permute-start.13 = (bf16[32,3072]{1,0:T(8,128)(2,1)S(1)}, bf16[32,3072]{1,0:T(8,128)(2,1)S(1)}, u32[]{:S(2)}, u32[]{:S(2)}) collective-permute-start(bf16[32,3072]{1,0:T(8,128)(2,1)S(1)} %get-tuple-element.45), channel_id=1, source_target_pairs={{0,3},{1,0},{2,1},{3,2},{4,7},{5,4},{6,5},{7,6},{8,11},{9,8},{10,9... | collective-permute-start | bytes 589832 | tf_op jit(solution)/shard_map/ppermute | solution.py:304
  47.5 9.0 %collective-permute-start.14 = (bf16[32,3072]{1,0:T(8,128)(2,1)S(1)}, bf16[32,3072]{1,0:T(8,128)(2,1)S(1)}, u32[]{:S(2)}, u32[]{:S(2)}) collective-permute-start(bf16[32,3072]{1,0:T(8,128)(2,1)S(1)} %get-tuple-element.46), channel_id=1, source_target_pairs={{0,1},{1,2},{2,3},{3,0},{4,5},{5,6},{6,7},{7,4},{8,9},{9,10},{10,1... | collective-permute-start | bytes 589832 | tf_op jit(solution)/shard_map/ppermute | solution.py:304
  47.9 11.7 %collective-permute-start.9 = (bf16[32,3072]{1,0:T(8,128)(2,1)S(1)}, bf16[32,3072]{1,0:T(8,128)(2,1)S(1)}, u32[]{:S(2)}, u32[]{:S(2)}) collective-permute-start(bf16[32,3072]{1,0:T(8,128)(2,1)S(1)} %get-tuple-element.40), channel_id=1, source_target_pairs={{0,2},{1,3},{2,0},{3,1},{4,6},{5,7},{6,4},{7,5},{8,10},{9,11},{10,... | collective-permute-start | bytes 589832 | tf_op jit(solution)/shard_map/ppermute | solution.py:304
  49.8 9.7 %collective-permute-start.10 = (bf16[32,3072]{1,0:T(8,128)(2,1)S(1)}, bf16[32,3072]{1,0:T(8,128)(2,1)S(1)}, u32[]{:S(2)}, u32[]{:S(2)}) collective-permute-start(bf16[32,3072]{1,0:T(8,128)(2,1)S(1)} %get-tuple-element.41), channel_id=1, source_target_pairs={{0,3},{1,0},{2,1},{3,2},{4,7},{5,4},{6,5},{7,6},{8,11},{9,8},{10,9... | collective-permute-start | bytes 589832 | tf_op jit(solution)/shard_map/ppermute | solution.py:304
  52.5 7.1 %collective-permute-start.11 = (bf16[32,3072]{1,0:T(8,128)(2,1)S(1)}, bf16[32,3072]{1,0:T(8,128)(2,1)S(1)}, u32[]{:S(2)}, u32[]{:S(2)}) collective-permute-start(bf16[32,3072]{1,0:T(8,128)(2,1)S(1)} %get-tuple-element.42), channel_id=1, source_target_pairs={{0,1},{1,2},{2,3},{3,0},{4,5},{5,6},{6,7},{7,4},{8,9},{9,10},{10,1... | collective-permute-start | bytes 589832 | tf_op jit(solution)/shard_map/ppermute | solution.py:304
  56.6 7.3 %collective-permute-start.15 = (bf16[32,3072]{1,0:T(8,128)(2,1)S(1)}, bf16[32,3072]{1,0:T(8,128)(2,1)S(1)}, u32[]{:S(2)}, u32[]{:S(2)}) collective-permute-start(bf16[32,3072]{1,0:T(8,128)(2,1)S(1)} %shard_map.113), channel_id=1, source_target_pairs={{0,8},{1,9},{2,10},{3,11},{4,12},{5,13},{6,14},{7,15},{8,0},{9,1},... | collective-permute-start | bytes 589832 | tf_op jit(solution)/shard_map/ppermute | solution.py:312

commit v4 on v3

--- a/solution.py
+++ b/solution.py
@@ -1,3 +1,5 @@
+import functools
+
 import jax
 import jax.numpy as jnp
 from jax import lax
@@ -25,7 +27,7 @@
 BF16 = jnp.bfloat16
 
 
-def call(body, out_shape, in_specs, flops=0, nbytes=0, scratch=()):
+def call(body, out_shape, in_specs, flops=0, nbytes=0, scratch=(), aliases=None):
     single = not isinstance(out_shape, (tuple, list))
     out_specs = VMEM_SPEC if single else [VMEM_SPEC] * len(out_shape)
     return pl.pallas_call(
@@ -34,6 +36,7 @@
         in_specs=in_specs,
         out_specs=out_specs,
         scratch_shapes=list(scratch),
+        input_output_aliases=aliases or {},
         compiler_params=pltpu.CompilerParams(vmem_limit_bytes=16 * 1024 * 1024),
         cost_estimate=pl.CostEstimate(flops=flops, bytes_accessed=nbytes, transcendentals=0),
     )
@@ -44,9 +47,9 @@
 
 
 def attend_body(
-    len_hbm, ids_hbm, logit_hbm, q_hbm, new_hbm, kv_hbm, res_hbm,
-    hidden_ref, out_ref, comb_ref,
-    len_ref, ids_ref, logit_ref, q_ref, new_ref, k_ref, v_ref, res_ref, sems,
+    len_hbm, ids_hbm, logit_hbm, q_hbm, new_hbm, kv_hbm, res_hbm, gain_hbm,
+    hidden_ref, out_ref, comb_ref, gain_out,
+    len_ref, ids_ref, logit_ref, q_ref, new_ref, k_ref, v_ref, res_ref, gain_ref, sems,
 ):
     pairs = (
         (kv_hbm.at[:, 0], k_ref),
@@ -57,6 +60,7 @@
         (res_hbm, res_ref),
         (ids_hbm, ids_ref),
         (logit_hbm, logit_ref),
+        (gain_hbm, gain_ref),
     )
     copies = [pltpu.make_async_copy(a, b, sems.at[i]) for i, (a, b) in enumerate(pairs)]
     for c in copies:
@@ -117,6 +121,8 @@
             hidden_ref[:, hs] = (
                 res_ref[:, hs].astype(F32) + attn[g * ROWS : (g + 1) * ROWS]
             ).astype(BF16)
+    for c in range(0, HALF, HD):
+        gain_out[:, c : c + HD] = gain_ref[pl.ds(c, HD)].astype(F32).reshape(1, HD)
     ids = [ids_ref[p % 2, p // 2] for p in range(2 * ROWS)]
     rows = slot_rows(ids)
     ri = lax.broadcasted_iota(jnp.int32, (EXPERTS * CAP, ROWS), 0)
@@ -160,13 +166,16 @@
 PART = 32
 
 
-def scale_rows(x_ref, gain, scaled_ref, at, sq_ref, send_ref):
-    lane = lax.broadcasted_iota(jnp.int32, (PART, HD), 1)
-    acc = jnp.zeros((PART, HD), F32)
-    for c in range(0, HALF, HD):
+def scale_rows(x_ref, gain_ref, scaled_ref, at, cols, acc):
+    for c in range(cols.start, cols.stop, HD):
         part = x_ref[:, c : c + HD].astype(F32)
         acc = acc + part * part
-        scaled_ref[at : at + PART, c : c + HD] = (part * gain(c)).astype(BF16)
+        scaled_ref[at : at + PART, c : c + HD] = (part * gain_ref[:, c : c + HD]).astype(BF16)
+    return acc
+
+
+def put_squares(acc, at, sq_ref, send_ref):
+    lane = lax.broadcasted_iota(jnp.int32, (PART, HD), 1)
     total = jnp.broadcast_to(jnp.sum(acc, axis=1, keepdims=True), (PART, HD))
     high = total.astype(BF16).astype(F32)
     low = jnp.where(high < jnp.inf, total - high, 0.0)
@@ -174,95 +183,124 @@
     send_ref[at : at + PART, 2 * HIDDEN :] = jnp.where(lane < HD // 2, high, low).astype(BF16)
 
 
+def gate_up(xs, gain_ref, wg_ref, wu_ref, own_ref, sq_ref, send_ref, scaled_ref, chunk):
+    accs = [jnp.zeros((PART, HD), F32) for _ in xs]
+    sums = [None, None]
+    for k in range(0, HALF, chunk):
+        rows = slice(k, k + chunk)
+        for n, x_ref in enumerate(xs):
+            accs[n] = scale_rows(x_ref, gain_ref, scaled_ref, n * PART, rows, accs[n])
+        x = scaled_ref[:, rows]
+        for i, w_ref in enumerate((wg_ref, wu_ref)):
+            got = jnp.dot(x, w_ref[rows], preferred_element_type=F32)
+            sums[i] = got if sums[i] is None else sums[i] + got
+    for i, at in enumerate((0, HIDDEN)):
+        own_ref[:, at : at + HIDDEN] = sums[i]
+        send_ref[:, at : at + HIDDEN] = sums[i].astype(BF16)
+    for n in range(len(xs)):
+        put_squares(accs[n], n * PART, sq_ref, send_ref)
+
+
+def weight_copies(sources, targets, sems):
+    steps = [(k, w) for k in range(0, HALF, CHUNK) for w in (0, 1)]
+    copies = []
+    for n, (k, w) in enumerate(steps):
+        rows = pl.ds(k, CHUNK)
+        copies.append(
+            pltpu.make_async_copy(sources[w].at[0, rows], targets[w].at[rows], sems.at[n])
+        )
+    return steps, copies
+
+
+def ahead_body(after_ref, wg_hbm, wu_hbm, wg_ref, wu_ref, sems):
+    del after_ref
+
+    @pl.when(lax.axis_index("role") == 1)
+    def _():
+        _, copies = weight_copies((wg_hbm, wu_hbm), (wg_ref, wu_ref), sems)
+        for c in copies:
+            c.start()
+        for c in copies:
+            c.wait()
+
+
 def first_body(*refs):
-    xs, (gain_hbm, wg_hbm, wu_hbm, wd_hbm) = refs[:5], refs[5:9]
-    own_ref, sq_ref, send_ref, gain_out, wg_ref, wu_ref, wd_ref = refs[9:16]
-    gain_ref, scaled_ref, sems = refs[16:]
-    steps = [(k, w) for k in range(0, HALF, CHUNK) for w in (0, 1)]
-    sources, targets = (wg_hbm, wu_hbm), (wg_ref, wu_ref)
-
-    def fetch(n):
-        k, w = steps[n]
-        rows = pl.ds(k, CHUNK)
-        return pltpu.make_async_copy(sources[w].at[0, rows], targets[w].at[rows], sems.at[n])
-
-    count = len(steps)
-    gain_copy = pltpu.make_async_copy(gain_hbm, gain_ref, sems.at[count])
-    down_copy = pltpu.make_async_copy(wd_hbm.at[0], wd_ref, sems.at[count + 1])
-    gain_copy.start()
-    for n in range(count):
-        fetch(n).start()
-    down_copy.start()
-    gain_copy.wait()
-    for c in range(0, HALF, HD):
-        gain_out[:, c : c + HD] = gain_ref[pl.ds(c, HD)].astype(F32).reshape(1, HD)
-    for n, x_ref in enumerate(xs):
-        scale_rows(
-            x_ref, lambda c: gain_out[:, c : c + HD], scaled_ref, n * PART, sq_ref, send_ref
-        )
-    for n, (k, w) in enumerate(steps):
-        fetch(n).wait()
-        rows = slice(k, k + CHUNK)
-        at = slice(w * HIDDEN, (w + 1) * HIDDEN)
-        got = jnp.dot(scaled_ref[:, rows], targets[w][rows], preferred_element_type=F32)
-        if k:
-            got = got + own_ref[:, at]
-        own_ref[:, at] = got
-        if k + CHUNK == HALF:
-            send_ref[:, at] = got.astype(BF16)
-    down_copy.wait()
+    xs, gain_ref, sources = refs[:5], refs[5], refs[6:8]
+    own_ref, sq_ref, send_ref, wg_ref, wu_ref = refs[10:15]
+    scaled_ref, sems = refs[15:]
+    late = lax.axis_index("role") == 0
+    targets = (wg_ref, wu_ref)
+    steps, copies = weight_copies(sources, targets, sems)
+
+    @pl.when(late)
+    def _():
+        for c in copies:
+            c.start()
+
+    @pl.when(late)
+    def _():
+        for n, x_ref in enumerate(xs):
+            zero = jnp.zeros((PART, HD), F32)
+            acc = scale_rows(x_ref, gain_ref, scaled_ref, n * PART, slice(0, HALF), zero)
+            put_squares(acc, n * PART, sq_ref, send_ref)
+        for n, (k, w) in enumerate(steps):
+            copies[n].wait()
+            rows = slice(k, k + CHUNK)
+            at = slice(w * HIDDEN, (w + 1) * HIDDEN)
+            got = jnp.dot(scaled_ref[:, rows], targets[w][rows], preferred_element_type=F32)
+            if k:
+                got = got + own_ref[:, at]
+            own_ref[:, at] = got
+            if k + CHUNK == HALF:
+                send_ref[:, at] = got.astype(BF16)
+    @pl.when(jnp.logical_not(late))
+    def _():
+        gate_up(xs, gain_ref, wg_ref, wu_ref, own_ref, sq_ref, send_ref, scaled_ref, 2 * CHUNK)
 
 
 def second_body(*refs):
     xs, (gain_ref, wg_ref, wu_ref) = refs[:3], refs[3:6]
     own_ref, sq_ref, send_ref, scaled_ref = refs[6:]
-    for n, x_ref in enumerate(xs):
-        scale_rows(
-            x_ref, lambda c: gain_ref[:, c : c + HD], scaled_ref, n * PART, sq_ref, send_ref
-        )
-    x = scaled_ref[...]
-    for at, w_ref in ((0, wg_ref), (HIDDEN, wu_ref)):
-        got = jnp.dot(x, w_ref[...], preferred_element_type=F32)
-        own_ref[:, at : at + HIDDEN] = got
-        send_ref[:, at : at + HIDDEN] = got.astype(BF16)
+    gate_up(xs, gain_ref, wg_ref, wu_ref, own_ref, sq_ref, send_ref, scaled_ref, 2 * CHUNK)
 
 
 def coordinates():
     role, x, y = (lax.axis_index(n) for n in ("role", "x", "y"))
-    return jnp.where(role == 0, x, y), jnp.where(role == 0, y, x)
-
-
-def down_body(own0, sq0, own1, sq1, got0, got1, wd_ref, *rest):
-    outs, (act_ref, got_ref) = rest[:8], rest[8:]
+    return jnp.where(role == 0, y, x), jnp.where(role == 0, x, y)
+
+
+def down_body(blocks, splits, own0, sq0, own1, sq1, got0, got1, wd_ref, *rest):
+    outs, (act_ref, got_ref) = rest[: len(splits)], rest[len(splits) :]
     early = got0.shape[0]
     got_ref[:early] = got0[...]
     got_ref[early:] = got1[...]
     my_a, my_b = coordinates()
-    for jp in range(2):
-        for jb in range(4):
-            for ai in range(2):
-                at = (jp * 8 + jb * 2 + ai) * 16
-                ours, sqs, mine = (own0, sq0, at) if at < early else (own1, sq1, at - early)
-                away = lax.rem(my_a - 2 * lax.rem(my_a // 2 + jp, 2) - ai + 4, 4)
-                peer_b = jnp.where(away == 2, 1, jnp.where(away == 1, 2, away))
-                peer_a = lax.rem(my_b - SHIFTS[jb] + 4, 4)
-                peer_p = lax.rem(peer_a // 2 + my_b // 2, 2)
-                peer = (peer_p * 8 + peer_b * 2 + lax.rem(peer_a, 2)) * 16
-                got = got_ref[pl.ds(pl.multiple_of(peer, 16), 16)].astype(F32)
-                lane = 2 * HIDDEN
-                extra = got[:, lane : lane + 1] + got[:, lane + HD // 2 : lane + HD // 2 + 1]
-                total = sqs[mine : mine + 16][:, :1] + extra
-                inv = lax.rsqrt(total / MODEL_WIDTH + 1e-05)
-                pre = ours[mine : mine + 16] + got[:, : 2 * HIDDEN]
-                pre = jnp.where(inv > 0.0, pre * inv, 0.0)
-                gate = pre[:, :HIDDEN]
-                act = gate * jax.nn.sigmoid(gate) * pre[:, HIDDEN:]
-                act_ref[at : at + 16] = act.astype(BF16)
+    for n, (jp, jb) in enumerate(blocks):
+        for ai in range(2):
+            at = (jp * 8 + jb * 2 + ai) * 16
+            ours, sqs, mine = (own0, sq0, at) if at < early else (own1, sq1, at - early)
+            away = lax.rem(my_a - 2 * lax.rem(my_a // 2 + jp, 2) - ai + 4, 4)
+            peer_b = jnp.where(away == 2, 1, jnp.where(away == 1, 2, away))
+            peer_a = lax.rem(my_b - SHIFTS[jb] + 4, 4)
+            peer_p = lax.rem(peer_a // 2 + my_b // 2, 2)
+            peer = (peer_p * 8 + peer_b * 2 + lax.rem(peer_a, 2)) * 16
+            got = got_ref[pl.ds(pl.multiple_of(peer, 16), 16)].astype(F32)
+            lane = 2 * HIDDEN
+            extra = got[:, lane : lane + 1] + got[:, lane + HD // 2 : lane + HD // 2 + 1]
+            total = sqs[mine : mine + 16][:, :1] + extra
+            inv = lax.rsqrt(total / MODEL_WIDTH + 1e-05)
+            pre = ours[mine : mine + 16] + got[:, : 2 * HIDDEN]
+            pre = jnp.where(inv > 0.0, pre * inv, 0.0)
+            gate = pre[:, :HIDDEN]
+            act = gate * jax.nn.sigmoid(gate) * pre[:, HIDDEN:]
+            act_ref[(n * 2 + ai) * 16 : (n * 2 + ai + 1) * 16] = act.astype(BF16)
     act = act_ref[...]
-    for n in range(0, HALF, 512):
-        got = jnp.dot(act, wd_ref[:, n : n + 512], preferred_element_type=F32).astype(BF16)
-        for j in range(8):
-            outs[j][:, n : n + 512] = got[j * PART : (j + 1) * PART]
+    for c in range(0, HALF, 512):
+        got = jnp.dot(act, wd_ref[:, c : c + 512], preferred_element_type=F32).astype(BF16)
+        start = 0
+        for out_ref, rows in zip(outs, splits):
+            out_ref[:, c : c + 512] = got[start : start + rows]
+            start += rows
 
 
 def sum_body(*refs):
@@ -304,7 +342,7 @@
     return lax.ppermute(
         value,
         AXES,
-        permutation(lambda r, z, x, y: along_y(s, r, z, x, y) if r == 0 else along_x(s, r, z, x, y)),
+        permutation(lambda r, z, x, y: along_x(s, r, z, x, y) if r == 0 else along_y(s, r, z, x, y)),
     )
 
 
@@ -312,7 +350,7 @@
     return lax.ppermute(
         value,
         AXES,
-        permutation(lambda r, z, x, y: along_x(2, r, z, x, y) if r == 0 else along_y(2, r, z, x, y)),
+        permutation(lambda r, z, x, y: along_y(2, r, z, x, y) if r == 0 else along_x(2, r, z, x, y)),
     )
 
 
@@ -325,8 +363,8 @@
     for p in (0, 2):
         for o in range(4):
             pair = [(a, z) for a in (p, p + 1) for z in range(8)]
-            groups.append([index_of(0, z, a, o) for a, z in pair])
-            groups.append([index_of(1, z, o, a) for a, z in pair])
+            groups.append([index_of(0, z, o, a) for a, z in pair])
+            groups.append([index_of(1, z, a, o) for a, z in pair])
     return lax.all_to_all(
         value, AXES, split_axis=0, concat_axis=0, axis_index_groups=groups, tiled=True
     )
@@ -336,10 +374,10 @@
     query, new_kv, kv_cache, lengths, residual, norm_gain, expert_ids, router_logits, w_gate, w_up, w_down
 ):
     shape = jax.ShapeDtypeStruct
-    hidden, outgoing, comb = call(
+    hidden, outgoing, comb, gain = call(
         attend_body,
-        (shape((ROWS, HALF), BF16), shape((2 * EXPERTS, CAP, HALF), BF16), shape((4 * ROWS, HD), BF16)),
-        [HBM_SPEC] * 7,
+        (shape((ROWS, HALF), BF16), shape((2 * EXPERTS, CAP, HALF), BF16), shape((4 * ROWS, HD), BF16), shape((1, HALF), F32)),
+        [HBM_SPEC] * 8,
         flops=50_000_000,
         nbytes=1_200_000,
         scratch=[
@@ -351,11 +389,26 @@
             pltpu.VMEM((ROWS, CTX, HIDDEN), BF16),
             pltpu.VMEM((ROWS, CTX, HIDDEN), BF16),
             pltpu.VMEM((ROWS, HALF), BF16),
-            pltpu.SemaphoreType.DMA((8,)),
+            pltpu.VMEM((HALF,), BF16),
+            pltpu.SemaphoreType.DMA((9,)),
         ],
-    )(*map(in_hbm, (lengths, expert_ids.T, router_logits, query, new_kv, kv_cache, residual)))
+    )(*map(in_hbm, (lengths, expert_ids.T, router_logits, query, new_kv, kv_cache, residual, norm_gain)))
     near = exchange(outgoing).reshape(PART, HALF)
     far = send_a(near)
+    blocks = (
+        pltpu.VMEM((HALF, HIDDEN), BF16),
+        pltpu.VMEM((HALF, HIDDEN), BF16),
+    )
+    count = 2 * HALF // CHUNK
+    sources = tuple(map(in_hbm, (w_gate, w_up)))
+    ahead = call(
+        ahead_body,
+        blocks,
+        [VMEM_SPEC] + [HBM_SPEC] * 2,
+        nbytes=12_000_000,
+        scratch=[pltpu.SemaphoreType.DMA((count,))],
+    )(near, *sources)
+    near, *ahead = lax.optimization_barrier((near, *ahead))
     near_b = [send_b(near, s) for s in ORDER]
     far_b = [send_b(far, s) for s in ORDER]
 
@@ -366,24 +419,18 @@
             shape((rows, 2 * HIDDEN + HD), BF16),
         )
 
-    own0, sq0, send0, gain, wg, wu, wd = call(
+    own0, sq0, send0, wg, wu = call(
         first_body,
-        partials(5 * PART)
-        + (
-            shape((1, HALF), F32),
-            pltpu.VMEM((HALF, HIDDEN), BF16),
-            pltpu.VMEM((HALF, HIDDEN), BF16),
-            pltpu.VMEM((HIDDEN, HALF), BF16),
-        ),
-        [VMEM_SPEC] * 5 + [HBM_SPEC] * 4,
+        partials(5 * PART) + blocks,
+        [VMEM_SPEC] * 6 + [HBM_SPEC] * 2 + [VMEM_SPEC] * 2,
         flops=2 * 5 * PART * HALF * 1024,
         nbytes=20_000_000,
         scratch=[
-            pltpu.VMEM((HALF,), BF16),
             pltpu.VMEM((5 * PART, HALF), BF16),
-            pltpu.SemaphoreType.DMA((2 * HALF // CHUNK + 2,)),
+            pltpu.SemaphoreType.DMA((count,)),
         ],
-    )(near, *near_b, far, *map(in_hbm, (norm_gain, w_gate, w_up, w_down)))
+        aliases={8: 3, 9: 4},
+    )(near, *near_b, far, gain, *sources, *ahead)
     own1, sq1, send1 = call(
         second_body,
         partials(3 * PART),
@@ -392,16 +439,23 @@
         nbytes=8_000_000,
         scratch=[pltpu.VMEM((3 * PART, HALF), BF16)],
     )(*far_b, gain, wg, wu)
-    terms = call(
-        down_body,
-        [shape((PART, HALF), BF16)] * 8,
-        [VMEM_SPEC] * 7,
-        flops=2 * 256 * HALF * 512,
-        nbytes=6_000_000,
-        scratch=[pltpu.VMEM((256, HIDDEN), BF16), pltpu.VMEM((256, 2 * HIDDEN + HD), BF16)],
-    )(own0, sq0, own1, sq1, swap(send0), swap(send1), wd)
-
-    def add_up(parts):
+    swapped0, swapped1 = swap(send0), swap(send1)
+
+    def down(blocks, splits):
+        rows = PART * len(blocks)
+        return call(
+            functools.partial(down_body, blocks, splits),
+            [shape((n, HALF), BF16) for n in splits],
+            [VMEM_SPEC] * 7,
+            flops=2 * rows * HALF * 512,
+            nbytes=5_000_000,
+            scratch=[pltpu.VMEM((rows, HIDDEN), BF16), pltpu.VMEM((256, 2 * HIDDEN + HD), BF16)],
+        )(own0, sq0, own1, sq1, swapped0, swapped1, w_down[0])
+
+    far_terms = down(tuple((1, j) for j in range(4)), (PART,) * 4)
+    near_terms = down(tuple((0, j) for j in range(4)), (PART,) * 4)
+
+    def add_up(*parts):
         return call(
             sum_body,
             shape((PART, HALF), BF16),
@@ -410,9 +464,9 @@
             nbytes=1_000_000,
         )(*parts)
 
-    far_sum = add_up([terms[4]] + [send_b(terms[4 + j], -SHIFTS[j]) for j in (1, 2, 3)])
-    near_got = [send_b(terms[j], -SHIFTS[j]) for j in (1, 2, 3)]
-    summed = add_up([terms[0]] + near_got + [send_a(far_sum)])
+    far_sum = add_up(far_terms[0], *[send_b(far_terms[j], -SHIFTS[j]) for j in (1, 2, 3)])
+    near_got = [send_b(near_terms[j], -SHIFTS[j]) for j in (2, 3, 1)]
+    summed = add_up(near_terms[0], *near_got, send_a(far_sum))
     back = exchange(summed.reshape(2 * EXPERTS, CAP, HALF)).reshape(PART, HALF)
     return call(
         combine_body,

time: 77.7 us -> 75.8 us (0.976)
  starting transfers between devices: 27.3 us -> 25.3 us
  blocking collectives: 30.8 us -> 31.6 us
    ppermute x14, starting transfers between devices: 26.6 us -> 25.1 us  [the longest x12 19.7 us: send_b(): lax.ppermute(value, AXES, permutation(lambda r, z, x, y: along_x(s, r, z,...]
    pallas_call x2 -> x4, Pallas kernels: 5.19 us -> 4.93 us  [the longest x1 3.24 us: per_device(): call(first_body, partials(5 * PART) + blocks, [VMEM_SPEC] * 6 + [HBM_SPEC...]
  transfers between devices with their start and end apart: 16 -> 16, of which waited for: 5 -> 6; matrix products, arithmetic and copies ran while one was open for 0% -> 0% of each run, Pallas kernels for 7% -> 7%
where the time goes in v4:
time: 75.8 us; the launch traced here: 75.6 us
  blocking collectives  31.6 us (42%)
  starting transfers between devices  25.3 us (33%)
  waiting for transfers between devices  9.3 us (12%)
  Pallas kernels  9.13 us (12%)
    all_to_all x2, blocking collectives, exchange(): lax.all_to_all(value, AXES, split_axis=0, concat_axis=0, axis_index_group...  31.6 us
    ppermute x12, starting transfers between devices, send_b(): lax.ppermute(value, AXES, permutation(lambda r, z, x, y: along_x(s, r, z,...  19.7 us
    ppermute x12, waiting for transfers between devices, send_b(): lax.ppermute(value, AXES, permutation(lambda r, z, x, y: along_x(s, r, z,...  7.84 us
    ppermute x2, starting transfers between devices, send_a(): lax.ppermute(value, AXES, permutation(lambda r, z, x, y: along_y(2, r, z,...  5.4 us
    pallas_call x1, Pallas kernels, per_device(): call(first_body, partials(5 * PART) + blocks, [VMEM_SPEC] * 6 + [HBM_SPEC...  3.24 us
    pallas_call x1, Pallas kernels, per_device(): call(attend_body, (shape((ROWS, HALF), BF16), shape((2 * EXPERTS, CAP, HA...  1.99 us
    pallas_call x2, Pallas kernels, down(): call(functools.partial(down_body, blocks, splits), [shape((n, HALF), BF16...  1.61 us
  transfers between devices with their start and end apart: 16, of which 6 were waited for; matrix products, arithmetic and copies ran while one was open for 0% of the time, Pallas kernels for 7%

profile of v4, /device:TPU:32, one launch (start us, length us, event | category | flops | bytes accessed | tf_op | source)
XLA Modules:
  0.0 75.6 jit_solution(16162739701275761711)
XLA Ops:
  0.0 2.0 %shard_map.109 = (bf16[4,3072]{1,0:T(4,128)(2,1)S(1)}, bf16[16,2,3072]{2,1,0:T(2,128)(2,1)S(1)}, bf16[16,128]{1,0:T(8,128)(2,1)S(1)}, f32[1,3072]{1,0:T(1,128)S(1)}) custom-call(s32[4]{0:T(128)} %len_hbm.1, s32[2,4]{1,0:T(2,128)} %bitcast.4, f32[4,8]{1,0:T(4,128)} %logit_hbm.1, bf16[4,3072]{1,0:T(4,128)(2,1)} %q_hbm.1, bf16[4,2,512]{2,1,0:T(2,128)(2,1)} %new_hbm.1, ...), custom_call_target="tpu_custom_call" | custom-call | flops 50000000 | bytes 1200000 | tf_op jit(solution)/shard_map/pallas_call | solution.py:377
  2.0 18.3 %all_to_all.10 = bf16[16,2,3072]{2,1,0:T(2,128)(2,1)S(1)} all-to-all(bf16[16,2,3072]{2,1,0:T(2,128)(2,1)S(1)} %get-tuple-element.32), channel_id=1, replica_groups={{0,16,32,48,64,80,96,112,1,17,33,49,65,81,97,113},{128,144,160,176,192,..., dimensions={0} | all-to-all | bytes 393216 | tf_op jit(solution)/shard_map/all_to_all | solution.py:368
  20.3 3.0 %collective-permute-start.3 = (bf16[32,3072]{1,0:T(8,128)(2,1)S(1)}, bf16[32,3072]{1,0:T(8,128)(2,1)S(1)}, u32[]{:S(2)}, u32[]{:S(2)}) collective-permute-start(bf16[32,3072]{1,0:T(8,128)(2,1)S(1)} %reshape.9.after_ref.refs_0_), channel_id=1, source_target_pairs={{0,2},{1,3},{2,0},{3,1},{4,6},{5,7},{6,4},{7,5},{8,10},{9,11},{10,... | collective-permute-start | bytes 589832 | tf_op jit(solution)/shard_map/ppermute | solution.py:350
  23.4 3.1 %collective-permute-start = (bf16[32,3072]{1,0:T(8,128)(2,1)S(1)}, bf16[32,3072]{1,0:T(8,128)(2,1)S(1)}, u32[]{:S(2)}, u32[]{:S(2)}) collective-permute-start(bf16[32,3072]{1,0:T(8,128)(2,1)S(1)} %reshape.9.after_ref.refs_0_), channel_id=1, source_target_pairs={{0,8},{1,9},{2,10},{3,11},{4,12},{5,13},{6,14},{7,15},{8,0},{9,1},... | collective-permute-start | bytes 589832 | tf_op jit(solution)/shard_map/ppermute | solution.py:342
  26.5 0.9 %collective-permute-start.1 = (bf16[32,3072]{1,0:T(8,128)(2,1)S(1)}, bf16[32,3072]{1,0:T(8,128)(2,1)S(1)}, u32[]{:S(2)}, u32[]{:S(2)}) collective-permute-start(bf16[32,3072]{1,0:T(8,128)(2,1)S(1)} %reshape.9.after_ref.refs_0_), channel_id=1, source_target_pairs={{0,4},{1,5},{2,6},{3,7},{4,8},{5,9},{6,10},{7,11},{8,12},{9,13},{1... | collective-permute-start | bytes 589832 | tf_op jit(solution)/shard_map/ppermute | solution.py:342
  27.4 2.3 %collective-permute-start.2 = (bf16[32,3072]{1,0:T(8,128)(2,1)S(1)}, bf16[32,3072]{1,0:T(8,128)(2,1)S(1)}, u32[]{:S(2)}, u32[]{:S(2)}) collective-permute-start(bf16[32,3072]{1,0:T(8,128)(2,1)S(1)} %reshape.9.after_ref.refs_0_), channel_id=1, source_target_pairs={{0,12},{1,13},{2,14},{3,15},{4,0},{5,1},{6,2},{7,3},{8,4},{9,5},{1... | collective-permute-start | bytes 589832 | tf_op jit(solution)/shard_map/ppermute | solution.py:342
  29.7 1.8 %collective-permute-start.4 = (bf16[32,3072]{1,0:T(8,128)(2,1)S(1)}, bf16[32,3072]{1,0:T(8,128)(2,1)S(1)}, u32[]{:S(2)}, u32[]{:S(2)}) collective-permute-start(bf16[32,3072]{1,0:T(8,128)(2,1)S(1)} %collective-permute-done.3.refs_4_), channel_id=1, source_target_pairs={{0,8},{1,9},{2,10},{3,11},{4,12},{5,13},{6,14},{7,15},{8,0},{9,1},... | collective-permute-start | bytes 589832 | tf_op jit(solution)/shard_map/ppermute | solution.py:342
  31.8 3.0 %collective-permute-start.6 = (bf16[32,3072]{1,0:T(8,128)(2,1)S(1)}, bf16[32,3072]{1,0:T(8,128)(2,1)S(1)}, u32[]{:S(2)}, u32[]{:S(2)}) collective-permute-start(bf16[32,3072]{1,0:T(8,128)(2,1)S(1)} %collective-permute-done.3.refs_4_), channel_id=1, source_target_pairs={{0,12},{1,13},{2,14},{3,15},{4,0},{5,1},{6,2},{7,3},{8,4},{9,5},{1... | collective-permute-start | bytes 589832 | tf_op jit(solution)/shard_map/ppermute | solution.py:342
  35.1 3.2 %shard_map.111 = (f32[160,1024]{1,0:T(8,128)S(1)}, f32[160,128]{1,0:T(8,128)S(1)}, bf16[160,1152]{1,0:T(8,128)(2,1)S(1)}, bf16[3072,512]{1,0:T(8,128)(2,1)S(1)}, bf16[3072,512]{1,0:T(8,128)(2,1)S(1)}) custom-call(bf16[32,3072]{1,0:T(8,128)(2,1)S(1)} %reshape.9.after_ref.refs_0_, ...), custom_call_target="tpu_custom_call", output_to_operand_aliasing={{3}: (8, {}), {4}: (9, {})} | custom-call | flops 1006632960 | bytes 20000000 | tf_op jit(solution)/shard_map/pallas_call | solution.py:422
  38.4 0.6 collective-permute-done.5.refs_1_
  39.0 1.2 %shard_map.112 = (f32[96,1024]{1,0:T(8,128)S(1)}, f32[96,128]{1,0:T(8,128)S(1)}, bf16[96,1152]{1,0:T(8,128)(2,1)S(1)}) custom-call(bf16[32,3072]{1,0:T(8,128)(2,1)S(1)} %collective-permute-done.4.refs_0_, bf16[32,3072]{1,0:T(8,128)(2,1)S(1)} %collective-permute-done.5.refs_1_, bf16[32,3072]{1,0:T(8,128)(2,1)S(1)} %collective-permute-done.6.refs_2_, ...), custom_call_target="tpu_custom_call" | custom-call | flops 603979776 | bytes 8000000 | tf_op jit(solution)/shard_map/pallas_call | solution.py:434
  40.4 1.5 %collective-permute-done.8.got1 = bf16[96,1152]{1,0:T(8,128)(2,1)S(1)} collective-permute-done((bf16[96,1152]{1,0:T(8,128)(2,1)S(1)}, bf16[96,1152]{1,0:T(8,128)(2,1)S(1)}, u32[]{:S(2)}, u32[]{:S(2)}) %collective-permute-start.8) | collective-permute-done | bytes 221216 | tf_op jit(solution)/shard_map/ppermute | solution.py:358
  41.8 0.8 %shard_map.114 = (bf16[32,3072]{1,0:T(8,128)(2,1)S(1)}, bf16[32,3072]{1,0:T(8,128)(2,1)S(1)}, bf16[32,3072]{1,0:T(8,128)(2,1)S(1)}, bf16[32,3072]{1,0:T(8,128)(2,1)S(1)}) custom-call(f32[160,1024]{1,0:T(8,128)S(1)} %get-tuple-element.39.own0, f32[160,128]{1,0:T(8,128)S(1)} %get-tuple-element.40.sq0, f32[96,1024]{1,0:T(8,128)S(1)} %get-tuple-element.43.own1, ...), custom_call_target="tpu_custom_call" | custom-call | flops 402653184 | bytes 5000000 | tf_op jit(solution)/shard_map/pallas_call | solution.py:446
  42.6 1.9 %collective-permute-start.12 = (bf16[32,3072]{1,0:T(8,128)(2,1)S(1)}, bf16[32,3072]{1,0:T(8,128)(2,1)S(1)}, u32[]{:S(2)}, u32[]{:S(2)}) collective-permute-start(bf16[32,3072]{1,0:T(8,128)(2,1)S(1)} %get-tuple-element.52), channel_id=1, source_target_pairs={{0,8},{1,9},{2,10},{3,11},{4,12},{5,13},{6,14},{7,15},{8,0},{9,1},... | collective-permute-start | bytes 589832 | tf_op jit(solution)/shard_map/ppermute | solution.py:342
  44.5 1.5 %collective-permute-start.13 = (bf16[32,3072]{1,0:T(8,128)(2,1)S(1)}, bf16[32,3072]{1,0:T(8,128)(2,1)S(1)}, u32[]{:S(2)}, u32[]{:S(2)}) collective-permute-start(bf16[32,3072]{1,0:T(8,128)(2,1)S(1)} %get-tuple-element.53), channel_id=1, source_target_pairs={{0,12},{1,13},{2,14},{3,15},{4,0},{5,1},{6,2},{7,3},{8,4},{9,5},{1... | collective-permute-start | bytes 589832 | tf_op jit(solution)/shard_map/ppermute | solution.py:342
  46.0 0.8 %collective-permute-start.14 = (bf16[32,3072]{1,0:T(8,128)(2,1)S(1)}, bf16[32,3072]{1,0:T(8,128)(2,1)S(1)}, u32[]{:S(2)}, u32[]{:S(2)}) collective-permute-start(bf16[32,3072]{1,0:T(8,128)(2,1)S(1)} %get-tuple-element.54), channel_id=1, source_target_pairs={{0,4},{1,5},{2,6},{3,7},{4,8},{5,9},{6,10},{7,11},{8,12},{9,13},{1... | collective-permute-start | bytes 589832 | tf_op jit(solution)/shard_map/ppermute | solution.py:342
  46.8 0.8 %shard_map.113 = (bf16[32,3072]{1,0:T(8,128)(2,1)S(1)}, bf16[32,3072]{1,0:T(8,128)(2,1)S(1)}, bf16[32,3072]{1,0:T(8,128)(2,1)S(1)}, bf16[32,3072]{1,0:T(8,128)(2,1)S(1)}) custom-call(f32[160,1024]{1,0:T(8,128)S(1)} %get-tuple-element.39.own0, f32[160,128]{1,0:T(8,128)S(1)} %get-tuple-element.40.sq0, f32[96,1024]{1,0:T(8,128)S(1)} %get-tuple-element.43.own1, ...), custom_call_target="tpu_custom_call" | custom-call | flops 402653184 | bytes 5000000 | tf_op jit(solution)/shard_map/pallas_call | solution.py:446
  47.6 2.5 %collective-permute-start.9 = (bf16[32,3072]{1,0:T(8,128)(2,1)S(1)}, bf16[32,3072]{1,0:T(8,128)(2,1)S(1)}, u32[]{:S(2)}, u32[]{:S(2)}) collective-permute-start(bf16[32,3072]{1,0:T(8,128)(2,1)S(1)} %get-tuple-element.48), channel_id=1, source_target_pairs={{0,12},{1,13},{2,14},{3,15},{4,0},{5,1},{6,2},{7,3},{8,4},{9,5},{1... | collective-permute-start | bytes 589832 | tf_op jit(solution)/shard_map/ppermute | solution.py:342
  50.1 1.6 %collective-permute-start.11 = (bf16[32,3072]{1,0:T(8,128)(2,1)S(1)}, bf16[32,3072]{1,0:T(8,128)(2,1)S(1)}, u32[]{:S(2)}, u32[]{:S(2)}) collective-permute-start(bf16[32,3072]{1,0:T(8,128)(2,1)S(1)} %get-tuple-element.50), channel_id=1, source_target_pairs={{0,8},{1,9},{2,10},{3,11},{4,12},{5,13},{6,14},{7,15},{8,0},{9,1},... | collective-permute-start | bytes 589832 | tf_op jit(solution)/shard_map/ppermute | solution.py:342
  51.8 0.8 %collective-permute-done.13.refs_2_ = bf16[32,3072]{1,0:T(8,128)(2,1)S(1)} collective-permute-done((bf16[32,3072]{1,0:T(8,128)(2,1)S(1)}, bf16[32,3072]{1,0:T(8,128)(2,1)S(1)}, u32[]{:S(2)}, u32[]{:S(2)}) %collective-permute-start.13) | collective-permute-done | bytes 196640 | tf_op jit(solution)/shard_map/ppermute | solution.py:342
  53.0 2.4 %collective-permute-start.15 = (bf16[32,3072]{1,0:T(8,128)(2,1)S(1)}, bf16[32,3072]{1,0:T(8,128)(2,1)S(1)}, u32[]{:S(2)}, u32[]{:S(2)}) collective-permute-start(bf16[32,3072]{1,0:T(8,128)(2,1)S(1)} %shard_map.115), channel_id=1, source_target_pairs={{0,2},{1,3},{2,0},{3,1},{4,6},{5,7},{6,4},{7,5},{8,10},{9,11},{10,... | collective-permute-start | bytes 589832 | tf_op jit(solution)/shard_map/ppermute | solution.py:350
  55.4 5.8 %collective-permute-done.10.refs_2_ = bf16[32,3072]{1,0:T(8,128)(2,1)S(1)} collective-permute-done((bf16[32,3072]{1,0:T(8,128)(2,1)S(1)}, bf16[32,3072]{1,0:T(8,128)(2,1)S(1)}, u32[]{:S(2)}, u32[]{:S(2)}) %collective-permute-start.10) | collective-permute-done | bytes 196640 | tf_op jit(solution)/shard_map/ppermute | solution.py:342
  61.4 13.3 %all_to_all.11 = bf16[16,2,3072]{2,1,0:T(2,128)(2,1)S(1)} all-to-all(bf16[16,2,3072]{2,1,0:T(2,128)(2,1)S(1)} %reshape.10), channel_id=1, replica_groups={{0,16,32,48,64,80,96,112,1,17,33,49,65,81,97,113},{128,144,160,176,192,..., dimensions={0} | all-to-all | bytes 393216 | tf_op jit(solution)/shard_map/all_to_all | solution.py:368
  74.8 0.8 %shard_map.117 = bf16[4,3072]{1,0:T(4,128)(2,1)} custom-call(bf16[16,128]{1,0:T(8,128)(2,1)S(1)} %get-tuple-element.30.comb_ref, bf16[4,3072]{1,0:T(4,128)(2,1)S(1)} %get-tuple-element.31.hidden_ref, bf16[32,3072]{1,0:T(8,128)(2,1)S(1)} %reshape.11.back_ref), custom_call_target="tpu_custom_call" | custom-call | flops 100000 | bytes 150000 | tf_op jit(solution)/shard_map/pallas_call | solution.py:471
  (24 shorter events, 1.6 us)
Async XLA Ops:
  20.3 9.4 %collective-permute-start.3 = (bf16[32,3072]{1,0:T(8,128)(2,1)S(1)}, bf16[32,3072]{1,0:T(8,128)(2,1)S(1)}, u32[]{:S(2)}, u32[]{:S(2)}) collective-permute-start(bf16[32,3072]{1,0:T(8,128)(2,1)S(1)} %reshape.9.after_ref.refs_0_), channel_id=1, source_target_pairs={{0,2},{1,3},{2,0},{3,1},{4,6},{5,7},{6,4},{7,5},{8,10},{9,11},{10,... | collective-permute-start | bytes 589832 | tf_op jit(solution)/shard_map/ppermute | solution.py:350
  23.4 8.4 %collective-permute-start = (bf16[32,3072]{1,0:T(8,128)(2,1)S(1)}, bf16[32,3072]{1,0:T(8,128)(2,1)S(1)}, u32[]{:S(2)}, u32[]{:S(2)}) collective-permute-start(bf16[32,3072]{1,0:T(8,128)(2,1)S(1)} %reshape.9.after_ref.refs_0_), channel_id=1, source_target_pairs={{0,8},{1,9},{2,10},{3,11},{4,12},{5,13},{6,14},{7,15},{8,0},{9,1},... | collective-permute-start | bytes 589832 | tf_op jit(solution)/shard_map/ppermute | solution.py:342
  26.5 8.3 %collective-permute-start.1 = (bf16[32,3072]{1,0:T(8,128)(2,1)S(1)}, bf16[32,3072]{1,0:T(8,128)(2,1)S(1)}, u32[]{:S(2)}, u32[]{:S(2)}) collective-permute-start(bf16[32,3072]{1,0:T(8,128)(2,1)S(1)} %reshape.9.after_ref.refs_0_), channel_id=1, source_target_pairs={{0,4},{1,5},{2,6},{3,7},{4,8},{5,9},{6,10},{7,11},{8,12},{9,13},{1... | collective-permute-start | bytes 589832 | tf_op jit(solution)/shard_map/ppermute | solution.py:342
  27.4 7.6 %collective-permute-start.2 = (bf16[32,3072]{1,0:T(8,128)(2,1)S(1)}, bf16[32,3072]{1,0:T(8,128)(2,1)S(1)}, u32[]{:S(2)}, u32[]{:S(2)}) collective-permute-start(bf16[32,3072]{1,0:T(8,128)(2,1)S(1)} %reshape.9.after_ref.refs_0_), channel_id=1, source_target_pairs={{0,12},{1,13},{2,14},{3,15},{4,0},{5,1},{6,2},{7,3},{8,4},{9,5},{1... | collective-permute-start | bytes 589832 | tf_op jit(solution)/shard_map/ppermute | solution.py:342
  29.7 8.7 %collective-permute-start.4 = (bf16[32,3072]{1,0:T(8,128)(2,1)S(1)}, bf16[32,3072]{1,0:T(8,128)(2,1)S(1)}, u32[]{:S(2)}, u32[]{:S(2)}) collective-permute-start(bf16[32,3072]{1,0:T(8,128)(2,1)S(1)} %collective-permute-done.3.refs_4_), channel_id=1, source_target_pairs={{0,8},{1,9},{2,10},{3,11},{4,12},{5,13},{6,14},{7,15},{8,0},{9,1},... | collective-permute-start | bytes 589832 | tf_op jit(solution)/shard_map/ppermute | solution.py:342
  31.5 7.5 %collective-permute-start.5 = (bf16[32,3072]{1,0:T(8,128)(2,1)S(1)}, bf16[32,3072]{1,0:T(8,128)(2,1)S(1)}, u32[]{:S(2)}, u32[]{:S(2)}) collective-permute-start(bf16[32,3072]{1,0:T(8,128)(2,1)S(1)} %collective-permute-done.3.refs_4_), channel_id=1, source_target_pairs={{0,4},{1,5},{2,6},{3,7},{4,8},{5,9},{6,10},{7,11},{8,12},{9,13},{1... | collective-permute-start | bytes 589832 | tf_op jit(solution)/shard_map/ppermute | solution.py:342
  31.8 7.2 %collective-permute-start.6 = (bf16[32,3072]{1,0:T(8,128)(2,1)S(1)}, bf16[32,3072]{1,0:T(8,128)(2,1)S(1)}, u32[]{:S(2)}, u32[]{:S(2)}) collective-permute-start(bf16[32,3072]{1,0:T(8,128)(2,1)S(1)} %collective-permute-done.3.refs_4_), channel_id=1, source_target_pairs={{0,12},{1,13},{2,14},{3,15},{4,0},{5,1},{6,2},{7,3},{8,4},{9,5},{1... | collective-permute-start | bytes 589832 | tf_op jit(solution)/shard_map/ppermute | solution.py:342
  38.3 2.0 %collective-permute-start.7 = (bf16[160,1152]{1,0:T(8,128)(2,1)S(1)}, bf16[160,1152]{1,0:T(8,128)(2,1)S(1)}, u32[]{:S(2)}, u32[]{:S(2)}) collective-permute-start(bf16[160,1152]{1,0:T(8,128)(2,1)S(1)} %get-tuple-element.45), channel_id=1, source_target_pairs={{0,128},{128,0},{1,129},{129,1},{2,130},{130,2},{3,131},{131,3},{4... | collective-permute-start | bytes 1105928 | tf_op jit(solution)/shard_map/ppermute | solution.py:358
  39.0 2.8 %copy-start = (bf16[1,512,3072]{2,1,0:T(8,128)(2,1)S(1)}, bf16[1,512,3072]{2,1,0:T(8,128)(2,1)}, u32[]{:S(2)}) copy-start(bf16[1,512,3072]{2,1,0:T(8,128)(2,1)} %param.21) | copy-start | bytes 9437188
  40.2 1.6 %collective-permute-start.8 = (bf16[96,1152]{1,0:T(8,128)(2,1)S(1)}, bf16[96,1152]{1,0:T(8,128)(2,1)S(1)}, u32[]{:S(2)}, u32[]{:S(2)}) collective-permute-start(bf16[96,1152]{1,0:T(8,128)(2,1)S(1)} %get-tuple-element.46), channel_id=1, source_target_pairs={{0,128},{128,0},{1,129},{129,1},{2,130},{130,2},{3,131},{131,3},{4... | collective-permute-start | bytes 663560 | tf_op jit(solution)/shard_map/ppermute | solution.py:358
  42.6 7.5 %collective-permute-start.12 = (bf16[32,3072]{1,0:T(8,128)(2,1)S(1)}, bf16[32,3072]{1,0:T(8,128)(2,1)S(1)}, u32[]{:S(2)}, u32[]{:S(2)}) collective-permute-start(bf16[32,3072]{1,0:T(8,128)(2,1)S(1)} %get-tuple-element.52), channel_id=1, source_target_pairs={{0,8},{1,9},{2,10},{3,11},{4,12},{5,13},{6,14},{7,15},{8,0},{9,1},... | collective-permute-start | bytes 589832 | tf_op jit(solution)/shard_map/ppermute | solution.py:342
  44.5 8.1 %collective-permute-start.13 = (bf16[32,3072]{1,0:T(8,128)(2,1)S(1)}, bf16[32,3072]{1,0:T(8,128)(2,1)S(1)}, u32[]{:S(2)}, u32[]{:S(2)}) collective-permute-start(bf16[32,3072]{1,0:T(8,128)(2,1)S(1)} %get-tuple-element.53), channel_id=1, source_target_pairs={{0,12},{1,13},{2,14},{3,15},{4,0},{5,1},{6,2},{7,3},{8,4},{9,5},{1... | collective-permute-start | bytes 589832 | tf_op jit(solution)/shard_map/ppermute | solution.py:342
  46.0 6.9 %collective-permute-start.14 = (bf16[32,3072]{1,0:T(8,128)(2,1)S(1)}, bf16[32,3072]{1,0:T(8,128)(2,1)S(1)}, u32[]{:S(2)}, u32[]{:S(2)}) collective-permute-start(bf16[32,3072]{1,0:T(8,128)(2,1)S(1)} %get-tuple-element.54), channel_id=1, source_target_pairs={{0,4},{1,5},{2,6},{3,7},{4,8},{5,9},{6,10},{7,11},{8,12},{9,13},{1... | collective-permute-start | bytes 589832 | tf_op jit(solution)/shard_map/ppermute | solution.py:342
  47.6 7.8 %collective-permute-start.9 = (bf16[32,3072]{1,0:T(8,128)(2,1)S(1)}, bf16[32,3072]{1,0:T(8,128)(2,1)S(1)}, u32[]{:S(2)}, u32[]{:S(2)}) collective-permute-start(bf16[32,3072]{1,0:T(8,128)(2,1)S(1)} %get-tuple-element.48), channel_id=1, source_target_pairs={{0,12},{1,13},{2,14},{3,15},{4,0},{5,1},{6,2},{7,3},{8,4},{9,5},{1... | collective-permute-start | bytes 589832 | tf_op jit(solution)/shard_map/ppermute | solution.py:342
  50.1 11.1 %collective-permute-start.10 = (bf16[32,3072]{1,0:T(8,128)(2,1)S(1)}, bf16[32,3072]{1,0:T(8,128)(2,1)S(1)}, u32[]{:S(2)}, u32[]{:S(2)}) collective-permute-start(bf16[32,3072]{1,0:T(8,128)(2,1)S(1)} %get-tuple-element.49), channel_id=1, source_target_pairs={{0,4},{1,5},{2,6},{3,7},{4,8},{5,9},{6,10},{7,11},{8,12},{9,13},{1... | collective-permute-start | bytes 589832 | tf_op jit(solution)/shard_map/ppermute | solution.py:342
  50.1 11.1 %collective-permute-start.11 = (bf16[32,3072]{1,0:T(8,128)(2,1)S(1)}, bf16[32,3072]{1,0:T(8,128)(2,1)S(1)}, u32[]{:S(2)}, u32[]{:S(2)}) collective-permute-start(bf16[32,3072]{1,0:T(8,128)(2,1)S(1)} %get-tuple-element.50), channel_id=1, source_target_pairs={{0,8},{1,9},{2,10},{3,11},{4,12},{5,13},{6,14},{7,15},{8,0},{9,1},... | collective-permute-start | bytes 589832 | tf_op jit(solution)/shard_map/ppermute | solution.py:342
  53.0 8.2 %collective-permute-start.15 = (bf16[32,3072]{1,0:T(8,128)(2,1)S(1)}, bf16[32,3072]{1,0:T(8,128)(2,1)S(1)}, u32[]{:S(2)}, u32[]{:S(2)}) collective-permute-start(bf16[32,3072]{1,0:T(8,128)(2,1)S(1)} %shard_map.115), channel_id=1, source_target_pairs={{0,2},{1,3},{2,0},{3,1},{4,6},{5,7},{6,4},{7,5},{8,10},{9,11},{10,... | collective-permute-start | bytes 589832 | tf_op jit(solution)/shard_map/ppermute | solution.py:350

commit v5 on v4

--- a/solution.py
+++ b/solution.py
@@ -266,14 +266,13 @@
 
 def coordinates():
     role, x, y = (lax.axis_index(n) for n in ("role", "x", "y"))
-    return jnp.where(role == 0, y, x), jnp.where(role == 0, x, y)
+    first, second = jnp.where(role == 0, y, x), jnp.where(role == 0, x, y)
+    return lax.rem(first + 3, 4), lax.rem(second + 3, 4)
 
 
 def down_body(blocks, splits, own0, sq0, own1, sq1, got0, got1, wd_ref, *rest):
-    outs, (act_ref, got_ref) = rest[: len(splits)], rest[len(splits) :]
-    early = got0.shape[0]
-    got_ref[:early] = got0[...]
-    got_ref[early:] = got1[...]
+    outs, act_ref = rest[: len(splits)], rest[len(splits)]
+    early, late = got0.shape[0], got1.shape[0]
     my_a, my_b = coordinates()
     for n, (jp, jb) in enumerate(blocks):
         for ai in range(2):
@@ -284,7 +283,13 @@
             peer_a = lax.rem(my_b - SHIFTS[jb] + 4, 4)
             peer_p = lax.rem(peer_a // 2 + my_b // 2, 2)
             peer = (peer_p * 8 + peer_b * 2 + lax.rem(peer_a, 2)) * 16
-            got = got_ref[pl.ds(pl.multiple_of(peer, 16), 16)].astype(F32)
+            first = pl.multiple_of(jnp.minimum(peer, early - 16), 16)
+            second = pl.multiple_of(jnp.clip(peer - early, 0, late - 16), 16)
+            got = jnp.where(
+                peer < early,
+                got0[pl.ds(first, 16)].astype(F32),
+                got1[pl.ds(second, 16)].astype(F32),
+            )
             lane = 2 * HIDDEN
             extra = got[:, lane : lane + 1] + got[:, lane + HD // 2 : lane + HD // 2 + 1]
             total = sqs[mine : mine + 16][:, :1] + extra
@@ -350,7 +355,7 @@
     return lax.ppermute(
         value,
         AXES,
-        permutation(lambda r, z, x, y: along_y(2, r, z, x, y) if r == 0 else along_x(2, r, z, x, y)),
+        permutation(lambda r, z, x, y: (r, z, x, y ^ 1) if r == 0 else (r, z, x ^ 1, y)),
     )
 
 
@@ -360,9 +365,9 @@
 
 def exchange(value):
     groups = []
-    for p in (0, 2):
+    for p in (1, 3):
         for o in range(4):
-            pair = [(a, z) for a in (p, p + 1) for z in range(8)]
+            pair = [(a, z) for a in (p, (p + 1) % 4) for z in range(8)]
             groups.append([index_of(0, z, o, a) for a, z in pair])
             groups.append([index_of(1, z, a, o) for a, z in pair])
     return lax.all_to_all(
@@ -449,7 +454,7 @@
             [VMEM_SPEC] * 7,
             flops=2 * rows * HALF * 512,
             nbytes=5_000_000,
-            scratch=[pltpu.VMEM((rows, HIDDEN), BF16), pltpu.VMEM((256, 2 * HIDDEN + HD), BF16)],
+            scratch=[pltpu.VMEM((rows, HIDDEN), BF16)],
         )(own0, sq0, own1, sq1, swapped0, swapped1, w_down[0])
 
     far_terms = down(tuple((1, j) for j in range(4)), (PART,) * 4)

time: 75.8 us -> 74.4 us (0.982)
  starting transfers between devices: 25.3 us -> 22.9 us
  blocking collectives: 31.6 us -> 34 us
  waiting for transfers between devices: 9.3 us -> 7.93 us
    all_to_all x2, blocking collectives: 31.6 us -> 34 us  [exchange(): lax.all_to_all(value, AXES, split_axis=0, concat_axis=0, axis_index_group...]
    ppermute x2, starting transfers between devices: 5.4 us -> 3.5 us  [send_a(): lax.ppermute(value, AXES, permutation(lambda r, z, x, y: (r, z, x, y ^ 1)...]
    ppermute x12, waiting for transfers between devices: 7.84 us -> 6.47 us  [send_b(): lax.ppermute(value, AXES, permutation(lambda r, z, x, y: along_x(s, r, z,...]
where the time goes in v5:
time: 74.4 us; the launch traced here: 74.2 us
  blocking collectives  34 us (46%)
  starting transfers between devices  22.9 us (31%)
  Pallas kernels  9.11 us (12%)
  waiting for transfers between devices  7.93 us (11%)
    all_to_all x2, blocking collectives, exchange(): lax.all_to_all(value, AXES, split_axis=0, concat_axis=0, axis_index_group...  34 us
    ppermute x12, starting transfers between devices, send_b(): lax.ppermute(value, AXES, permutation(lambda r, z, x, y: along_x(s, r, z,...  19.2 us
    ppermute x12, waiting for transfers between devices, send_b(): lax.ppermute(value, AXES, permutation(lambda r, z, x, y: along_x(s, r, z,...  6.47 us
    ppermute x2, starting transfers between devices, send_a(): lax.ppermute(value, AXES, permutation(lambda r, z, x, y: (r, z, x, y ^ 1)...  3.5 us
    pallas_call x1, Pallas kernels, per_device(): call(first_body, partials(5 * PART) + blocks, [VMEM_SPEC] * 6 + [HBM_SPEC...  3.25 us
    pallas_call x1, Pallas kernels, per_device(): call(attend_body, (shape((ROWS, HALF), BF16), shape((2 * EXPERTS, CAP, HA...  1.99 us
    pallas_call x2, Pallas kernels, down(): call(functools.partial(down_body, blocks, splits), [shape((n, HALF), BF16...  1.6 us
  transfers between devices with their start and end apart: 16, of which 6 were waited for; matrix products, arithmetic and copies ran while one was open for 0% of the time, Pallas kernels for 7%

profile of v5, /device:TPU:32, one launch (start us, length us, event | category | flops | bytes accessed | tf_op | source)
XLA Modules:
  0.0 74.2 jit_solution(7736069275588899603)
XLA Ops:
  0.0 2.0 %shard_map.109 = (bf16[4,3072]{1,0:T(4,128)(2,1)S(1)}, bf16[16,2,3072]{2,1,0:T(2,128)(2,1)S(1)}, bf16[16,128]{1,0:T(8,128)(2,1)S(1)}, f32[1,3072]{1,0:T(1,128)S(1)}) custom-call(s32[4]{0:T(128)} %len_hbm.1, s32[2,4]{1,0:T(2,128)} %bitcast.4, f32[4,8]{1,0:T(4,128)} %logit_hbm.1, bf16[4,3072]{1,0:T(4,128)(2,1)} %q_hbm.1, bf16[4,2,512]{2,1,0:T(2,128)(2,1)} %new_hbm.1, ...), custom_call_target="tpu_custom_call" | custom-call | flops 50000000 | bytes 1200000 | tf_op jit(solution)/shard_map/pallas_call | solution.py:382
  2.0 19.2 %all_to_all.10 = bf16[16,2,3072]{2,1,0:T(2,128)(2,1)S(1)} all-to-all(bf16[16,2,3072]{2,1,0:T(2,128)(2,1)S(1)} %get-tuple-element.32), channel_id=1, replica_groups={{1,17,33,49,65,81,97,113,2,18,34,50,66,82,98,114},{132,148,164,180,196,..., dimensions={0} | all-to-all | bytes 393216 | tf_op jit(solution)/shard_map/all_to_all | solution.py:373
  21.3 1.9 %collective-permute-start.3 = (bf16[32,3072]{1,0:T(8,128)(2,1)S(1)}, bf16[32,3072]{1,0:T(8,128)(2,1)S(1)}, u32[]{:S(2)}, u32[]{:S(2)}) collective-permute-start(bf16[32,3072]{1,0:T(8,128)(2,1)S(1)} %reshape.9.after_ref.refs_0_), channel_id=1, source_target_pairs={{0,1},{1,0},{2,3},{3,2},{4,5},{5,4},{6,7},{7,6},{8,9},{9,8},{10,11... | collective-permute-start | bytes 589832 | tf_op jit(solution)/shard_map/ppermute | solution.py:355
  23.3 2.3 %collective-permute-start = (bf16[32,3072]{1,0:T(8,128)(2,1)S(1)}, bf16[32,3072]{1,0:T(8,128)(2,1)S(1)}, u32[]{:S(2)}, u32[]{:S(2)}) collective-permute-start(bf16[32,3072]{1,0:T(8,128)(2,1)S(1)} %reshape.9.after_ref.refs_0_), channel_id=1, source_target_pairs={{0,8},{1,9},{2,10},{3,11},{4,12},{5,13},{6,14},{7,15},{8,0},{9,1},... | collective-permute-start | bytes 589832 | tf_op jit(solution)/shard_map/ppermute | solution.py:347
  25.5 3.2 %collective-permute-start.2 = (bf16[32,3072]{1,0:T(8,128)(2,1)S(1)}, bf16[32,3072]{1,0:T(8,128)(2,1)S(1)}, u32[]{:S(2)}, u32[]{:S(2)}) collective-permute-start(bf16[32,3072]{1,0:T(8,128)(2,1)S(1)} %reshape.9.after_ref.refs_0_), channel_id=1, source_target_pairs={{0,12},{1,13},{2,14},{3,15},{4,0},{5,1},{6,2},{7,3},{8,4},{9,5},{1... | collective-permute-start | bytes 589832 | tf_op jit(solution)/shard_map/ppermute | solution.py:347
  28.8 1.9 %collective-permute-start.4 = (bf16[32,3072]{1,0:T(8,128)(2,1)S(1)}, bf16[32,3072]{1,0:T(8,128)(2,1)S(1)}, u32[]{:S(2)}, u32[]{:S(2)}) collective-permute-start(bf16[32,3072]{1,0:T(8,128)(2,1)S(1)} %collective-permute-done.3.refs_4_), channel_id=1, source_target_pairs={{0,8},{1,9},{2,10},{3,11},{4,12},{5,13},{6,14},{7,15},{8,0},{9,1},... | collective-permute-start | bytes 589832 | tf_op jit(solution)/shard_map/ppermute | solution.py:347
  30.7 3.2 %collective-permute-start.6 = (bf16[32,3072]{1,0:T(8,128)(2,1)S(1)}, bf16[32,3072]{1,0:T(8,128)(2,1)S(1)}, u32[]{:S(2)}, u32[]{:S(2)}) collective-permute-start(bf16[32,3072]{1,0:T(8,128)(2,1)S(1)} %collective-permute-done.3.refs_4_), channel_id=1, source_target_pairs={{0,12},{1,13},{2,14},{3,15},{4,0},{5,1},{6,2},{7,3},{8,4},{9,5},{1... | collective-permute-start | bytes 589832 | tf_op jit(solution)/shard_map/ppermute | solution.py:347
  34.1 3.2 %shard_map.111 = (f32[160,1024]{1,0:T(8,128)S(1)}, f32[160,128]{1,0:T(8,128)S(1)}, bf16[160,1152]{1,0:T(8,128)(2,1)S(1)}, bf16[3072,512]{1,0:T(8,128)(2,1)S(1)}, bf16[3072,512]{1,0:T(8,128)(2,1)S(1)}) custom-call(bf16[32,3072]{1,0:T(8,128)(2,1)S(1)} %reshape.9.after_ref.refs_0_, ...), custom_call_target="tpu_custom_call", output_to_operand_aliasing={{3}: (8, {}), {4}: (9, {})} | custom-call | flops 1006632960 | bytes 20000000 | tf_op jit(solution)/shard_map/pallas_call | solution.py:427
  37.5 0.6 collective-permute-done.5.refs_1_
  38.0 1.2 %shard_map.112 = (f32[96,1024]{1,0:T(8,128)S(1)}, f32[96,128]{1,0:T(8,128)S(1)}, bf16[96,1152]{1,0:T(8,128)(2,1)S(1)}) custom-call(bf16[32,3072]{1,0:T(8,128)(2,1)S(1)} %collective-permute-done.4.refs_0_, bf16[32,3072]{1,0:T(8,128)(2,1)S(1)} %collective-permute-done.5.refs_1_, bf16[32,3072]{1,0:T(8,128)(2,1)S(1)} %collective-permute-done.6.refs_2_, ...), custom_call_target="tpu_custom_call" | custom-call | flops 603979776 | bytes 8000000 | tf_op jit(solution)/shard_map/pallas_call | solution.py:439
  39.4 1.5 %collective-permute-done.8.got1 = bf16[96,1152]{1,0:T(8,128)(2,1)S(1)} collective-permute-done((bf16[96,1152]{1,0:T(8,128)(2,1)S(1)}, bf16[96,1152]{1,0:T(8,128)(2,1)S(1)}, u32[]{:S(2)}, u32[]{:S(2)}) %collective-permute-start.8) | collective-permute-done | bytes 221216 | tf_op jit(solution)/shard_map/ppermute | solution.py:363
  40.8 0.8 %shard_map.114 = (bf16[32,3072]{1,0:T(8,128)(2,1)S(1)}, bf16[32,3072]{1,0:T(8,128)(2,1)S(1)}, bf16[32,3072]{1,0:T(8,128)(2,1)S(1)}, bf16[32,3072]{1,0:T(8,128)(2,1)S(1)}) custom-call(f32[160,1024]{1,0:T(8,128)S(1)} %get-tuple-element.39.own0, f32[160,128]{1,0:T(8,128)S(1)} %get-tuple-element.40.sq0, f32[96,1024]{1,0:T(8,128)S(1)} %get-tuple-element.43.own1, ...), custom_call_target="tpu_custom_call" | custom-call | flops 402653184 | bytes 5000000 | tf_op jit(solution)/shard_map/pallas_call | solution.py:451
  41.6 2.0 %collective-permute-start.12 = (bf16[32,3072]{1,0:T(8,128)(2,1)S(1)}, bf16[32,3072]{1,0:T(8,128)(2,1)S(1)}, u32[]{:S(2)}, u32[]{:S(2)}) collective-permute-start(bf16[32,3072]{1,0:T(8,128)(2,1)S(1)} %get-tuple-element.52), channel_id=1, source_target_pairs={{0,8},{1,9},{2,10},{3,11},{4,12},{5,13},{6,14},{7,15},{8,0},{9,1},... | collective-permute-start | bytes 589832 | tf_op jit(solution)/shard_map/ppermute | solution.py:347
  43.6 1.7 %collective-permute-start.13 = (bf16[32,3072]{1,0:T(8,128)(2,1)S(1)}, bf16[32,3072]{1,0:T(8,128)(2,1)S(1)}, u32[]{:S(2)}, u32[]{:S(2)}) collective-permute-start(bf16[32,3072]{1,0:T(8,128)(2,1)S(1)} %get-tuple-element.53), channel_id=1, source_target_pairs={{0,12},{1,13},{2,14},{3,15},{4,0},{5,1},{6,2},{7,3},{8,4},{9,5},{1... | collective-permute-start | bytes 589832 | tf_op jit(solution)/shard_map/ppermute | solution.py:347
  45.3 0.5 collective-permute-start.14
  45.8 0.8 %shard_map.113 = (bf16[32,3072]{1,0:T(8,128)(2,1)S(1)}, bf16[32,3072]{1,0:T(8,128)(2,1)S(1)}, bf16[32,3072]{1,0:T(8,128)(2,1)S(1)}, bf16[32,3072]{1,0:T(8,128)(2,1)S(1)}) custom-call(f32[160,1024]{1,0:T(8,128)S(1)} %get-tuple-element.39.own0, f32[160,128]{1,0:T(8,128)S(1)} %get-tuple-element.40.sq0, f32[96,1024]{1,0:T(8,128)S(1)} %get-tuple-element.43.own1, ...), custom_call_target="tpu_custom_call" | custom-call | flops 402653184 | bytes 5000000 | tf_op jit(solution)/shard_map/pallas_call | solution.py:451
  46.6 2.8 %collective-permute-start.9 = (bf16[32,3072]{1,0:T(8,128)(2,1)S(1)}, bf16[32,3072]{1,0:T(8,128)(2,1)S(1)}, u32[]{:S(2)}, u32[]{:S(2)}) collective-permute-start(bf16[32,3072]{1,0:T(8,128)(2,1)S(1)} %get-tuple-element.48), channel_id=1, source_target_pairs={{0,12},{1,13},{2,14},{3,15},{4,0},{5,1},{6,2},{7,3},{8,4},{9,5},{1... | collective-permute-start | bytes 589832 | tf_op jit(solution)/shard_map/ppermute | solution.py:347
  49.4 1.6 %collective-permute-start.11 = (bf16[32,3072]{1,0:T(8,128)(2,1)S(1)}, bf16[32,3072]{1,0:T(8,128)(2,1)S(1)}, u32[]{:S(2)}, u32[]{:S(2)}) collective-permute-start(bf16[32,3072]{1,0:T(8,128)(2,1)S(1)} %get-tuple-element.50), channel_id=1, source_target_pairs={{0,8},{1,9},{2,10},{3,11},{4,12},{5,13},{6,14},{7,15},{8,0},{9,1},... | collective-permute-start | bytes 589832 | tf_op jit(solution)/shard_map/ppermute | solution.py:347
  51.0 0.6 collective-permute-done.13.refs_2_
  51.6 0.6 collective-permute-done.14.refs_3_
  52.3 1.6 %collective-permute-start.15 = (bf16[32,3072]{1,0:T(8,128)(2,1)S(1)}, bf16[32,3072]{1,0:T(8,128)(2,1)S(1)}, u32[]{:S(2)}, u32[]{:S(2)}) collective-permute-start(bf16[32,3072]{1,0:T(8,128)(2,1)S(1)} %shard_map.115), channel_id=1, source_target_pairs={{0,1},{1,0},{2,3},{3,2},{4,5},{5,4},{6,7},{7,6},{8,9},{9,8},{10,11... | collective-permute-start | bytes 589832 | tf_op jit(solution)/shard_map/ppermute | solution.py:355
  53.9 4.5 %collective-permute-done.10.refs_2_ = bf16[32,3072]{1,0:T(8,128)(2,1)S(1)} collective-permute-done((bf16[32,3072]{1,0:T(8,128)(2,1)S(1)}, bf16[32,3072]{1,0:T(8,128)(2,1)S(1)}, u32[]{:S(2)}, u32[]{:S(2)}) %collective-permute-start.10) | collective-permute-done | bytes 196640 | tf_op jit(solution)/shard_map/ppermute | solution.py:347
  58.6 14.7 %all_to_all.11 = bf16[16,2,3072]{2,1,0:T(2,128)(2,1)S(1)} all-to-all(bf16[16,2,3072]{2,1,0:T(2,128)(2,1)S(1)} %reshape.10), channel_id=1, replica_groups={{1,17,33,49,65,81,97,113,2,18,34,50,66,82,98,114},{132,148,164,180,196,..., dimensions={0} | all-to-all | bytes 393216 | tf_op jit(solution)/shard_map/all_to_all | solution.py:373
  73.5 0.8 %shard_map.117 = bf16[4,3072]{1,0:T(4,128)(2,1)} custom-call(bf16[16,128]{1,0:T(8,128)(2,1)S(1)} %get-tuple-element.30.comb_ref, bf16[4,3072]{1,0:T(4,128)(2,1)S(1)} %get-tuple-element.31.hidden_ref, bf16[32,3072]{1,0:T(8,128)(2,1)S(1)} %reshape.11.back_ref), custom_call_target="tpu_custom_call" | custom-call | flops 100000 | bytes 150000 | tf_op jit(solution)/shard_map/pallas_call | solution.py:476
  (24 shorter events, 0.9 us)
Async XLA Ops:
  21.3 7.4 %collective-permute-start.3 = (bf16[32,3072]{1,0:T(8,128)(2,1)S(1)}, bf16[32,3072]{1,0:T(8,128)(2,1)S(1)}, u32[]{:S(2)}, u32[]{:S(2)}) collective-permute-start(bf16[32,3072]{1,0:T(8,128)(2,1)S(1)} %reshape.9.after_ref.refs_0_), channel_id=1, source_target_pairs={{0,1},{1,0},{2,3},{3,2},{4,5},{5,4},{6,7},{7,6},{8,9},{9,8},{10,11... | collective-permute-start | bytes 589832 | tf_op jit(solution)/shard_map/ppermute | solution.py:355
  23.3 7.4 %collective-permute-start = (bf16[32,3072]{1,0:T(8,128)(2,1)S(1)}, bf16[32,3072]{1,0:T(8,128)(2,1)S(1)}, u32[]{:S(2)}, u32[]{:S(2)}) collective-permute-start(bf16[32,3072]{1,0:T(8,128)(2,1)S(1)} %reshape.9.after_ref.refs_0_), channel_id=1, source_target_pairs={{0,8},{1,9},{2,10},{3,11},{4,12},{5,13},{6,14},{7,15},{8,0},{9,1},... | collective-permute-start | bytes 589832 | tf_op jit(solution)/shard_map/ppermute | solution.py:347
  25.5 8.4 %collective-permute-start.1 = (bf16[32,3072]{1,0:T(8,128)(2,1)S(1)}, bf16[32,3072]{1,0:T(8,128)(2,1)S(1)}, u32[]{:S(2)}, u32[]{:S(2)}) collective-permute-start(bf16[32,3072]{1,0:T(8,128)(2,1)S(1)} %reshape.9.after_ref.refs_0_), channel_id=1, source_target_pairs={{0,4},{1,5},{2,6},{3,7},{4,8},{5,9},{6,10},{7,11},{8,12},{9,13},{1... | collective-permute-start | bytes 589832 | tf_op jit(solution)/shard_map/ppermute | solution.py:347
  25.5 8.6 %collective-permute-start.2 = (bf16[32,3072]{1,0:T(8,128)(2,1)S(1)}, bf16[32,3072]{1,0:T(8,128)(2,1)S(1)}, u32[]{:S(2)}, u32[]{:S(2)}) collective-permute-start(bf16[32,3072]{1,0:T(8,128)(2,1)S(1)} %reshape.9.after_ref.refs_0_), channel_id=1, source_target_pairs={{0,12},{1,13},{2,14},{3,15},{4,0},{5,1},{6,2},{7,3},{8,4},{9,5},{1... | collective-permute-start | bytes 589832 | tf_op jit(solution)/shard_map/ppermute | solution.py:347
  28.8 8.7 %collective-permute-start.4 = (bf16[32,3072]{1,0:T(8,128)(2,1)S(1)}, bf16[32,3072]{1,0:T(8,128)(2,1)S(1)}, u32[]{:S(2)}, u32[]{:S(2)}) collective-permute-start(bf16[32,3072]{1,0:T(8,128)(2,1)S(1)} %collective-permute-done.3.refs_4_), channel_id=1, source_target_pairs={{0,8},{1,9},{2,10},{3,11},{4,12},{5,13},{6,14},{7,15},{8,0},{9,1},... | collective-permute-start | bytes 589832 | tf_op jit(solution)/shard_map/ppermute | solution.py:347
  30.7 7.4 %collective-permute-start.5 = (bf16[32,3072]{1,0:T(8,128)(2,1)S(1)}, bf16[32,3072]{1,0:T(8,128)(2,1)S(1)}, u32[]{:S(2)}, u32[]{:S(2)}) collective-permute-start(bf16[32,3072]{1,0:T(8,128)(2,1)S(1)} %collective-permute-done.3.refs_4_), channel_id=1, source_target_pairs={{0,4},{1,5},{2,6},{3,7},{4,8},{5,9},{6,10},{7,11},{8,12},{9,13},{1... | collective-permute-start | bytes 589832 | tf_op jit(solution)/shard_map/ppermute | solution.py:347
  30.7 7.4 %collective-permute-start.6 = (bf16[32,3072]{1,0:T(8,128)(2,1)S(1)}, bf16[32,3072]{1,0:T(8,128)(2,1)S(1)}, u32[]{:S(2)}, u32[]{:S(2)}) collective-permute-start(bf16[32,3072]{1,0:T(8,128)(2,1)S(1)} %collective-permute-done.3.refs_4_), channel_id=1, source_target_pairs={{0,12},{1,13},{2,14},{3,15},{4,0},{5,1},{6,2},{7,3},{8,4},{9,5},{1... | collective-permute-start | bytes 589832 | tf_op jit(solution)/shard_map/ppermute | solution.py:347
  37.3 2.0 %collective-permute-start.7 = (bf16[160,1152]{1,0:T(8,128)(2,1)S(1)}, bf16[160,1152]{1,0:T(8,128)(2,1)S(1)}, u32[]{:S(2)}, u32[]{:S(2)}) collective-permute-start(bf16[160,1152]{1,0:T(8,128)(2,1)S(1)} %get-tuple-element.45), channel_id=1, source_target_pairs={{0,128},{128,0},{1,129},{129,1},{2,130},{130,2},{3,131},{131,3},{4... | collective-permute-start | bytes 1105928 | tf_op jit(solution)/shard_map/ppermute | solution.py:363
  38.0 2.8 %copy-start = (bf16[1,512,3072]{2,1,0:T(8,128)(2,1)S(1)}, bf16[1,512,3072]{2,1,0:T(8,128)(2,1)}, u32[]{:S(2)}) copy-start(bf16[1,512,3072]{2,1,0:T(8,128)(2,1)} %param.21) | copy-start | bytes 9437188
  39.3 1.6 %collective-permute-start.8 = (bf16[96,1152]{1,0:T(8,128)(2,1)S(1)}, bf16[96,1152]{1,0:T(8,128)(2,1)S(1)}, u32[]{:S(2)}, u32[]{:S(2)}) collective-permute-start(bf16[96,1152]{1,0:T(8,128)(2,1)S(1)} %get-tuple-element.46), channel_id=1, source_target_pairs={{0,128},{128,0},{1,129},{129,1},{2,130},{130,2},{3,131},{131,3},{4... | collective-permute-start | bytes 663560 | tf_op jit(solution)/shard_map/ppermute | solution.py:363
  41.6 7.8 %collective-permute-start.12 = (bf16[32,3072]{1,0:T(8,128)(2,1)S(1)}, bf16[32,3072]{1,0:T(8,128)(2,1)S(1)}, u32[]{:S(2)}, u32[]{:S(2)}) collective-permute-start(bf16[32,3072]{1,0:T(8,128)(2,1)S(1)} %get-tuple-element.52), channel_id=1, source_target_pairs={{0,8},{1,9},{2,10},{3,11},{4,12},{5,13},{6,14},{7,15},{8,0},{9,1},... | collective-permute-start | bytes 589832 | tf_op jit(solution)/shard_map/ppermute | solution.py:347
  43.6 8.0 %collective-permute-start.13 = (bf16[32,3072]{1,0:T(8,128)(2,1)S(1)}, bf16[32,3072]{1,0:T(8,128)(2,1)S(1)}, u32[]{:S(2)}, u32[]{:S(2)}) collective-permute-start(bf16[32,3072]{1,0:T(8,128)(2,1)S(1)} %get-tuple-element.53), channel_id=1, source_target_pairs={{0,12},{1,13},{2,14},{3,15},{4,0},{5,1},{6,2},{7,3},{8,4},{9,5},{1... | collective-permute-start | bytes 589832 | tf_op jit(solution)/shard_map/ppermute | solution.py:347
  45.3 6.9 %collective-permute-start.14 = (bf16[32,3072]{1,0:T(8,128)(2,1)S(1)}, bf16[32,3072]{1,0:T(8,128)(2,1)S(1)}, u32[]{:S(2)}, u32[]{:S(2)}) collective-permute-start(bf16[32,3072]{1,0:T(8,128)(2,1)S(1)} %get-tuple-element.54), channel_id=1, source_target_pairs={{0,4},{1,5},{2,6},{3,7},{4,8},{5,9},{6,10},{7,11},{8,12},{9,13},{1... | collective-permute-start | bytes 589832 | tf_op jit(solution)/shard_map/ppermute | solution.py:347
  46.6 7.3 %collective-permute-start.9 = (bf16[32,3072]{1,0:T(8,128)(2,1)S(1)}, bf16[32,3072]{1,0:T(8,128)(2,1)S(1)}, u32[]{:S(2)}, u32[]{:S(2)}) collective-permute-start(bf16[32,3072]{1,0:T(8,128)(2,1)S(1)} %get-tuple-element.48), channel_id=1, source_target_pairs={{0,12},{1,13},{2,14},{3,15},{4,0},{5,1},{6,2},{7,3},{8,4},{9,5},{1... | collective-permute-start | bytes 589832 | tf_op jit(solution)/shard_map/ppermute | solution.py:347
  49.4 9.0 %collective-permute-start.10 = (bf16[32,3072]{1,0:T(8,128)(2,1)S(1)}, bf16[32,3072]{1,0:T(8,128)(2,1)S(1)}, u32[]{:S(2)}, u32[]{:S(2)}) collective-permute-start(bf16[32,3072]{1,0:T(8,128)(2,1)S(1)} %get-tuple-element.49), channel_id=1, source_target_pairs={{0,4},{1,5},{2,6},{3,7},{4,8},{5,9},{6,10},{7,11},{8,12},{9,13},{1... | collective-permute-start | bytes 589832 | tf_op jit(solution)/shard_map/ppermute | solution.py:347
  49.4 9.0 %collective-permute-start.11 = (bf16[32,3072]{1,0:T(8,128)(2,1)S(1)}, bf16[32,3072]{1,0:T(8,128)(2,1)S(1)}, u32[]{:S(2)}, u32[]{:S(2)}) collective-permute-start(bf16[32,3072]{1,0:T(8,128)(2,1)S(1)} %get-tuple-element.50), channel_id=1, source_target_pairs={{0,8},{1,9},{2,10},{3,11},{4,12},{5,13},{6,14},{7,15},{8,0},{9,1},... | collective-permute-start | bytes 589832 | tf_op jit(solution)/shard_map/ppermute | solution.py:347
  52.3 6.1 %collective-permute-start.15 = (bf16[32,3072]{1,0:T(8,128)(2,1)S(1)}, bf16[32,3072]{1,0:T(8,128)(2,1)S(1)}, u32[]{:S(2)}, u32[]{:S(2)}) collective-permute-start(bf16[32,3072]{1,0:T(8,128)(2,1)S(1)} %shard_map.115), channel_id=1, source_target_pairs={{0,1},{1,0},{2,3},{3,2},{4,5},{5,4},{6,7},{7,6},{8,9},{9,8},{10,11... | collective-permute-start | bytes 589832 | tf_op jit(solution)/shard_map/ppermute | solution.py:355

commit v6 on v5

--- a/solution.py
+++ b/solution.py
@@ -195,8 +195,9 @@
             got = jnp.dot(x, w_ref[rows], preferred_element_type=F32)
             sums[i] = got if sums[i] is None else sums[i] + got
     for i, at in enumerate((0, HIDDEN)):
-        own_ref[:, at : at + HIDDEN] = sums[i]
-        send_ref[:, at : at + HIDDEN] = sums[i].astype(BF16)
+        kept = sums[i][: own_ref.shape[0]]
+        own_ref[:, at : at + HIDDEN] = kept
+        send_ref[:, at : at + HIDDEN] = kept.astype(BF16)
     for n in range(len(xs)):
         put_squares(accs[n], n * PART, sq_ref, send_ref)
 
@@ -261,6 +262,7 @@
 def second_body(*refs):
     xs, (gain_ref, wg_ref, wu_ref) = refs[:3], refs[3:6]
     own_ref, sq_ref, send_ref, scaled_ref = refs[6:]
+    scaled_ref[3 * PART :] = jnp.zeros((PART, HALF), BF16)
     gate_up(xs, gain_ref, wg_ref, wu_ref, own_ref, sq_ref, send_ref, scaled_ref, 2 * CHUNK)
 
 
@@ -442,7 +444,7 @@
         [VMEM_SPEC] * 6,
         flops=2 * 3 * PART * HALF * 1024,
         nbytes=8_000_000,
-        scratch=[pltpu.VMEM((3 * PART, HALF), BF16)],
+        scratch=[pltpu.VMEM((4 * PART, HALF), BF16)],
     )(*far_b, gain, wg, wu)
     swapped0, swapped1 = swap(send0), swap(send1)
 

time: 74.4 us -> 74.2 us (level)
  no operation moved by 1% of the time
where the time goes in v6:
time: 74.2 us; the launch traced here: 74.1 us
  blocking collectives  33.9 us (46%)
  starting transfers between devices  22.8 us (31%)
  Pallas kernels  8.98 us (12%)
  waiting for transfers between devices  7.94 us (11%)
    all_to_all x2, blocking collectives, exchange(): lax.all_to_all(value, AXES, split_axis=0, concat_axis=0, axis_index_group...  33.9 us
    ppermute x12, starting transfers between devices, send_b(): lax.ppermute(value, AXES, permutation(lambda r, z, x, y: along_x(s, r, z,...  19.2 us
    ppermute x12, waiting for transfers between devices, send_b(): lax.ppermute(value, AXES, permutation(lambda r, z, x, y: along_x(s, r, z,...  6.48 us
    ppermute x2, starting transfers between devices, send_a(): lax.ppermute(value, AXES, permutation(lambda r, z, x, y: (r, z, x, y ^ 1)...  3.49 us
    pallas_call x1, Pallas kernels, per_device(): call(first_body, partials(5 * PART) + blocks, [VMEM_SPEC] * 6 + [HBM_SPEC...  3.25 us
    pallas_call x1, Pallas kernels, per_device(): call(attend_body, (shape((ROWS, HALF), BF16), shape((2 * EXPERTS, CAP, HA...  1.99 us
    pallas_call x2, Pallas kernels, down(): call(functools.partial(down_body, blocks, splits), [shape((n, HALF), BF16...  1.6 us
  transfers between devices with their start and end apart: 16, of which 6 were waited for; matrix products, arithmetic and copies ran while one was open for 0% of the time, Pallas kernels for 7%

profile of v6, /device:TPU:32, one launch (start us, length us, event | category | flops | bytes accessed | tf_op | source)
XLA Modules:
  0.0 74.1 jit_solution(17905006609823324442)
XLA Ops:
  0.0 2.0 %shard_map.109 = (bf16[4,3072]{1,0:T(4,128)(2,1)S(1)}, bf16[16,2,3072]{2,1,0:T(2,128)(2,1)S(1)}, bf16[16,128]{1,0:T(8,128)(2,1)S(1)}, f32[1,3072]{1,0:T(1,128)S(1)}) custom-call(s32[4]{0:T(128)} %len_hbm.1, s32[2,4]{1,0:T(2,128)} %bitcast.4, f32[4,8]{1,0:T(4,128)} %logit_hbm.1, bf16[4,3072]{1,0:T(4,128)(2,1)} %q_hbm.1, bf16[4,2,512]{2,1,0:T(2,128)(2,1)} %new_hbm.1, ...), custom_call_target="tpu_custom_call" | custom-call | flops 50000000 | bytes 1200000 | tf_op jit(solution)/shard_map/pallas_call | solution.py:384
  2.0 19.2 %all_to_all.10 = bf16[16,2,3072]{2,1,0:T(2,128)(2,1)S(1)} all-to-all(bf16[16,2,3072]{2,1,0:T(2,128)(2,1)S(1)} %get-tuple-element.32), channel_id=1, replica_groups={{1,17,33,49,65,81,97,113,2,18,34,50,66,82,98,114},{132,148,164,180,196,..., dimensions={0} | all-to-all | bytes 393216 | tf_op jit(solution)/shard_map/all_to_all | solution.py:375
  21.3 1.9 %collective-permute-start.3 = (bf16[32,3072]{1,0:T(8,128)(2,1)S(1)}, bf16[32,3072]{1,0:T(8,128)(2,1)S(1)}, u32[]{:S(2)}, u32[]{:S(2)}) collective-permute-start(bf16[32,3072]{1,0:T(8,128)(2,1)S(1)} %reshape.9.after_ref.refs_0_), channel_id=1, source_target_pairs={{0,1},{1,0},{2,3},{3,2},{4,5},{5,4},{6,7},{7,6},{8,9},{9,8},{10,11... | collective-permute-start | bytes 589832 | tf_op jit(solution)/shard_map/ppermute | solution.py:357
  23.3 2.3 %collective-permute-start = (bf16[32,3072]{1,0:T(8,128)(2,1)S(1)}, bf16[32,3072]{1,0:T(8,128)(2,1)S(1)}, u32[]{:S(2)}, u32[]{:S(2)}) collective-permute-start(bf16[32,3072]{1,0:T(8,128)(2,1)S(1)} %reshape.9.after_ref.refs_0_), channel_id=1, source_target_pairs={{0,8},{1,9},{2,10},{3,11},{4,12},{5,13},{6,14},{7,15},{8,0},{9,1},... | collective-permute-start | bytes 589832 | tf_op jit(solution)/shard_map/ppermute | solution.py:349
  25.5 3.2 %collective-permute-start.2 = (bf16[32,3072]{1,0:T(8,128)(2,1)S(1)}, bf16[32,3072]{1,0:T(8,128)(2,1)S(1)}, u32[]{:S(2)}, u32[]{:S(2)}) collective-permute-start(bf16[32,3072]{1,0:T(8,128)(2,1)S(1)} %reshape.9.after_ref.refs_0_), channel_id=1, source_target_pairs={{0,12},{1,13},{2,14},{3,15},{4,0},{5,1},{6,2},{7,3},{8,4},{9,5},{1... | collective-permute-start | bytes 589832 | tf_op jit(solution)/shard_map/ppermute | solution.py:349
  28.8 1.9 %collective-permute-start.4 = (bf16[32,3072]{1,0:T(8,128)(2,1)S(1)}, bf16[32,3072]{1,0:T(8,128)(2,1)S(1)}, u32[]{:S(2)}, u32[]{:S(2)}) collective-permute-start(bf16[32,3072]{1,0:T(8,128)(2,1)S(1)} %collective-permute-done.3.refs_4_), channel_id=1, source_target_pairs={{0,8},{1,9},{2,10},{3,11},{4,12},{5,13},{6,14},{7,15},{8,0},{9,1},... | collective-permute-start | bytes 589832 | tf_op jit(solution)/shard_map/ppermute | solution.py:349
  30.7 3.2 %collective-permute-start.6 = (bf16[32,3072]{1,0:T(8,128)(2,1)S(1)}, bf16[32,3072]{1,0:T(8,128)(2,1)S(1)}, u32[]{:S(2)}, u32[]{:S(2)}) collective-permute-start(bf16[32,3072]{1,0:T(8,128)(2,1)S(1)} %collective-permute-done.3.refs_4_), channel_id=1, source_target_pairs={{0,12},{1,13},{2,14},{3,15},{4,0},{5,1},{6,2},{7,3},{8,4},{9,5},{1... | collective-permute-start | bytes 589832 | tf_op jit(solution)/shard_map/ppermute | solution.py:349
  34.1 3.2 %shard_map.111 = (f32[160,1024]{1,0:T(8,128)S(1)}, f32[160,128]{1,0:T(8,128)S(1)}, bf16[160,1152]{1,0:T(8,128)(2,1)S(1)}, bf16[3072,512]{1,0:T(8,128)(2,1)S(1)}, bf16[3072,512]{1,0:T(8,128)(2,1)S(1)}) custom-call(bf16[32,3072]{1,0:T(8,128)(2,1)S(1)} %reshape.9.after_ref.refs_0_, ...), custom_call_target="tpu_custom_call", output_to_operand_aliasing={{3}: (8, {}), {4}: (9, {})} | custom-call | flops 1006632960 | bytes 20000000 | tf_op jit(solution)/shard_map/pallas_call | solution.py:429
  37.5 0.6 collective-permute-done.5.refs_1_
  38.0 1.1 %shard_map.112 = (f32[96,1024]{1,0:T(8,128)S(1)}, f32[96,128]{1,0:T(8,128)S(1)}, bf16[96,1152]{1,0:T(8,128)(2,1)S(1)}) custom-call(bf16[32,3072]{1,0:T(8,128)(2,1)S(1)} %collective-permute-done.4.refs_0_, bf16[32,3072]{1,0:T(8,128)(2,1)S(1)} %collective-permute-done.5.refs_1_, bf16[32,3072]{1,0:T(8,128)(2,1)S(1)} %collective-permute-done.6.refs_2_, ...), custom_call_target="tpu_custom_call" | custom-call | flops 603979776 | bytes 8000000 | tf_op jit(solution)/shard_map/pallas_call | solution.py:441
  39.2 1.5 %collective-permute-done.8.got1 = bf16[96,1152]{1,0:T(8,128)(2,1)S(1)} collective-permute-done((bf16[96,1152]{1,0:T(8,128)(2,1)S(1)}, bf16[96,1152]{1,0:T(8,128)(2,1)S(1)}, u32[]{:S(2)}, u32[]{:S(2)}) %collective-permute-start.8) | collective-permute-done | bytes 221216 | tf_op jit(solution)/shard_map/ppermute | solution.py:365
  40.7 0.8 %shard_map.114 = (bf16[32,3072]{1,0:T(8,128)(2,1)S(1)}, bf16[32,3072]{1,0:T(8,128)(2,1)S(1)}, bf16[32,3072]{1,0:T(8,128)(2,1)S(1)}, bf16[32,3072]{1,0:T(8,128)(2,1)S(1)}) custom-call(f32[160,1024]{1,0:T(8,128)S(1)} %get-tuple-element.39.own0, f32[160,128]{1,0:T(8,128)S(1)} %get-tuple-element.40.sq0, f32[96,1024]{1,0:T(8,128)S(1)} %get-tuple-element.43.own1, ...), custom_call_target="tpu_custom_call" | custom-call | flops 402653184 | bytes 5000000 | tf_op jit(solution)/shard_map/pallas_call | solution.py:453
  41.5 2.0 %collective-permute-start.12 = (bf16[32,3072]{1,0:T(8,128)(2,1)S(1)}, bf16[32,3072]{1,0:T(8,128)(2,1)S(1)}, u32[]{:S(2)}, u32[]{:S(2)}) collective-permute-start(bf16[32,3072]{1,0:T(8,128)(2,1)S(1)} %get-tuple-element.52), channel_id=1, source_target_pairs={{0,8},{1,9},{2,10},{3,11},{4,12},{5,13},{6,14},{7,15},{8,0},{9,1},... | collective-permute-start | bytes 589832 | tf_op jit(solution)/shard_map/ppermute | solution.py:349
  43.5 1.7 %collective-permute-start.13 = (bf16[32,3072]{1,0:T(8,128)(2,1)S(1)}, bf16[32,3072]{1,0:T(8,128)(2,1)S(1)}, u32[]{:S(2)}, u32[]{:S(2)}) collective-permute-start(bf16[32,3072]{1,0:T(8,128)(2,1)S(1)} %get-tuple-element.53), channel_id=1, source_target_pairs={{0,12},{1,13},{2,14},{3,15},{4,0},{5,1},{6,2},{7,3},{8,4},{9,5},{1... | collective-permute-start | bytes 589832 | tf_op jit(solution)/shard_map/ppermute | solution.py:349
  45.2 0.5 collective-permute-start.14
  45.7 0.8 %shard_map.113 = (bf16[32,3072]{1,0:T(8,128)(2,1)S(1)}, bf16[32,3072]{1,0:T(8,128)(2,1)S(1)}, bf16[32,3072]{1,0:T(8,128)(2,1)S(1)}, bf16[32,3072]{1,0:T(8,128)(2,1)S(1)}) custom-call(f32[160,1024]{1,0:T(8,128)S(1)} %get-tuple-element.39.own0, f32[160,128]{1,0:T(8,128)S(1)} %get-tuple-element.40.sq0, f32[96,1024]{1,0:T(8,128)S(1)} %get-tuple-element.43.own1, ...), custom_call_target="tpu_custom_call" | custom-call | flops 402653184 | bytes 5000000 | tf_op jit(solution)/shard_map/pallas_call | solution.py:453
  46.5 2.8 %collective-permute-start.9 = (bf16[32,3072]{1,0:T(8,128)(2,1)S(1)}, bf16[32,3072]{1,0:T(8,128)(2,1)S(1)}, u32[]{:S(2)}, u32[]{:S(2)}) collective-permute-start(bf16[32,3072]{1,0:T(8,128)(2,1)S(1)} %get-tuple-element.48), channel_id=1, source_target_pairs={{0,12},{1,13},{2,14},{3,15},{4,0},{5,1},{6,2},{7,3},{8,4},{9,5},{1... | collective-permute-start | bytes 589832 | tf_op jit(solution)/shard_map/ppermute | solution.py:349
  49.3 1.6 %collective-permute-start.11 = (bf16[32,3072]{1,0:T(8,128)(2,1)S(1)}, bf16[32,3072]{1,0:T(8,128)(2,1)S(1)}, u32[]{:S(2)}, u32[]{:S(2)}) collective-permute-start(bf16[32,3072]{1,0:T(8,128)(2,1)S(1)} %get-tuple-element.50), channel_id=1, source_target_pairs={{0,8},{1,9},{2,10},{3,11},{4,12},{5,13},{6,14},{7,15},{8,0},{9,1},... | collective-permute-start | bytes 589832 | tf_op jit(solution)/shard_map/ppermute | solution.py:349
  50.9 0.6 collective-permute-done.13.refs_2_
  51.4 0.6 collective-permute-done.14.refs_3_
  52.2 1.6 %collective-permute-start.15 = (bf16[32,3072]{1,0:T(8,128)(2,1)S(1)}, bf16[32,3072]{1,0:T(8,128)(2,1)S(1)}, u32[]{:S(2)}, u32[]{:S(2)}) collective-permute-start(bf16[32,3072]{1,0:T(8,128)(2,1)S(1)} %shard_map.115), channel_id=1, source_target_pairs={{0,1},{1,0},{2,3},{3,2},{4,5},{5,4},{6,7},{7,6},{8,9},{9,8},{10,11... | collective-permute-start | bytes 589832 | tf_op jit(solution)/shard_map/ppermute | solution.py:357
  53.8 4.5 %collective-permute-done.10.refs_2_ = bf16[32,3072]{1,0:T(8,128)(2,1)S(1)} collective-permute-done((bf16[32,3072]{1,0:T(8,128)(2,1)S(1)}, bf16[32,3072]{1,0:T(8,128)(2,1)S(1)}, u32[]{:S(2)}, u32[]{:S(2)}) %collective-permute-start.10) | collective-permute-done | bytes 196640 | tf_op jit(solution)/shard_map/ppermute | solution.py:349
  58.5 14.7 %all_to_all.11 = bf16[16,2,3072]{2,1,0:T(2,128)(2,1)S(1)} all-to-all(bf16[16,2,3072]{2,1,0:T(2,128)(2,1)S(1)} %reshape.10), channel_id=1, replica_groups={{1,17,33,49,65,81,97,113,2,18,34,50,66,82,98,114},{132,148,164,180,196,..., dimensions={0} | all-to-all | bytes 393216 | tf_op jit(solution)/shard_map/all_to_all | solution.py:375
  73.3 0.8 %shard_map.117 = bf16[4,3072]{1,0:T(4,128)(2,1)} custom-call(bf16[16,128]{1,0:T(8,128)(2,1)S(1)} %get-tuple-element.30.comb_ref, bf16[4,3072]{1,0:T(4,128)(2,1)S(1)} %get-tuple-element.31.hidden_ref, bf16[32,3072]{1,0:T(8,128)(2,1)S(1)} %reshape.11.back_ref), custom_call_target="tpu_custom_call" | custom-call | flops 100000 | bytes 150000 | tf_op jit(solution)/shard_map/pallas_call | solution.py:478
  (24 shorter events, 0.9 us)
Async XLA Ops:
  21.3 7.4 %collective-permute-start.3 = (bf16[32,3072]{1,0:T(8,128)(2,1)S(1)}, bf16[32,3072]{1,0:T(8,128)(2,1)S(1)}, u32[]{:S(2)}, u32[]{:S(2)}) collective-permute-start(bf16[32,3072]{1,0:T(8,128)(2,1)S(1)} %reshape.9.after_ref.refs_0_), channel_id=1, source_target_pairs={{0,1},{1,0},{2,3},{3,2},{4,5},{5,4},{6,7},{7,6},{8,9},{9,8},{10,11... | collective-permute-start | bytes 589832 | tf_op jit(solution)/shard_map/ppermute | solution.py:357
  23.3 7.4 %collective-permute-start = (bf16[32,3072]{1,0:T(8,128)(2,1)S(1)}, bf16[32,3072]{1,0:T(8,128)(2,1)S(1)}, u32[]{:S(2)}, u32[]{:S(2)}) collective-permute-start(bf16[32,3072]{1,0:T(8,128)(2,1)S(1)} %reshape.9.after_ref.refs_0_), channel_id=1, source_target_pairs={{0,8},{1,9},{2,10},{3,11},{4,12},{5,13},{6,14},{7,15},{8,0},{9,1},... | collective-permute-start | bytes 589832 | tf_op jit(solution)/shard_map/ppermute | solution.py:349
  25.5 8.4 %collective-permute-start.1 = (bf16[32,3072]{1,0:T(8,128)(2,1)S(1)}, bf16[32,3072]{1,0:T(8,128)(2,1)S(1)}, u32[]{:S(2)}, u32[]{:S(2)}) collective-permute-start(bf16[32,3072]{1,0:T(8,128)(2,1)S(1)} %reshape.9.after_ref.refs_0_), channel_id=1, source_target_pairs={{0,4},{1,5},{2,6},{3,7},{4,8},{5,9},{6,10},{7,11},{8,12},{9,13},{1... | collective-permute-start | bytes 589832 | tf_op jit(solution)/shard_map/ppermute | solution.py:349
  25.5 8.6 %collective-permute-start.2 = (bf16[32,3072]{1,0:T(8,128)(2,1)S(1)}, bf16[32,3072]{1,0:T(8,128)(2,1)S(1)}, u32[]{:S(2)}, u32[]{:S(2)}) collective-permute-start(bf16[32,3072]{1,0:T(8,128)(2,1)S(1)} %reshape.9.after_ref.refs_0_), channel_id=1, source_target_pairs={{0,12},{1,13},{2,14},{3,15},{4,0},{5,1},{6,2},{7,3},{8,4},{9,5},{1... | collective-permute-start | bytes 589832 | tf_op jit(solution)/shard_map/ppermute | solution.py:349
  28.8 8.7 %collective-permute-start.4 = (bf16[32,3072]{1,0:T(8,128)(2,1)S(1)}, bf16[32,3072]{1,0:T(8,128)(2,1)S(1)}, u32[]{:S(2)}, u32[]{:S(2)}) collective-permute-start(bf16[32,3072]{1,0:T(8,128)(2,1)S(1)} %collective-permute-done.3.refs_4_), channel_id=1, source_target_pairs={{0,8},{1,9},{2,10},{3,11},{4,12},{5,13},{6,14},{7,15},{8,0},{9,1},... | collective-permute-start | bytes 589832 | tf_op jit(solution)/shard_map/ppermute | solution.py:349
  30.7 7.4 %collective-permute-start.5 = (bf16[32,3072]{1,0:T(8,128)(2,1)S(1)}, bf16[32,3072]{1,0:T(8,128)(2,1)S(1)}, u32[]{:S(2)}, u32[]{:S(2)}) collective-permute-start(bf16[32,3072]{1,0:T(8,128)(2,1)S(1)} %collective-permute-done.3.refs_4_), channel_id=1, source_target_pairs={{0,4},{1,5},{2,6},{3,7},{4,8},{5,9},{6,10},{7,11},{8,12},{9,13},{1... | collective-permute-start | bytes 589832 | tf_op jit(solution)/shard_map/ppermute | solution.py:349
  30.7 7.4 %collective-permute-start.6 = (bf16[32,3072]{1,0:T(8,128)(2,1)S(1)}, bf16[32,3072]{1,0:T(8,128)(2,1)S(1)}, u32[]{:S(2)}, u32[]{:S(2)}) collective-permute-start(bf16[32,3072]{1,0:T(8,128)(2,1)S(1)} %collective-permute-done.3.refs_4_), channel_id=1, source_target_pairs={{0,12},{1,13},{2,14},{3,15},{4,0},{5,1},{6,2},{7,3},{8,4},{9,5},{1... | collective-permute-start | bytes 589832 | tf_op jit(solution)/shard_map/ppermute | solution.py:349
  37.3 1.9 %collective-permute-start.7 = (bf16[160,1152]{1,0:T(8,128)(2,1)S(1)}, bf16[160,1152]{1,0:T(8,128)(2,1)S(1)}, u32[]{:S(2)}, u32[]{:S(2)}) collective-permute-start(bf16[160,1152]{1,0:T(8,128)(2,1)S(1)} %get-tuple-element.45), channel_id=1, source_target_pairs={{0,128},{128,0},{1,129},{129,1},{2,130},{130,2},{3,131},{131,3},{4... | collective-permute-start | bytes 1105928 | tf_op jit(solution)/shard_map/ppermute | solution.py:365
  38.0 2.7 %copy-start = (bf16[1,512,3072]{2,1,0:T(8,128)(2,1)S(1)}, bf16[1,512,3072]{2,1,0:T(8,128)(2,1)}, u32[]{:S(2)}) copy-start(bf16[1,512,3072]{2,1,0:T(8,128)(2,1)} %param.21) | copy-start | bytes 9437188
  39.1 1.6 %collective-permute-start.8 = (bf16[96,1152]{1,0:T(8,128)(2,1)S(1)}, bf16[96,1152]{1,0:T(8,128)(2,1)S(1)}, u32[]{:S(2)}, u32[]{:S(2)}) collective-permute-start(bf16[96,1152]{1,0:T(8,128)(2,1)S(1)} %get-tuple-element.46), channel_id=1, source_target_pairs={{0,128},{128,0},{1,129},{129,1},{2,130},{130,2},{3,131},{131,3},{4... | collective-permute-start | bytes 663560 | tf_op jit(solution)/shard_map/ppermute | solution.py:365
  41.5 7.8 %collective-permute-start.12 = (bf16[32,3072]{1,0:T(8,128)(2,1)S(1)}, bf16[32,3072]{1,0:T(8,128)(2,1)S(1)}, u32[]{:S(2)}, u32[]{:S(2)}) collective-permute-start(bf16[32,3072]{1,0:T(8,128)(2,1)S(1)} %get-tuple-element.52), channel_id=1, source_target_pairs={{0,8},{1,9},{2,10},{3,11},{4,12},{5,13},{6,14},{7,15},{8,0},{9,1},... | collective-permute-start | bytes 589832 | tf_op jit(solution)/shard_map/ppermute | solution.py:349
  43.5 7.9 %collective-permute-start.13 = (bf16[32,3072]{1,0:T(8,128)(2,1)S(1)}, bf16[32,3072]{1,0:T(8,128)(2,1)S(1)}, u32[]{:S(2)}, u32[]{:S(2)}) collective-permute-start(bf16[32,3072]{1,0:T(8,128)(2,1)S(1)} %get-tuple-element.53), channel_id=1, source_target_pairs={{0,12},{1,13},{2,14},{3,15},{4,0},{5,1},{6,2},{7,3},{8,4},{9,5},{1... | collective-permute-start | bytes 589832 | tf_op jit(solution)/shard_map/ppermute | solution.py:349
  45.2 6.9 %collective-permute-start.14 = (bf16[32,3072]{1,0:T(8,128)(2,1)S(1)}, bf16[32,3072]{1,0:T(8,128)(2,1)S(1)}, u32[]{:S(2)}, u32[]{:S(2)}) collective-permute-start(bf16[32,3072]{1,0:T(8,128)(2,1)S(1)} %get-tuple-element.54), channel_id=1, source_target_pairs={{0,4},{1,5},{2,6},{3,7},{4,8},{5,9},{6,10},{7,11},{8,12},{9,13},{1... | collective-permute-start | bytes 589832 | tf_op jit(solution)/shard_map/ppermute | solution.py:349
  46.5 7.3 %collective-permute-start.9 = (bf16[32,3072]{1,0:T(8,128)(2,1)S(1)}, bf16[32,3072]{1,0:T(8,128)(2,1)S(1)}, u32[]{:S(2)}, u32[]{:S(2)}) collective-permute-start(bf16[32,3072]{1,0:T(8,128)(2,1)S(1)} %get-tuple-element.48), channel_id=1, source_target_pairs={{0,12},{1,13},{2,14},{3,15},{4,0},{5,1},{6,2},{7,3},{8,4},{9,5},{1... | collective-permute-start | bytes 589832 | tf_op jit(solution)/shard_map/ppermute | solution.py:349
  49.3 9.0 %collective-permute-start.10 = (bf16[32,3072]{1,0:T(8,128)(2,1)S(1)}, bf16[32,3072]{1,0:T(8,128)(2,1)S(1)}, u32[]{:S(2)}, u32[]{:S(2)}) collective-permute-start(bf16[32,3072]{1,0:T(8,128)(2,1)S(1)} %get-tuple-element.49), channel_id=1, source_target_pairs={{0,4},{1,5},{2,6},{3,7},{4,8},{5,9},{6,10},{7,11},{8,12},{9,13},{1... | collective-permute-start | bytes 589832 | tf_op jit(solution)/shard_map/ppermute | solution.py:349
  49.3 9.0 %collective-permute-start.11 = (bf16[32,3072]{1,0:T(8,128)(2,1)S(1)}, bf16[32,3072]{1,0:T(8,128)(2,1)S(1)}, u32[]{:S(2)}, u32[]{:S(2)}) collective-permute-start(bf16[32,3072]{1,0:T(8,128)(2,1)S(1)} %get-tuple-element.50), channel_id=1, source_target_pairs={{0,8},{1,9},{2,10},{3,11},{4,12},{5,13},{6,14},{7,15},{8,0},{9,1},... | collective-permute-start | bytes 589832 | tf_op jit(solution)/shard_map/ppermute | solution.py:349
  52.2 6.1 %collective-permute-start.15 = (bf16[32,3072]{1,0:T(8,128)(2,1)S(1)}, bf16[32,3072]{1,0:T(8,128)(2,1)S(1)}, u32[]{:S(2)}, u32[]{:S(2)}) collective-permute-start(bf16[32,3072]{1,0:T(8,128)(2,1)S(1)} %shard_map.115), channel_id=1, source_target_pairs={{0,1},{1,0},{2,3},{3,2},{4,5},{5,4},{6,7},{7,6},{8,9},{9,8},{10,11... | collective-permute-start | bytes 589832 | tf_op jit(solution)/shard_map/ppermute | solution.py:357
